TPU v7x, 32 devices: a whole 2x2x4 slice. The times are simulated.
32 devices in a mesh: dp: 16 (over z, y, x), ctx: 2 (over core).
Axes of the slice: x: 2, y: 2, z: 4, core: 2. Of those that a mesh axis runs over, the one named last changes fastest.
Arguments:
- queries: bfloat16 [16, 512, 1024], P('dp', 'ctx'), may hold values from -7 to 7
- key_states: bfloat16 [16, 512, 1024], P('dp', 'ctx'), may hold values from -7 to 7
- value_states: bfloat16 [16, 512, 1024], P('dp', 'ctx'), may hold values from -6 to 6
- token_order: int32 [16, 512], P('dp', 'ctx'), may hold values from 0 to 511, each once within a row
- block_pattern: int32 [16, 4, 4], P('dp'), may hold values from -1 to 3, as said below
- out_weight: bfloat16 [1024, 2048], P('dp'), may hold values from -0.1875 to 0.1875
- out_grad: bfloat16 [16, 512, 2048], P('dp', 'ctx'), may hold values from -6 to 6
Outputs:
- layer_out: bfloat16 [16, 512, 2048], P('dp', 'ctx')
- query_grad: bfloat16 [16, 512, 1024], P('dp', 'ctx')
- key_grad: bfloat16 [16, 512, 1024], P('dp', 'ctx')
- value_grad: bfloat16 [16, 512, 1024], P('dp', 'ctx')
- weight_grad: float32 [1024, 2048], P('dp')
Inputs may be any that keep to these rules, and one draw needn't show every extreme that they name: `block_pattern`: row b of a session lists key blocks of the same session, each within 2 blocks of b, none twice; slot 0 holds b itself, used slots come before the slots that hold -1, and a row is full whenever 4 blocks lie within that reach.
All inputs are finite; a program needn't handle non-finite values.
Results may differ from a plain program's by a relative error of at most 0.012.
Values may be sent and summed in bfloat16 or wider, within the bound.
No kernel may reach another device: no remote copies, remote signals or barrier semaphores. Data moves between devices by JAX's collectives and lax.ppermute only.
A program may use at most 128 MiB of HBM per device.

v0:
```python
import math

import jax
import jax.numpy as jnp
from jax import lax
from jax.sharding import PartitionSpec as P

H = 8
HD = 128
BLK = 128
KB = 4


def padded(shard, sides, width):
    for axis, dim in sides:
        devices, length = (lax.axis_size(axis), shard.shape[dim])
        up = [(i, (i + 1) % devices) for i in range(devices - 1)]
        down = [(j, i) for i, j in up]
        last = lax.slice_in_dim(shard, length - width, length, axis=dim)
        leading = lax.slice_in_dim(shard, 0, width, axis=dim)
        before = lax.ppermute(last, axis, up)
        after = lax.ppermute(leading, axis, down)
        shard = jnp.concatenate([before, shard, after], axis=dim)
    return shard


def from_behind(block, axis, distance):
    devices = range(lax.axis_size(axis))
    route = [(i - distance, i) for i in devices if i - distance in devices]
    return lax.ppermute(block, axis, route)


def rope_tables(positions):
    coords = jnp.stack(
        [positions % 8, positions // 8 % 8, positions // 64 % 4, positions // 256], axis=1
    ).astype(jnp.float32)
    per_axis = HD // 16
    frequency = 100.0 ** (-jnp.arange(per_axis, dtype=jnp.float32) / per_axis)
    angle = (coords[:, :, None] * frequency[None, None, :]).reshape(
        positions.shape[0], 4 * per_axis
    )
    return (jnp.cos(angle), jnp.sin(angle))


def rotate_heads(heads, cosine, sine_vals, direction):
    quarter = HD // 4
    first_part = heads[..., :quarter]
    second_part = heads[..., quarter : 2 * quarter]
    cos_rows = cosine[:, None, :]
    sin_rows = direction * sine_vals[:, None, :]
    return jnp.concatenate(
        [
            first_part * cos_rows - second_part * sin_rows,
            second_part * cos_rows + first_part * sin_rows,
            heads[..., 2 * quarter :],
        ],
        axis=-1,
    )


def attend_forward(query_blocks, key_sets, value_sets, key_mask, score_scale):
    scores = (
        jnp.einsum("nqhd,nkhd->nhqk", query_blocks, key_sets, preferred_element_type=jnp.float32)
        * score_scale
    )
    scores = jnp.where(key_mask[:, None, None, :], scores, -jnp.inf)
    row_peak = jnp.max(scores, axis=-1)
    row_total = jnp.sum(jnp.exp(scores - row_peak[..., None]), axis=-1)
    log_total = row_peak + jnp.log(row_total)
    soft_probs = jnp.exp(scores - log_total[..., None]).astype(jnp.bfloat16)
    block_out = jnp.einsum(
        "nhqk,nkhd->nqhd", soft_probs, value_sets, preferred_element_type=jnp.float32
    ).astype(jnp.bfloat16)
    return (block_out, log_total)


def attend_backward(
    query_blocks,
    key_sets,
    value_sets,
    key_mask,
    log_total,
    grad_dot,
    grad_blocks,
    score_scale,
    key_form,
):
    scores = (
        jnp.einsum(
            "nqhd," + key_form + "->nhqk",
            query_blocks,
            key_sets,
            preferred_element_type=jnp.float32,
        )
        * score_scale
    )
    scores = jnp.where(key_mask[:, None, None, :], scores, -jnp.inf)
    exact_probs = jnp.exp(scores - log_total[..., None])
    soft_probs = exact_probs.astype(jnp.bfloat16)
    value_part = jnp.einsum(
        "nhqk,nqhd->" + key_form, soft_probs, grad_blocks, preferred_element_type=jnp.float32
    )
    prob_grad = jnp.einsum(
        "nqhd," + key_form + "->nhqk", grad_blocks, value_sets, preferred_element_type=jnp.float32
    )
    score_grad = (exact_probs * (prob_grad - grad_dot[..., None]) * score_scale).astype(
        jnp.bfloat16
    )
    query_part = jnp.einsum(
        "nhqk," + key_form + "->nqhd", score_grad, key_sets, preferred_element_type=jnp.float32
    )
    key_part = jnp.einsum(
        "nhqk,nqhd->" + key_form, score_grad, query_blocks, preferred_element_type=jnp.float32
    )
    return (query_part, key_part, value_part)


def shards(queries, key_states, value_states, token_order, block_pattern, out_weight, out_grad):
    row_count = queries.shape[1]
    feature_width = queries.shape[2]
    local_blocks = row_count // BLK
    shard_index = lax.axis_index("ctx")
    score_scale = 1.0 / math.sqrt(HD)
    cosine, sine_vals = rope_tables(token_order[0])
    rot_query = rotate_heads(
        queries[0].astype(jnp.float32).reshape(row_count, H, HD), cosine, sine_vals, 1.0
    ).astype(jnp.bfloat16)
    rot_keys = rotate_heads(
        key_states[0].astype(jnp.float32).reshape(row_count, H, HD), cosine, sine_vals, 1.0
    ).astype(jnp.bfloat16)
    stacked = jnp.stack([rot_keys.reshape(row_count, feature_width), value_states[0]], axis=1)
    extended = padded(stacked, (("ctx", 0),), row_count)
    ext_blocks = extended.reshape(3 * local_blocks, BLK, 2, H, HD)
    pattern_rows = block_pattern[0]
    first_block = shard_index * local_blocks
    my_pattern = lax.dynamic_slice_in_dim(pattern_rows, first_block, local_blocks, 0)
    slot_valid = my_pattern >= 0
    slot_local = jnp.where(slot_valid, my_pattern - first_block + local_blocks, 0)
    gathered = jnp.take(ext_blocks, slot_local, axis=0)
    key_sets = gathered[:, :, :, 0].reshape(local_blocks, KB * BLK, H, HD)
    value_sets = gathered[:, :, :, 1].reshape(local_blocks, KB * BLK, H, HD)
    key_mask = jnp.repeat(slot_valid, BLK, axis=1)
    query_blocks = rot_query.reshape(local_blocks, BLK, H, HD)
    block_out, log_total = attend_forward(query_blocks, key_sets, value_sets, key_mask, score_scale)
    attn = block_out.reshape(row_count, feature_width)
    grad_rows = out_grad[0]
    forward_weight = lax.all_gather(out_weight, "dp", axis=0, tiled=True)
    layer_out = jnp.dot(attn, forward_weight, preferred_element_type=jnp.float32).astype(
        jnp.bfloat16
    )
    attn_grad = lax.dot_general(
        grad_rows,
        lax.all_gather(out_weight, "dp", axis=0, tiled=True),
        (((1,), (1,)), ((), ())),
        preferred_element_type=jnp.float32,
    ).astype(jnp.bfloat16)
    batch_count = lax.axis_size("dp")
    local_grad = lax.psum_scatter(
        lax.dot_general(
            attn, grad_rows, (((0,), (0,)), ((), ())), preferred_element_type=jnp.float32
        )
        / batch_count,
        "dp",
        scatter_dimension=0,
        tiled=True,
    )
    weight_grad = lax.psum(local_grad, "ctx")
    dot_rows = jnp.sum(
        (attn_grad.astype(jnp.float32) * attn.astype(jnp.float32)).reshape(row_count, H, HD),
        axis=-1,
    )
    grad_dot = dot_rows.reshape(local_blocks, BLK, H).transpose(0, 2, 1)
    grad_blocks = attn_grad.reshape(local_blocks, BLK, H, HD)
    query_part, key_part, value_part = attend_backward(
        query_blocks,
        key_sets,
        value_sets,
        key_mask,
        log_total,
        grad_dot,
        grad_blocks,
        score_scale,
        "nkhd",
    )
    query_grad = (
        rotate_heads(query_part.reshape(row_count, H, HD), cosine, sine_vals, -1.0)
        .reshape(row_count, feature_width)
        .astype(jnp.bfloat16)
    )
    keep = slot_valid.reshape(local_blocks * KB).astype(jnp.float32)[:, None, None, None, None]
    both_parts = (
        jnp.stack(
            [
                key_part.reshape(local_blocks * KB, BLK, H, HD),
                value_part.reshape(local_blocks * KB, BLK, H, HD),
            ],
            axis=2,
        )
        * keep
    )
    accumulated = (
        jnp.zeros((3 * local_blocks, BLK, 2, H, HD), jnp.float32)
        .at[slot_local.reshape(-1)]
        .add(both_parts)
    )
    accumulated = accumulated.reshape(3 * row_count, 2, feature_width)
    own_part = accumulated[row_count : 2 * row_count]
    from_right = from_behind(accumulated[:row_count], "ctx", -1)
    from_left = from_behind(accumulated[2 * row_count :], "ctx", 1)
    summed = own_part + from_right + from_left
    key_total = summed[:, 0]
    value_total = summed[:, 1]
    key_grad = (
        rotate_heads(key_total.reshape(row_count, H, HD), cosine, sine_vals, -1.0)
        .reshape(row_count, feature_width)
        .astype(jnp.bfloat16)
    )
    value_grad = value_total.astype(jnp.bfloat16)
    return (layer_out[None], query_grad[None], key_grad[None], value_grad[None], weight_grad)


def solution(mesh):
    in_specs = (
        P("dp", "ctx", None),
        P("dp", "ctx", None),
        P("dp", "ctx", None),
        P("dp", "ctx"),
        P("dp", None, None),
        P("dp", None),
        P("dp", "ctx", None),
    )
    out_specs = (
        P("dp", "ctx", None),
        P("dp", "ctx", None),
        P("dp", "ctx", None),
        P("dp", "ctx", None),
        P("dp", None),
    )
    return jax.shard_map(shards, mesh=mesh, in_specs=in_specs, out_specs=out_specs, check_vma=False)
```

profile of v0, /device:TPU:0, one launch (start us, length us, event | category | flops | bytes accessed | tf_op | source)
XLA Modules:
  0.0 300.0 jit_solution(13280898733726044079)
XLA Ops:
  8.1 0.7 and_select_fusion.5
  9.2 1.1 copy.104
  10.4 1.3 copy.101
  12.1 1.7 subtract_convert_fusion.2
  13.8 1.3 pad_maximum_fusion.2
  15.1 1.3 convert_element_type.105
  16.4 2.1 pad_maximum_fusion.1
  18.5 1.3 collective-permute-start.1
  19.8 5.0 %collective-permute-start = (bf16[256,2,1024]{2,0,1:T(8,128)(2,1)}, bf16[256,2,1024]{2,0,1:T(8,128)(2,1)}, u32[]{:S(2)}, u32[]{:S(2)}) collective-permute-start(bf16[256,2,1024]{2,0,1:T(8,128)(2,1)} %pad_maximum_fusion.1), channel_id=1, source_target_pairs={{0,1},{2,3},{4,5},{6,7},{8,9},{10,11},{12,13},{14,15},{16,17},{18,... | collective-permute-start | bytes 3145736 | tf_op jit(solution)/shard_map/ppermute | solution.py:21
  25.2 0.9 copy.73
  26.1 0.9 copy.71
  27.0 0.9 copy.72
  27.9 1.8 pad_maximum_fusion
  29.7 0.8 copy.102
  30.5 2.2 copy.91
  32.8 4.9 %gather_fusion = bf16[8,128,2,8,128]{4,3,2,1,0:T(8,128)(2,1)} fusion(bf16[6,128,2,8,128]{4,3,2,1,0:T(8,128)(2,1)} %copy.91, s32[1024]{0:T(1024)S(1)} %pad_clamp_fusion), kind=kCustom, calls=%fused_computation | custom fusion | bytes 8388640 | tf_op jit(solution)/shard_map/jit(_take)/gather | solution.py:139
  37.7 2.7 broadcast_select_fusion
  40.3 2.0 fusion.30
  42.9 4.3 %copy.92 = bf16[2,512,8,128]{1,3,2,0:T(8,128)(2,1)} copy(bf16[2,512,8,128]{3,2,1,0:T(8,128)(2,1)} %bitcast.147) | data formatting | bytes 4194304 | tf_op jit(solution)/shard_map/reshape;squeeze | solution.py:141
  47.2 2.6 fusion.1
  49.9 1.3 exponential_reduce_fusion
  51.9 1.9 fusion.4
  53.8 2.1 copy.75
  55.9 5.7 %convolution_multiply_fusion = f32[1024,2048]{1,0:T(8,128)} fusion(bf16[1,256,2048]{2,1,0:T(8,128)(2,1)S(1)} %copy-done, bf16[32,8,8,128]{3,2,1,0:T(8,128)(2,1)} %bitcast.148), kind=kOutput, calls=%fused_computation.3 | convolution fusion | flops 1075838976 | bytes 9961472 | tf_op jit(solution)/shard_map/dot_general | solution.py:159
  62.1 27.3 %all-gather.2.cloned.1.call-done = bf16[1024,2048]{1,0:T(8,128)(2,1)} async-done(((bf16[64,2048]{1,0:T(8,128)(2,1)}), bf16[1024,2048]{1,0:T(8,128)(2,1)}) %all-gather.2.cloned.1.call-update) | async-done | bytes 4194320 | tf_op jit(solution)/shard_map/all_gather | solution.py:147
  89.3 3.5 %convolution_convert_fusion.1 = bf16[256,1024]{1,0:T(8,128)(2,1)S(1)} fusion(bf16[1024,2048]{1,0:T(8,128)(2,1)} %all-gather.2.cloned.1.call-done, bf16[1,256,2048]{2,1,0:T(8,128)(2,1)S(1)} %copy-done), kind=kOutput, calls=%fused_computation.19 | convolution fusion | flops 1074003968 | bytes 5767168 | tf_op jit(solution)/shard_map/dot_general | solution.py:151
  92.8 0.8 copy-done.16
  93.7 1.1 copy.83
  94.8 1.4 multiply_bitcast_fusion
  96.2 1.2 copy.107
  97.4 1.6 reduce_sum.19
  99.0 5.5 %convolution_bitcast_fusion = f32[2,512,8,128]{1,3,2,0:T(8,128)} fusion(bf16[2,128,8,128]{1,3,2,0:T(8,128)(2,1)} %copy.83, f32[2,8,128,512]{3,2,1,0:T(8,128)} %copy-done.2, f32[2,8,128]{2,1,0:T(8,128)S(1)} %log_add_fusion, pred[2,512]{1,0:T(4,128)(4,1)S(1)} %bitcast.166), kind=kOutput, calls=%fused_computation.14 | convolution fusion | flops 272629760 | bytes 8922112 | tf_op jit(solution)/shard_map/nhqk,nqhd->nkhd/dot_general | solution.py:100
  104.5 5.3 %copy.84 = f32[2,512,8,128]{3,2,1,0:T(8,128)} copy(f32[2,512,8,128]{1,3,2,0:T(8,128)} %convolution_bitcast_fusion) | data formatting | bytes 8388608 | tf_op jit(solution)/shard_map/nhqk,nqhd->nkhd/transpose | solution.py:100
  109.8 4.7 %multiply_convert_fusion = bf16[2,8,128,512]{3,2,1,0:T(8,128)(2,1)S(1)} fusion(f32[2,8,128,512]{3,2,1,0:T(8,128)} %copy-done.2, bf16[2,128,8,128]{1,3,2,0:T(8,128)(2,1)} %copy.83, bf16[2,512,8,128]{1,3,2,0:T(8,128)(2,1)} %copy.92, f32[2,8,128]{2,1,0:T(8,128)S(1)} %bitcast.168, f32[2,8,128]{2,1,0:T(8,128)S(1)} %log_add_fusion, pred[2,512]{1,0:T(4,128)(4,1)S(1)} %bitcast.167), kind=kOutput, calls=%fused_computation.4 | convolution fusion | flops 275775488 | bytes 8930304 | tf_op jit(solution)/shard_map/nqhd,nkhd->nhqk/dot_general | solution.py:103
  114.5 1.3 copy-done.3
  115.9 3.0 %convolution_bitcast_fusion.1 = f32[2,512,8,128]{1,3,2,0:T(8,128)} fusion(bf16[2,8,128,512]{3,2,1,0:T(8,128)(2,1)S(1)} %multiply_convert_fusion, bf16[2,128,8,64]{3,1,2,0:T(8,128)(2,1)S(1)} %copy-done.9, bf16[2,128,8,32]{3,1,2,0:T(8,128)(2,1)S(1)} %copy-done.11, bf16[2,128,8,32]{3,1,2,0:T(8,128)(2,1)S(1)} %copy-done.10), kind=kOutput, calls=%fused_computation.15 | convolution fusion | flops 270008320 | bytes 6815744 | tf_op jit(solution)/shard_map/nhqk,nqhd->nkhd/dot_general | solution.py:112
  118.9 5.3 %copy.82 = f32[2,512,8,128]{3,2,1,0:T(8,128)} copy(f32[2,512,8,128]{1,3,2,0:T(8,128)} %convolution_bitcast_fusion.1) | data formatting | bytes 8388608 | tf_op jit(solution)/shard_map/nhqk,nqhd->nkhd/transpose | solution.py:112
  124.2 4.7 %maximum_multiply_fusion = f32[8,128,2,8,128]{4,3,1,0,2:T(8,128)S(1)} fusion(f32[8,128,1,8,128]{4,3,1,0,2:T(8,128)} %bitcast.138, f32[8,128,1,8,128]{4,3,1,0,2:T(8,128)} %bitcast.139, f32[8]{0:T(128)S(1)} %reshape.587), kind=kLoop, calls=%fused_computation.2 | loop fusion | flops 4194304 | bytes 16777248 | tf_op jit(solution)/shard_map/mul | solution.py:192
  128.9 3.9 %copy.85 = f32[8,128,2,8,128]{4,3,2,1,0:T(8,128)} copy(f32[8,128,2,8,128]{4,3,1,0,2:T(8,128)S(1)} %maximum_multiply_fusion) | data formatting | bytes 16777216 | tf_op jit(solution)/shard_map/mul | solution.py:192
  132.9 3.2 %broadcast_in_dim.65 = f32[6,128,2,8,128]{4,3,2,1,0:T(8,128)} broadcast(f32[]{:T(128)} %constant.104.clone.1), dimensions={} | broadcast | bytes 6291460 | tf_op jit(solution)/shard_map/broadcast_in_dim | solution.py:202
  136.1 17.5 %scatter_fusion = f32[6,128,2,8,128]{4,3,2,1,0:T(8,128)} fusion(f32[6,128,2,8,128]{4,3,2,1,0:T(8,128)} %broadcast_in_dim.65, s32[8]{0:T(128)S(1)} %fusion.20, f32[8,128,2,8,128]{4,3,2,1,0:T(8,128)} %copy.85), kind=kCustom, calls=%fused_computation.1 | custom fusion | flops 2097152 | bytes 25165856 | tf_op jit(solution)/shard_map/scatter-add | solution.py:204
  153.5 5.8 %fusion.29 = (f32[2,128,2,8,128]{4,3,2,1,0:T(8,128)}, f32[2,128,2,8,128]{4,3,2,1,0:T(8,128)}, f32[2,128,2,8,128]{4,3,2,1,0:T(8,128)}) fusion(f32[6,128,2,8,128]{4,3,2,1,0:T(8,128)} %scatter_fusion), kind=kLoop, calls=%fused_computation.98 | loop fusion | bytes 12582912 | tf_op jit(solution)/shard_map/slice | solution.py:207
  159.3 3.2 %slice.87 = f32[256,2,1024]{2,1,0:T(2,128)} reshape(f32[2,128,2,8,128]{4,3,2,1,0:T(8,128)} %get-tuple-element.8) | data formatting | bytes 4194304 | tf_op jit(solution)/shard_map/slice | solution.py:209
  162.6 3.7 %copy.88 = f32[256,2,1024]{2,0,1:T(8,128)} copy(f32[256,2,1024]{2,1,0:T(2,128)} %slice.87) | data formatting | bytes 4194304 | tf_op jit(solution)/shard_map/slice | solution.py:209
  166.2 3.3 %slice.85 = f32[256,2,1024]{2,1,0:T(2,128)} reshape(f32[2,128,2,8,128]{4,3,2,1,0:T(8,128)} %get-tuple-element.9) | data formatting | bytes 4194304 | tf_op jit(solution)/shard_map/slice | solution.py:208
  169.5 3.6 %copy.86 = f32[256,2,1024]{2,0,1:T(8,128)} copy(f32[256,2,1024]{2,1,0:T(2,128)} %slice.85) | data formatting | bytes 4194304 | tf_op jit(solution)/shard_map/slice | solution.py:208
  173.1 1.3 collective-permute-start.2
  174.4 5.7 %collective-permute-start.3 = (f32[256,2,1024]{2,0,1:T(8,128)}, f32[256,2,1024]{2,0,1:T(8,128)}, u32[]{:S(2)}, u32[]{:S(2)}) collective-permute-start(f32[256,2,1024]{2,0,1:T(8,128)} %copy.88), channel_id=1, source_target_pairs={{0,1},{2,3},{4,5},{6,7},{8,9},{10,11},{12,13},{14,15},{16,17},{18,... | collective-permute-start | bytes 6291464 | tf_op jit(solution)/shard_map/ppermute | solution.py:30
  180.1 2.3 convolution_bitcast_fusion.2
  183.1 1.0 slice.137
  184.1 2.1 slice.83
  186.2 4.7 %fusion.2 = bf16[1,256,2048]{2,1,0:T(8,128)(2,1)} fusion(bf16[1024,2048]{1,0:T(8,128)(2,1)} %all-gather.2.cloned.1.call-done, bf16[32,8,8,128]{3,2,1,0:T(8,128)(2,1)} %bitcast.150), kind=kOutput, calls=%fused_computation.13 | convolution fusion | flops 1074266112 | bytes 5767168 | tf_op jit(solution)/shard_map/dot_general | solution.py:148
  190.9 3.2 %fusion.3 = f32[256,2,1024]{2,0,1:T(8,128)S(1)} fusion(f32[256,2,1024]{2,0,1:T(8,128)} %collective-permute-done.3, f32[256,2,1024]{2,0,1:T(8,128)} %collective-permute-done.2, f32[256,2,1024]{2,1,0:T(2,128)S(1)} %copy-done.5), kind=kLoop, calls=%fused_computation.17 | loop fusion | flops 1048576 | bytes 8388608 | tf_op jit(solution)/shard_map/add | solution.py:210
  194.1 1.4 copy-done.6
  195.8 72.3 %reduce-scatter.2.cloned.1.call-done = f32[64,2048]{1,0:T(8,128)} async-done(((f32[1024,2048]{1,0:T(8,128)}), f32[64,2048]{1,0:T(8,128)}) %reduce-scatter.2.cloned.1.call-update) | async-done | bytes 524304 | tf_op jit(solution)/shard_map/reduce_scatter | solution.py:158
  268.1 0.7 subtract_convert_fusion
  268.9 1.0 slice.136
  269.9 1.6 pad_maximum_fusion.4
  271.5 1.0 convert_element_type.116
  272.5 1.5 pad_maximum_fusion.5
  274.0 1.0 convert_element_type.119
  275.0 2.1 fusion.7
  277.1 14.4 %all-reduce.2.cloned.1.call-done = f32[64,2048]{1,0:T(8,128)} async-done(((f32[64,2048]{1,0:T(8,128)}), f32[64,2048]{1,0:T(8,128)}) %all-reduce.2.cloned.1.call-update) | async-done | bytes 524304 | tf_op jit(solution)/shard_map/psum | solution.py:167
  291.6 1.9 copy.125
  (71 shorter events, 4.9 us)
Async XLA Ops:
  7.2 48.7 %copy-start = (bf16[1,256,2048]{2,1,0:T(8,128)(2,1)S(1)}, bf16[1,256,2048]{2,1,0:T(8,128)(2,1)}, u32[]{:S(2)}) copy-start(bf16[1,256,2048]{2,1,0:T(8,128)(2,1)} %param.13) | copy-start | bytes 3145732
  7.2 82.2 %all-gather.2.cloned.1.call-start = ((), (), s32[]{:S(2)}) async-start(), calls=%async_computation.1 | async-start | bytes 4456448 | tf_op jit(solution)/shard_map/all_gather | solution.py:147
  7.9 260.2 %reduce-scatter.2.cloned.1.call-start = ((), (), s32[]{:S(2)}) async-start(), calls=%async_computation.2 | async-start | bytes 8912896 | tf_op jit(solution)/shard_map/reduce_scatter | solution.py:158
  10.3 1.6 copy-start.7
  13.8 10.9 %copy-start.17 = (s32[1,4,4]{2,1,0:T(4,128)S(1)}, s32[1,4,4]{2,1,0:T(4,128)}, u32[]{:S(2)}) copy-start(s32[1,4,4]{2,1,0:T(4,128)} %param.11) | copy-start | bytes 196
  13.8 11.1 %copy-start.8 = (bf16[32,8,8,128]{3,2,1,0:T(8,128)(2,1)S(1)}, bf16[32,8,8,128]{3,2,1,0:T(8,128)(2,1)}, u32[]{:S(2)}) copy-start(bf16[32,8,8,128]{3,2,1,0:T(8,128)(2,1)} %copy-done.7) | copy-start | bytes 1572868
  13.8 12.2 %copy-start.13 = (bf16[256,8,32]{2,1,0:T(8,128)(2,1)S(1)}, bf16[256,8,32]{2,1,0:T(8,128)(2,1)}, u32[]{:S(2)}) copy-start(bf16[256,8,32]{2,1,0:T(8,128)(2,1)} %get-tuple-element.16) | copy-start | bytes 393220
  13.8 13.1 %copy-start.12 = (bf16[256,8,32]{2,1,0:T(8,128)(2,1)S(1)}, bf16[256,8,32]{2,1,0:T(8,128)(2,1)}, u32[]{:S(2)}) copy-start(bf16[256,8,32]{2,1,0:T(8,128)(2,1)} %get-tuple-element.17) | copy-start | bytes 393220
  18.5 9.4 %collective-permute-start.1 = (bf16[256,2,1024]{2,0,1:T(8,128)(2,1)}, bf16[256,2,1024]{2,0,1:T(8,128)(2,1)}, u32[]{:S(2)}, u32[]{:S(2)}) collective-permute-start(bf16[256,2,1024]{2,0,1:T(8,128)(2,1)} %pad_maximum_fusion.1), channel_id=1, source_target_pairs={{1,0},{3,2},{5,4},{7,6},{9,8},{11,10},{13,12},{15,14},{17,16},{19,... | collective-permute-start | bytes 3145736 | tf_op jit(solution)/shard_map/ppermute | solution.py:22
  19.8 8.1 %collective-permute-start = (bf16[256,2,1024]{2,0,1:T(8,128)(2,1)}, bf16[256,2,1024]{2,0,1:T(8,128)(2,1)}, u32[]{:S(2)}, u32[]{:S(2)}) collective-permute-start(bf16[256,2,1024]{2,0,1:T(8,128)(2,1)} %pad_maximum_fusion.1), channel_id=1, source_target_pairs={{0,1},{2,3},{4,5},{6,7},{8,9},{10,11},{12,13},{14,15},{16,17},{18,... | collective-permute-start | bytes 3145736 | tf_op jit(solution)/shard_map/ppermute | solution.py:21
  24.9 3.0 %copy-start.15 = (bf16[1,256,1024]{2,1,0:T(8,128)(2,1)S(1)}, bf16[1,256,1024]{2,1,0:T(8,128)(2,1)}, u32[]{:S(2)}) copy-start(bf16[1,256,1024]{2,1,0:T(8,128)(2,1)} %param.9) | copy-start | bytes 1572868
  47.2 4.6 %copy-start.14 = (bf16[2,512,8,128]{1,3,2,0:T(8,128)(2,1)S(1)}, bf16[2,512,8,128]{1,3,2,0:T(8,128)(2,1)}, u32[]{:S(2)}) copy-start(bf16[2,512,8,128]{1,3,2,0:T(8,128)(2,1)} %copy.92) | copy-start | bytes 6291460
  49.9 2.0 copy-start.2
  61.6 230.0 %all-reduce.2.cloned.1.call-start = ((), (), s32[]{:S(2)}) async-start(), calls=%async_computation.3 | async-start | bytes 1048576 | tf_op jit(solution)/shard_map/psum | solution.py:167
  92.8 0.8 copy-start.16
  109.8 6.1 %copy-start.9 = (bf16[2,128,8,64]{3,1,2,0:T(8,128)(2,1)S(1)}, bf16[2,128,8,64]{3,1,2,0:T(8,128)(2,1)}, u32[]{:S(2)}) copy-start(bf16[2,128,8,64]{3,1,2,0:T(8,128)(2,1)} %copy.73) | copy-start | bytes 786436
  109.8 6.1 %copy-start.10 = (bf16[2,128,8,32]{3,1,2,0:T(8,128)(2,1)S(1)}, bf16[2,128,8,32]{3,1,2,0:T(8,128)(2,1)}, u32[]{:S(2)}) copy-start(bf16[2,128,8,32]{3,1,2,0:T(8,128)(2,1)} %copy.71) | copy-start | bytes 393220
  109.8 6.1 %copy-start.11 = (bf16[2,128,8,32]{3,1,2,0:T(8,128)(2,1)S(1)}, bf16[2,128,8,32]{3,1,2,0:T(8,128)(2,1)}, u32[]{:S(2)}) copy-start(bf16[2,128,8,32]{3,1,2,0:T(8,128)(2,1)} %copy.72) | copy-start | bytes 393220
  114.5 1.3 copy-start.3
  173.1 17.8 %collective-permute-start.2 = (f32[256,2,1024]{2,0,1:T(8,128)}, f32[256,2,1024]{2,0,1:T(8,128)}, u32[]{:S(2)}, u32[]{:S(2)}) collective-permute-start(f32[256,2,1024]{2,0,1:T(8,128)} %copy.86), channel_id=1, source_target_pairs={{1,0},{3,2},{5,4},{7,6},{9,8},{11,10},{13,12},{15,14},{17,16},{19,... | collective-permute-start | bytes 6291464 | tf_op jit(solution)/shard_map/ppermute | solution.py:30
  174.4 16.5 %collective-permute-start.3 = (f32[256,2,1024]{2,0,1:T(8,128)}, f32[256,2,1024]{2,0,1:T(8,128)}, u32[]{:S(2)}, u32[]{:S(2)}) collective-permute-start(f32[256,2,1024]{2,0,1:T(8,128)} %copy.88), channel_id=1, source_target_pairs={{0,1},{2,3},{4,5},{6,7},{8,9},{10,11},{12,13},{14,15},{16,17},{18,... | collective-permute-start | bytes 6291464 | tf_op jit(solution)/shard_map/ppermute | solution.py:30
  182.5 1.6 copy-start.4
  186.2 4.7 %copy-start.5 = (f32[256,2,1024]{2,1,0:T(2,128)S(1)}, f32[256,2,1024]{2,1,0:T(2,128)}, u32[]{:S(2)}) copy-start(f32[256,2,1024]{2,1,0:T(2,128)} %slice.83) | copy-start | bytes 6291460
  194.1 1.4 copy-start.6
  269.9 23.6 %copy-start.1 = (bf16[1,256,2048]{2,1,0:T(8,128)(2,1)S(1)}, bf16[1,256,2048]{2,1,0:T(8,128)(2,1)}, u32[]{:S(2)}) copy-start(bf16[1,256,2048]{2,1,0:T(8,128)(2,1)} %param.13) | copy-start | bytes 3145732
Sparse Core Ops, SparseCore 0:
  10.8 78.5 all-gather.1
  91.6 176.4 reduce-scatter.1
  270.4 21.0 all-reduce.1
where the time goes:
time: 301 us; the launch traced here: 300 us
  waiting for transfers between devices  115 us (38%)
  local copies, waits for them, and re-layouts  79.3 us (26%)
  other arithmetic  44.3 us (15%)
  matrix products  34 us (11%)
  between operations  14.1 us (5%)
  starting transfers between devices  13.6 us (5%)
    reduce_scatter x1, waiting for transfers between devices, shards(): lax.psum_scatter(lax.dot_general(attn, grad_rows, (((0,), (0,)), ((), ())...  72.3 us
    all_gather x1, waiting for transfers between devices, shards(): forward_weight = lax.all_gather(out_weight, 'dp', axis=0, tiled=True)  27.3 us
    scatter-add x1, other arithmetic, shards(): accumulated = jnp.zeros((3 * local_blocks, BLK, 2, H, HD), jnp.float32).a...  17.5 us
    psum x1, waiting for transfers between devices, shards(): weight_grad = lax.psum(local_grad, 'ctx')  14.4 us
    unnamed x46, local copies, waits for them, and re-layouts  10.9 us
    slice x2, local copies, waits for them, and re-layouts, shards(): own_part = accumulated[row_count:2 * row_count]  7.85 us
    ppermute x2, starting transfers between devices, from_behind(): return lax.ppermute(block, axis, route)  6.95 us
    slice x2, local copies, waits for them, and re-layouts, shards(): from_left = from_behind(accumulated[2 * row_count:], 'ctx', 1)  6.92 us
  transfers between devices with their start and end apart: 7, of which 3 were waited for; matrix products, arithmetic and copies ran while one was open for 51% of the time, Pallas kernels for 0%

commit v1 on v0

--- a/solution.py
+++ b/solution.py
@@ -1,8 +1,12 @@
+import itertools
 import math
 
 import jax
 import jax.numpy as jnp
+import numpy as np
 from jax import lax
+from jax.experimental import pallas as pl
+from jax.experimental.pallas import tpu as pltpu
 from jax.sharding import PartitionSpec as P
 
 H = 8
@@ -218,6 +222,369 @@
     value_grad = value_total.astype(jnp.bfloat16)
     return (layer_out[None], query_grad[None], key_grad[None], value_grad[None], weight_grad)
 
+def chip_moves(rule):
+    pairs = []
+    for z, y, x, core in itertools.product(range(4), range(2), range(2), range(2)):
+        target = rule(z, y, x, core)
+        if target is not None:
+            tz, ty, tx, tcore = target
+            pairs.append((((z * 2 + y) * 2 + x) * 2 + core, ((tz * 2 + ty) * 2 + tx) * 2 + tcore))
+    return pairs
+
+
+def swap_x(z, y, x, core):
+    return (z, y, 1 - x, core)
+
+
+def swap_y(z, y, x, core):
+    return (z, 1 - y, x, core)
+
+
+def move(array, rule):
+    return lax.ppermute(array, ("dp", "ctx"), chip_moves(rule))
+
+
+def swap_core(array):
+    return lax.ppermute(array, "ctx", [(0, 1), (1, 0)])
+
+
+def gather_first(z, y, x, core):
+    return (z ^ 2, y, x, core) if z // 2 == core else (z ^ 1, y, x, 1 - core)
+
+
+def gather_second(z, y, x, core):
+    return (z ^ 3, y, x, core) if z // 2 == core else None
+
+
+def gather_near(z, y, x, core):
+    return swap_y(z, y, x, core) if core == 0 else swap_x(z, y, x, core)
+
+
+def gather_far(z, y, x, core):
+    return swap_x(z, y, x, core) if core == 0 else swap_y(z, y, x, core)
+
+
+def scatter_first(z, y, x, core):
+    return (z ^ 1, y, x, 1 - core) if z // 2 == core else (z ^ 2, y, x, core)
+
+
+def scatter_second(z, y, x, core):
+    return None if z // 2 == core else (z ^ 3, y, x, core)
+
+
+def dot_nt(a, b):
+    return lax.dot_general(a, b, (((1,), (1,)), ((), ())), preferred_element_type=jnp.float32)
+
+
+def dot_tn(a, b):
+    return lax.dot_general(a, b, (((0,), (0,)), ((), ())), preferred_element_type=jnp.float32)
+
+
+def dot_nn(a, b):
+    return jnp.dot(a, b, preferred_element_type=jnp.float32)
+
+
+def rope_rows(order):
+    lane = np.arange(HD)
+    entry = lane % (HD // 4)
+    axis_of, step = entry // (HD // 16), entry % (HD // 16)
+    rotated = lane < HD // 2
+    shift = np.array([0, 3, 6, 8], np.int32)[axis_of]
+    keep = np.array([7, 7, 3, -1], np.int32)[axis_of]
+    per_axis = HD // 16
+    frequency = 100.0 ** (-jnp.arange(per_axis, dtype=jnp.float32) / per_axis)
+    lane_frequency = jnp.where(rotated, jnp.tile(frequency, HD // per_axis), 0.0)
+    coords = jnp.bitwise_and(jnp.right_shift(order[:, None], shift[None, :]), keep[None, :])
+    angle = coords.astype(jnp.float32) * lane_frequency[None, :]
+    sign = np.where(lane < HD // 4, -1.0, 1.0).astype(np.float32)
+    return jnp.cos(angle), jnp.sin(angle) * sign[None, :]
+
+
+def rotate(x, cos_ref, sin_ref, direction):
+    quarter = HD // 4
+    lane = lax.broadcasted_iota(jnp.int32, x.shape, 1)
+    other = jnp.where(
+        lane < quarter, pltpu.roll(x, HD - quarter, 1), pltpu.roll(x, quarter, 1)
+    )
+    return x * cos_ref[...] + direction * (other * sin_ref[...])
+
+
+def block_bias(info, row_block, width):
+    core = info[0]
+    lane_block = lax.broadcasted_iota(jnp.int32, (1, width), 1) // BLK
+    bias = jnp.full((1, width), -jnp.inf, jnp.float32)
+    query_block = (row_block + 2 * core) % 4
+    for key_local in range(4):
+        key_block = (key_local + 2 * core) % 4
+        listed = jnp.int32(0)
+        for slot in range(KB):
+            listed = listed + jnp.where(info[4 + query_block * KB + slot] == key_block, 1, 0)
+        bias = jnp.where((lane_block == key_local) & (listed > 0), 0.0, bias)
+    return bias
+
+
+def forward_kernel(info, q, k, v, r, cos, sin, rot_q, rot_k, attn, lse):
+    head = pl.program_id(0)
+    tokens = cos.shape[0]
+    half = tokens // 2
+    scale = 1.0 / math.sqrt(HD)
+    xq = jnp.concatenate([q[...], r[0]], axis=0).astype(jnp.float32)
+    rot_q[...] = rotate(xq, cos, sin, 1.0).astype(jnp.bfloat16)
+    xk = jnp.concatenate([k[...], r[1]], axis=0).astype(jnp.float32)
+    rot_k[...] = rotate(xk, cos, sin, 1.0).astype(jnp.bfloat16)
+    keys = rot_k[...]
+    values = jnp.concatenate([v[...], r[2]], axis=0)
+    lane = lax.broadcasted_iota(jnp.int32, (BLK, HD), 1)
+    for b in range(tokens // BLK):
+        rows = slice(b * BLK, (b + 1) * BLK)
+        scores = dot_nt(rot_q[rows, :], keys) * scale + block_bias(info, b, tokens)
+        peak = jnp.max(scores, axis=1, keepdims=True)
+        raised = jnp.exp(scores - peak)
+        total = jnp.sum(raised, axis=1, keepdims=True)
+        probs = (raised * (1.0 / total)).astype(jnp.bfloat16)
+        attn[rows, :] = dot_nn(probs, values).astype(jnp.bfloat16)
+        log_total = peak + jnp.log(total)
+        lse[rows, :] = jnp.where(lane == head, log_total, lse[rows, :])
+
+
+def weight_grad_kernel(info, attn, own, other, send, keep):
+    core, z, y, x = info[0], info[1], info[2], info[3]
+    half = own.shape[0]
+    part = dot_tn(attn[0:half, :], own[...]) + dot_tn(attn[half:, :], other[...])
+    piece = send.shape[2]
+    for low in range(2):
+        for head_y in range(2):
+            for head_x in range(2):
+                start = ((low * 2 + head_y) * 2 + head_x) * piece
+                rows = part[start : start + piece, :]
+                z_rel = low ^ (z & 1)
+                first = jnp.where(core == 0, head_x ^ x, head_y ^ y)
+                sub = jnp.where(core == 0, head_y ^ y, head_x ^ x)
+
+                @pl.when(first == 1)
+                def _():
+                    send[sub, z_rel] = rows.astype(send.dtype)
+
+                @pl.when(first == 0)
+                def _():
+                    keep[sub, z_rel] = rows
+
+
+def projection_kernel(info, attn, own, other, near, far, out_own, out_send, grad, weight):
+    core, z, y, x = info[0], info[1], info[2], info[3]
+    piece = near.shape[2]
+    for e3, ref in enumerate((near, far)):
+        for e2 in range(2):
+            y_at = jnp.where(core == 0, y ^ e2, y ^ e3)
+            x_at = jnp.where(core == 0, x ^ e3, x ^ e2)
+            for low in range(2):
+                start = pl.multiple_of(((low * 2 + y_at) * 2 + x_at) * piece, piece)
+                weight[pl.ds(start, piece), :] = ref[e2, low]
+    half = own.shape[0]
+    out_send[...] = dot_nn(attn[half:, :], weight[...]).astype(out_send.dtype)
+    out_own[...] = dot_nn(attn[0:half, :], weight[...])
+    grad[0:half, :] = dot_nt(own[...], weight[...]).astype(grad.dtype)
+    grad[half:, :] = dot_nt(other[...], weight[...]).astype(grad.dtype)
+
+
+def backward_kernel(
+    info, rot_q, rot_k, v, r, attn, grad, lse, cos, sin, own, send, key_sum, value_sum, query_sum
+):
+    head = pl.program_id(0)
+    tokens = cos.shape[0]
+    half = tokens // 2
+    scale = 1.0 / math.sqrt(HD)
+    keys = rot_k[...]
+    values = jnp.concatenate([v[...], r[0]], axis=0)
+    lane = lax.broadcasted_iota(jnp.int32, (BLK, HD), 1)
+    for b in range(tokens // BLK):
+        rows = slice(b * BLK, (b + 1) * BLK)
+        queries = rot_q[rows, :]
+        grads = grad[rows, :]
+        log_total = jnp.sum(jnp.where(lane == head, lse[rows, :], 0.0), axis=1, keepdims=True)
+        dots = jnp.sum(
+            grads.astype(jnp.float32) * attn[rows, :].astype(jnp.float32), axis=1, keepdims=True
+        )
+        scores = dot_nt(queries, keys) * scale + block_bias(info, b, tokens)
+        exact = jnp.exp(scores - log_total)
+        prob_grad = dot_nt(grads, values)
+        score_grad = (exact * (prob_grad - dots) * scale).astype(jnp.bfloat16)
+        value_part = dot_tn(exact.astype(jnp.bfloat16), grads)
+        key_part = dot_tn(score_grad, queries)
+        query_sum[rows, :] = dot_nn(score_grad, keys)
+        if b == 0:
+            key_sum[...] = key_part
+            value_sum[...] = value_part
+        else:
+            key_sum[...] += key_part
+            value_sum[...] += value_part
+    outs = (
+        rotate(query_sum[...], cos, sin, -1.0),
+        rotate(key_sum[...], cos, sin, -1.0),
+        value_sum[...],
+    )
+    for i, out in enumerate(outs):
+        out = out.astype(jnp.bfloat16)
+        own[i] = out[0:half, :]
+        send[i] = out[half:, :]
+
+
+def chip_shards(queries, key_states, value_states, token_order, block_pattern, out_weight, out_grad):
+    rows, width = queries.shape[1:]
+    model = out_grad.shape[2]
+    tokens, mine = 2 * rows, width // 2
+    heads = mine // HD
+    owned = out_weight.shape[0]
+    core = lax.axis_index("ctx")
+    dp = lax.axis_index("dp")
+    z, y, x = dp // 4, dp // 2 % 2, dp % 2
+    at_home = z // 2 == core
+    odd = z % 2 == 1
+    params = pltpu.CompilerParams(vmem_limit_bytes=56 * 1024 * 1024)
+    bf16 = jnp.bfloat16
+
+    first = move(out_weight, gather_first)
+    second = move(out_weight, gather_second)
+
+    order_other = swap_core(token_order[0])
+    start_other = (1 - core) * mine
+    pack = jnp.stack(
+        [
+            lax.dynamic_slice_in_dim(a[0], start_other, mine, axis=1)
+            for a in (queries, key_states, value_states)
+        ]
+    )
+    received = swap_core(pack)
+    dy_own = out_grad[0]
+    dy_other = swap_core(dy_own)
+
+    order = jnp.concatenate([token_order[0], order_other])
+    cos, sin = rope_rows(order)
+    info = jnp.concatenate([jnp.stack([core, z, y, x]), block_pattern[0].reshape(-1)]).astype(
+        jnp.int32
+    )
+
+    def whole(*shape):
+        return pl.BlockSpec(shape, lambda *_: (0,) * len(shape))
+
+    own_head = pl.BlockSpec((None, rows, HD), lambda h, info: (0, 0, info[0] * heads + h))
+    by_head = pl.BlockSpec((tokens, HD), lambda h, info: (0, h))
+    rot_q, rot_k, attn, lse = pl.pallas_call(
+        forward_kernel,
+        grid_spec=pltpu.PrefetchScalarGridSpec(
+            num_scalar_prefetch=1,
+            grid=(heads,),
+            in_specs=[
+                own_head,
+                own_head,
+                own_head,
+                pl.BlockSpec((3, rows, HD), lambda h, info: (0, 0, h)),
+                whole(tokens, HD),
+                whole(tokens, HD),
+            ],
+            out_specs=[by_head, by_head, by_head, whole(tokens, HD)],
+        ),
+        out_shape=[jax.ShapeDtypeStruct((tokens, mine), bf16)] * 3
+        + [jax.ShapeDtypeStruct((tokens, HD), jnp.float32)],
+        compiler_params=params,
+        name="forward",
+    )(info, queries, key_states, value_states, received, cos, sin)
+
+    piece = (2, 2, owned, model)
+    send, keep = pl.pallas_call(
+        weight_grad_kernel,
+        grid_spec=pltpu.PrefetchScalarGridSpec(
+            num_scalar_prefetch=1,
+            grid=(1,),
+            in_specs=[whole(tokens, mine), whole(rows, model), whole(rows, model)],
+            out_specs=[whole(*piece), whole(*piece)],
+        ),
+        out_shape=[
+            jax.ShapeDtypeStruct(piece, bf16),
+            jax.ShapeDtypeStruct(piece, jnp.float32),
+        ],
+        compiler_params=params,
+        name="weight_grad",
+    )(info, attn, dy_own, dy_other)
+    got = move(send, gather_far).astype(jnp.float32)
+    second_send = (keep[1] + got[1]).astype(bf16)
+    kept = keep[0] + got[0]
+    kept = kept + move(second_send, gather_near).astype(jnp.float32)
+    to_first = jnp.where(at_home, kept[1], kept[0]).astype(bf16)
+    to_second = kept[1].astype(bf16)
+    from_first = move(to_first, scatter_first).astype(jnp.float32)
+    from_second = move(to_second, scatter_second).astype(jnp.float32)
+    share = jnp.where(at_home, kept[0] + from_first + from_second, from_first)
+    weight_grad = (share + swap_core(share)) * (1.0 / lax.axis_size("dp"))
+
+    a = jnp.where(at_home, out_weight, first)
+    b = jnp.where(at_home, first, second)
+    near = jnp.where(odd, jnp.stack([b, a]), jnp.stack([a, b]))
+    near = jnp.stack([near, move(near, gather_near)])
+    far = move(near, gather_far)
+
+    out_own, out_send, grad = pl.pallas_call(
+        projection_kernel,
+        grid_spec=pltpu.PrefetchScalarGridSpec(
+            num_scalar_prefetch=1,
+            grid=(1,),
+            in_specs=[
+                whole(tokens, mine),
+                whole(rows, model),
+                whole(rows, model),
+                whole(*piece),
+                whole(*piece),
+            ],
+            out_specs=[whole(rows, model), whole(rows, model), whole(tokens, mine)],
+            scratch_shapes=[pltpu.VMEM((mine, model), bf16)],
+        ),
+        out_shape=[
+            jax.ShapeDtypeStruct((rows, model), jnp.float32),
+            jax.ShapeDtypeStruct((rows, model), bf16),
+            jax.ShapeDtypeStruct((tokens, mine), bf16),
+        ],
+        compiler_params=params,
+        name="projection",
+    )(info, attn, dy_own, dy_other, near, far)
+    layer_out = (out_own + swap_core(out_send).astype(jnp.float32)).astype(bf16)
+
+    grads_own, grads_send = pl.pallas_call(
+        backward_kernel,
+        grid_spec=pltpu.PrefetchScalarGridSpec(
+            num_scalar_prefetch=1,
+            grid=(heads,),
+            in_specs=[
+                by_head,
+                by_head,
+                own_head,
+                pl.BlockSpec((1, rows, HD), lambda h, info: (2, 0, h)),
+                by_head,
+                by_head,
+                whole(tokens, HD),
+                whole(tokens, HD),
+                whole(tokens, HD),
+            ],
+            out_specs=[pl.BlockSpec((3, rows, HD), lambda h, info: (0, 0, h))] * 2,
+            scratch_shapes=[pltpu.VMEM((tokens, HD), jnp.float32)] * 3,
+        ),
+        out_shape=[jax.ShapeDtypeStruct((3, rows, mine), bf16)] * 2,
+        compiler_params=params,
+        name="backward",
+    )(info, rot_q, rot_k, value_states, received, attn, grad, lse, cos, sin)
+    grads_other = swap_core(grads_send)
+    on_left = core == 0
+    outs = [
+        jnp.concatenate(
+            [
+                jnp.where(on_left, grads_own[i], grads_other[i]),
+                jnp.where(on_left, grads_other[i], grads_own[i]),
+            ],
+            axis=1,
+        )[None]
+        for i in range(3)
+    ]
+    return (layer_out[None], *outs, weight_grad)
+
 
 def solution(mesh):
     in_specs = (
@@ -236,4 +603,5 @@
         P("dp", "ctx", None),
         P("dp", None),
     )
-    return jax.shard_map(shards, mesh=mesh, in_specs=in_specs, out_specs=out_specs, check_vma=False)
+    body = chip_shards if (mesh.shape["dp"], mesh.shape["ctx"]) == (16, 2) else shards
+    return jax.shard_map(body, mesh=mesh, in_specs=in_specs, out_specs=out_specs, check_vma=False)

time: 301 us -> 103 us (0.34)
  waiting for transfers between devices: 115 us -> 40.5 us
  local copies, waits for them, and re-layouts: 79.3 us -> 4.82 us
  other arithmetic: 44.3 us -> 9.65 us
  matrix products: 34 us -> 0 us
  Pallas kernels: 0 us -> 31.4 us
  between operations: 14.1 us -> 1.07 us
    reduce_scatter x1 -> x0, waiting for transfers between devices: 72.3 us -> none  [shards(): lax.psum_scatter(lax.dot_general(attn, grad_rows, (((0,), (0,)), ((), ())...]
    ppermute x4 -> x14, waiting for transfers between devices: 0.01 us -> 40.5 us  [the longest x8 39.8 us: move(): return lax.ppermute(array, ('dp', 'ctx'), chip_moves(rule))]
    dot_general x9 -> x0, matrix products: 34 us -> none  [the longest x1 5.7 us: shards(): lax.dot_general(attn, grad_rows, (((0,), (0,)), ((), ())), preferred_elem...]
    pallas_call x0 -> x4, Pallas kernels: none -> 31.4 us  [the longest x1 9.81 us: chip_shards(): pl.pallas_call(backward_kernel, grid_spec=pltpu.PrefetchScalarGridSpec(nu...]
    all_gather x1 -> x0, waiting for transfers between devices: 27.3 us -> none  [shards(): forward_weight = lax.all_gather(out_weight, 'dp', axis=0, tiled=True)]
    slice x12 -> x0, local copies, waits for them, and re-layouts: 26.6 us -> none  [the longest x2 7.85 us: shards(): own_part = accumulated[row_count:2 * row_count]]
    scatter-add x1 -> x0, other arithmetic: 17.5 us -> none  [shards(): accumulated = jnp.zeros((3 * local_blocks, BLK, 2, H, HD), jnp.float32).a...]
    psum x1 -> x0, waiting for transfers between devices: 14.4 us -> none  [shards(): weight_grad = lax.psum(local_grad, 'ctx')]
  transfers between devices with their start and end apart: 7 -> 14, of which waited for: 3 -> 6; matrix products, arithmetic and copies ran while one was open for 51% -> 11% of each run, Pallas kernels for 0% -> 31%
where the time goes in v1:
time: 103 us; the launch traced here: 102 us
  waiting for transfers between devices  40.5 us (39%)
  Pallas kernels  31.4 us (30%)
  starting transfers between devices  14.8 us (14%)
  other arithmetic  9.65 us (9%)
  local copies, waits for them, and re-layouts  4.82 us (5%)
  between operations  1.07 us (1%)
    ppermute x8, waiting for transfers between devices, move(): return lax.ppermute(array, ('dp', 'ctx'), chip_moves(rule))  39.8 us
    ppermute x8, starting transfers between devices, move(): return lax.ppermute(array, ('dp', 'ctx'), chip_moves(rule))  13.6 us
    pallas_call x1, Pallas kernels, chip_shards(): pl.pallas_call(backward_kernel, grid_spec=pltpu.PrefetchScalarGridSpec(nu...  9.81 us
    pallas_call x1, Pallas kernels, chip_shards(): pl.pallas_call(forward_kernel, grid_spec=pltpu.PrefetchScalarGridSpec(num...  9.78 us
    pallas_call x1, Pallas kernels, chip_shards(): pl.pallas_call(projection_kernel, grid_spec=pltpu.PrefetchScalarGridSpec(...  6.27 us
    pallas_call x1, Pallas kernels, chip_shards(): pl.pallas_call(weight_grad_kernel, grid_spec=pltpu.PrefetchScalarGridSpec...  5.58 us
    broadcast_in_dim x3, other arithmetic, chip_shards(): jnp.concatenate([jnp.where(on_left, grads_own[i], grads_other[i]), jnp.wh...  2.56 us
  transfers between devices with their start and end apart: 14, of which 6 were waited for; matrix products, arithmetic and copies ran while one was open for 11% of the time, Pallas kernels for 31%

profile of v1, /device:TPU:0, one launch (start us, length us, event | category | flops | bytes accessed | tf_op | source)
XLA Modules:
  0.0 102.4 jit_solution(9754437887099380982)
XLA Ops:
  0.6 0.0 copy-start.9
  0.6 0.0 copy-start.11
  0.7 0.0 copy-start.12
  0.7 0.0 copy-start.13
  0.7 0.5 collective-permute-start.2
  1.2 1.0 constant_dynamic-slice_fusion.2
  2.2 1.1 %constant_dynamic-slice_fusion = (bf16[1,256,512]{2,1,0:T(8,128)(2,1)S(1)}, bf16[1,256,512]{2,1,0:T(8,128)(2,1)S(1)}) fusion(bf16[1,256,1024]{2,1,0:T(8,128)(2,1)} %v.3, s32[]{:T(128)S(6)} %select_n.125, bf16[1,256,1024]{2,1,0:T(8,128)(2,1)} %k.1), kind=kLoop, calls=%fused_computation.40 | loop fusion | bytes 1048580 | tf_op jit(solution)/shard_map/dynamic_slice | solution.py:453
  3.3 0.1 pad_maximum_fusion.1
  3.4 0.1 collective-permute-start
  3.5 0.0 copy-done.7
  3.5 4.0 %collective-permute-start.3 = (bf16[64,2048]{1,0:T(8,128)(2,1)S(1)}, bf16[64,2048]{1,0:T(8,128)(2,1)S(1)}, u32[]{:S(2)}, u32[]{:S(2)}) collective-permute-start(bf16[64,2048]{1,0:T(8,128)(2,1)S(1)} %copy-done.7), channel_id=1, source_target_pairs={{0,16},{1,8},{2,18},{3,10},{4,20},{5,12},{6,22},{7,14},{8,24},{9,0... | collective-permute-start | bytes 786440 | tf_op jit(solution)/shard_map/ppermute | solution.py:244
  7.5 3.1 %collective-permute-start.4 = (bf16[64,2048]{1,0:T(8,128)(2,1)S(1)}, bf16[64,2048]{1,0:T(8,128)(2,1)S(1)}, u32[]{:S(2)}, u32[]{:S(2)}) collective-permute-start(bf16[64,2048]{1,0:T(8,128)(2,1)S(1)} %copy-done.7), channel_id=1, source_target_pairs={{0,24},{2,26},{4,28},{6,30},{8,16},{10,18},{12,20},{14,22},{17,9},... | collective-permute-start | bytes 786440 | tf_op jit(solution)/shard_map/ppermute | solution.py:244
  10.6 0.0 copy-done.10
  10.6 0.1 collective-permute-start.1
  10.8 0.1 reshape_squeeze.3
  10.9 0.1 reshape.100
  11.0 0.6 concatenate.29.info
  11.6 0.2 collective-permute-done.1
  11.8 1.9 %sine_multiply_fusion = (f32[512,128]{1,0:T(8,128)}, f32[512,128]{1,0:T(8,128)}) fusion(f32[128]{0:T(128)S(1)} %copy-done.11, f32[128]{0:T(128)S(1)} %reshape.100, s32[128]{0:T(128)S(1)} %copy-done.12, s32[128]{0:T(128)S(1)} %copy-done.13, s32[512]{0:T(512)S(1)} %pad_add_fusion), kind=kLoop, calls=%fused_computation.29 | loop fusion | flops 327680 | bytes 528384 | tf_op jit(solution)/shard_map/mul | solution.py:300
  13.7 0.0 collective-permute-done.r
  13.7 1.0 copy-done.2
  14.7 9.8 %forward.1 = (bf16[512,512]{1,0:T(8,128)(2,1)}, bf16[512,512]{1,0:T(8,128)(2,1)}, bf16[512,512]{1,0:T(8,128)(2,1)}, f32[512,128]{1,0:T(8,128)}) custom-call(s32[20]{0:T(128)} %concatenate.29.info, bf16[1,256,1024]{2,1,0:T(8,128)(2,1)} %q.1, bf16[1,256,1024]{2,1,0:T(8,128)(2,1)} %k.1, bf16[1,256,1024]{2,1,0:T(8,128)(2,1)} %v.3, ...), custom_call_target="tpu_custom_call" | custom-call | tf_op jit(solution)/shard_map/forward/pallas_call | solution.py:472
  24.5 0.0 collective-permute-done.2.other
  24.5 0.0 copy-start
  24.5 1.0 copy-done
  25.4 5.6 %weight_grad.1 = (bf16[2,2,64,2048]{3,2,1,0:T(8,128)(2,1)}, f32[2,2,64,2048]{3,2,1,0:T(8,128)}) custom-call(s32[20]{0:T(128)} %concatenate.29.info, bf16[512,512]{1,0:T(8,128)(2,1)} %get-tuple-element.16.attn, bf16[256,2048]{1,0:T(8,128)(2,1)} %bitcast.54, bf16[256,2048]{1,0:T(8,128)(2,1)} %copy-done), custom_call_target="tpu_custom_call" | custom-call | tf_op jit(solution)/shard_map/weight_grad/pallas_call | solution.py:494
  31.0 1.5 %collective-permute-start.9 = (bf16[2,2,64,2048]{3,2,1,0:T(8,128)(2,1)}, bf16[2,2,64,2048]{3,2,1,0:T(8,128)(2,1)S(1)}, u32[]{:S(2)}, u32[]{:S(2)}) collective-permute-start(bf16[2,2,64,2048]{3,2,1,0:T(8,128)(2,1)} %get-tuple-element.26), channel_id=1, source_target_pairs={{0,2},{1,5},{2,0},{3,7},{4,6},{5,1},{6,4},{7,3},{8,10},{9,13},{10,... | collective-permute-start | bytes 3145736 | tf_op jit(solution)/shard_map/ppermute | solution.py:244
  32.5 0.0 collective-permute-done.3
  32.5 0.0 collective-permute-done.4
  32.5 0.1 fusion.9
  32.6 0.1 maximum_select_fusion.1
  32.7 1.6 %collective-permute-start.5 = (bf16[2,64,2048]{2,1,0:T(8,128)(2,1)S(1)}, bf16[2,64,2048]{2,1,0:T(8,128)(2,1)S(1)}, u32[]{:S(2)}, u32[]{:S(2)}) collective-permute-start(bf16[2,64,2048]{2,1,0:T(8,128)(2,1)S(1)} %maximum_select_fusion.1), channel_id=1, source_target_pairs={{0,4},{1,3},{2,6},{3,1},{4,0},{5,7},{6,2},{7,5},{8,12},{9,11},{10,... | collective-permute-start | bytes 1572872 | tf_op jit(solution)/shard_map/ppermute | solution.py:244
  34.3 0.1 maximum_select_fusion
  34.3 13.3 %collective-permute-done.5 = bf16[2,64,2048]{2,1,0:T(8,128)(2,1)S(1)} collective-permute-done((bf16[2,64,2048]{2,1,0:T(8,128)(2,1)S(1)}, bf16[2,64,2048]{2,1,0:T(8,128)(2,1)S(1)}, u32[]{:S(2)}, u32[]{:S(2)}) %collective-permute-start.5) | collective-permute-done | bytes 524320 | tf_op jit(solution)/shard_map/ppermute | solution.py:244
  47.6 0.1 pad_maximum_fusion.near
  47.7 0.6 collective-permute-start.6
  48.3 3.3 %collective-permute-done.9 = bf16[2,2,64,2048]{3,2,1,0:T(8,128)(2,1)S(1)} collective-permute-done((bf16[2,2,64,2048]{3,2,1,0:T(8,128)(2,1)}, bf16[2,2,64,2048]{3,2,1,0:T(8,128)(2,1)S(1)}, u32[]{:S(2)}, u32[]{:S(2)}) %collective-permute-start.9) | collective-permute-done | bytes 1048608 | tf_op jit(solution)/shard_map/ppermute | solution.py:244
  51.6 0.2 convert_element_type.36
  51.9 0.9 fusion.5
  52.8 1.0 %collective-permute-start.10 = (bf16[2,64,2048]{2,1,0:T(8,128)(2,1)}, bf16[2,64,2048]{2,1,0:T(8,128)(2,1)}, u32[]{:S(2)}, u32[]{:S(2)}) collective-permute-start(bf16[2,64,2048]{2,1,0:T(8,128)(2,1)} %fusion.5), channel_id=1, source_target_pairs={{0,4},{1,3},{2,6},{3,1},{4,0},{5,7},{6,2},{7,5},{8,12},{9,11},{10,... | collective-permute-start | bytes 1572872 | tf_op jit(solution)/shard_map/ppermute | solution.py:244
  53.9 14.7 %collective-permute-done.6.far = bf16[2,2,64,2048]{3,2,1,0:T(8,128)(2,1)} collective-permute-done((bf16[2,2,64,2048]{3,2,1,0:T(8,128)(2,1)S(1)}, bf16[2,2,64,2048]{3,2,1,0:T(8,128)(2,1)}, u32[]{:S(2)}, u32[]{:S(2)}) %collective-permute-start.6) | collective-permute-done | bytes 1048608 | tf_op jit(solution)/shard_map/ppermute | solution.py:244
  68.6 6.3 %projection.1 = (f32[256,2048]{1,0:T(8,128)}, bf16[256,2048]{1,0:T(8,128)(2,1)}, bf16[512,512]{1,0:T(8,128)(2,1)}) custom-call(s32[20]{0:T(128)} %concatenate.29.info, bf16[512,512]{1,0:T(8,128)(2,1)} %get-tuple-element.16.attn, bf16[256,2048]{1,0:T(8,128)(2,1)} %bitcast.55, bf16[256,2048]{1,0:T(8,128)(2,1)} %copy-done, bf16[2,2,64,2048]{3,2,1,0:T(8,128)(2,1)} %copy-done.1, ...), custom_call_target="tpu_custom_call" | custom-call | tf_op jit(solution)/shard_map/projection/pallas_call | solution.py:526
  74.9 9.8 %backward.1 = (bf16[3,256,512]{2,1,0:T(8,128)(2,1)}, bf16[3,256,512]{2,1,0:T(8,128)(2,1)}) custom-call(s32[20]{0:T(128)} %concatenate.29.info, bf16[512,512]{1,0:T(8,128)(2,1)} %get-tuple-element.19.rot_q, bf16[512,512]{1,0:T(8,128)(2,1)} %get-tuple-element.20.rot_k, bf16[1,256,1024]{2,1,0:T(8,128)(2,1)} %v.3, bf16[3,256,512]{2,1,0:T(8,128)(2,1)} %copy-done.2, ...), custom_call_target="tpu_custom_call" | custom-call | tf_op jit(solution)/shard_map/backward/pallas_call | solution.py:551
  84.7 0.0 collective-permute-start.8
  84.7 0.0 copy-start.6
  84.7 0.5 collective-permute-start.7
  85.2 0.0 collective-permute-done.10
  85.2 1.2 %fusion.3 = f32[2,64,2048]{2,1,0:T(8,128)S(1)} fusion(f32[2,2,64,2048]{3,2,1,0:T(8,128)S(1)} %convert_element_type.36, bf16[2,64,2048]{2,1,0:T(8,128)(2,1)} %collective-permute-done.10, f32[2,2,64,2048]{3,2,1,0:T(8,128)S(1)} %copy-done.4), kind=kLoop, calls=%fused_computation.6 | loop fusion | flops 786432 | bytes 3670016 | tf_op jit(solution)/shard_map/add | solution.py:512
  86.4 0.1 select_convert_fusion
  86.5 0.5 collective-permute-start.11
  87.0 1.3 %collective-permute-start.12 = (bf16[64,2048]{1,0:T(8,128)(2,1)S(1)}, bf16[64,2048]{1,0:T(8,128)(2,1)S(1)}, u32[]{:S(2)}, u32[]{:S(2)}) collective-permute-start(bf16[64,2048]{1,0:T(8,128)(2,1)S(1)} %fusion.6), channel_id=1, source_target_pairs={{1,25},{3,27},{5,29},{7,31},{9,17},{11,19},{13,21},{15,23},{16,8},... | collective-permute-start | bytes 786440 | tf_op jit(solution)/shard_map/ppermute | solution.py:244
  88.3 0.0 collective-permute-done.8
  88.3 0.1 select_bitcast_fusion.1
  88.4 0.9 maximum_bitcast_fusion.2
  89.3 0.9 maximum_bitcast_fusion
  90.2 0.9 maximum_bitcast_fusion.1
  91.0 8.4 %collective-permute-done.11 = bf16[64,2048]{1,0:T(8,128)(2,1)S(1)} collective-permute-done((bf16[64,2048]{1,0:T(8,128)(2,1)S(1)}, bf16[64,2048]{1,0:T(8,128)(2,1)S(1)}, u32[]{:S(2)}, u32[]{:S(2)}) %collective-permute-start.11) | collective-permute-done | bytes 262176 | tf_op jit(solution)/shard_map/ppermute | solution.py:244
  99.4 0.0 collective-permute-done.12
  99.4 0.1 convert_select_fusion
  99.5 0.1 collective-permute-start.13
  99.6 0.0 collective-permute-done.7
  99.6 1.3 %fusion = bf16[1,256,2048]{2,1,0:T(8,128)(2,1)} fusion(f32[256,2048]{1,0:T(8,128)S(1)} %copy-done.5, bf16[256,2048]{1,0:T(8,128)(2,1)S(1)} %collective-permute-done.7), kind=kLoop, calls=%fused_computation.1 | loop fusion | flops 1572864 | bytes 4194304 | tf_op jit(solution)/shard_map/broadcast_in_dim | solution.py:586
  100.9 0.6 collective-permute-done.13
  101.5 0.9 add_multiply_fusion
  (24 shorter events, 0.1 us)
Async XLA Ops:
  0.6 10.1 %copy-start.9 = (pred[16,8]{1,0:T(8,128)(4,1)S(1)}, pred[16,8]{1,0:T(8,128)(4,1)}, u32[]{:S(2)}) copy-start(pred[16,8]{1,0:T(8,128)(4,1)} %constant.96) | copy-start | bytes 388
  0.6 11.2 %copy-start.11 = (f32[128]{0:T(128)S(1)}, f32[128]{0:T(128)}, u32[]{:S(2)}) copy-start(f32[128]{0:T(128)} %constant.95) | copy-start | bytes 1540
  0.7 11.2 %copy-start.12 = (s32[128]{0:T(128)S(1)}, s32[128]{0:T(128)}, u32[]{:S(2)}) copy-start(s32[128]{0:T(128)} %constant.94) | copy-start | bytes 1540
  0.7 11.2 %copy-start.13 = (s32[128]{0:T(128)S(1)}, s32[128]{0:T(128)}, u32[]{:S(2)}) copy-start(s32[128]{0:T(128)} %constant.93) | copy-start | bytes 1540
  0.7 2.8 %copy-start.7 = (bf16[64,2048]{1,0:T(8,128)(2,1)S(1)}, bf16[64,2048]{1,0:T(8,128)(2,1)}, u32[]{:S(2)}) copy-start(bf16[64,2048]{1,0:T(8,128)(2,1)} %param.16) | copy-start | bytes 786436
  0.7 9.9 %copy-start.10 = (s32[1,256]{1,0:T(1,128)S(1)}, s32[1,256]{1,0:T(1,128)}, u32[]{:S(2)}) copy-start(s32[1,256]{1,0:T(1,128)} %param.14) | copy-start | bytes 3076
  0.7 10.1 %copy-start.8 = (s32[1,4,4]{2,1,0:T(4,128)S(1)}, s32[1,4,4]{2,1,0:T(4,128)}, u32[]{:S(2)}) copy-start(s32[1,4,4]{2,1,0:T(4,128)} %param.15) | copy-start | bytes 196
  0.7 23.8 %collective-permute-start.2 = (bf16[256,2048]{1,0:T(8,128)(2,1)}, bf16[256,2048]{1,0:T(8,128)(2,1)S(1)}, u32[]{:S(2)}, u32[]{:S(2)}) collective-permute-start(bf16[256,2048]{1,0:T(8,128)(2,1)} %bitcast.53), channel_id=1, source_target_pairs={{0,1},{1,0},{2,3},{3,2},{4,5},{5,4},{6,7},{7,6},{8,9},{9,8},{10,11... | collective-permute-start | bytes 3145736 | tf_op jit(solution)/shard_map/ppermute | solution.py:248
  3.4 10.4 %collective-permute-start = (bf16[3,256,512]{2,1,0:T(8,128)(2,1)S(1)}, bf16[3,256,512]{2,1,0:T(8,128)(2,1)S(1)}, u32[]{:S(2)}, u32[]{:S(2)}) collective-permute-start(bf16[3,256,512]{2,1,0:T(8,128)(2,1)S(1)} %pad_maximum_fusion.1), channel_id=1, source_target_pairs={{0,1},{1,0},{2,3},{3,2},{4,5},{5,4},{6,7},{7,6},{8,9},{9,8},{10,11... | collective-permute-start | bytes 2359304 | tf_op jit(solution)/shard_map/ppermute | solution.py:248
  3.5 29.0 %collective-permute-start.3 = (bf16[64,2048]{1,0:T(8,128)(2,1)S(1)}, bf16[64,2048]{1,0:T(8,128)(2,1)S(1)}, u32[]{:S(2)}, u32[]{:S(2)}) collective-permute-start(bf16[64,2048]{1,0:T(8,128)(2,1)S(1)} %copy-done.7), channel_id=1, source_target_pairs={{0,16},{1,8},{2,18},{3,10},{4,20},{5,12},{6,22},{7,14},{8,24},{9,0... | collective-permute-start | bytes 786440 | tf_op jit(solution)/shard_map/ppermute | solution.py:244
  7.5 25.0 %collective-permute-start.4 = (bf16[64,2048]{1,0:T(8,128)(2,1)S(1)}, bf16[64,2048]{1,0:T(8,128)(2,1)S(1)}, u32[]{:S(2)}, u32[]{:S(2)}) collective-permute-start(bf16[64,2048]{1,0:T(8,128)(2,1)S(1)} %copy-done.7), channel_id=1, source_target_pairs={{0,24},{2,26},{4,28},{6,30},{8,16},{10,18},{12,20},{14,22},{17,9},... | collective-permute-start | bytes 786440 | tf_op jit(solution)/shard_map/ppermute | solution.py:244
  10.6 1.2 %collective-permute-start.1 = (s32[256]{0:T(256)S(1)}, s32[256]{0:T(256)S(1)}, u32[]{:S(2)}, u32[]{:S(2)}) collective-permute-start(s32[256]{0:T(256)S(1)} %bitcast.57), channel_id=1, source_target_pairs={{0,1},{1,0},{2,3},{3,2},{4,5},{5,4},{6,7},{7,6},{8,9},{9,8},{10,11... | collective-permute-start | bytes 3080 | tf_op jit(solution)/shard_map/ppermute | solution.py:248
  13.7 1.0 copy-start.2
  24.5 1.0 copy-start
  31.0 20.6 %collective-permute-start.9 = (bf16[2,2,64,2048]{3,2,1,0:T(8,128)(2,1)}, bf16[2,2,64,2048]{3,2,1,0:T(8,128)(2,1)S(1)}, u32[]{:S(2)}, u32[]{:S(2)}) collective-permute-start(bf16[2,2,64,2048]{3,2,1,0:T(8,128)(2,1)} %get-tuple-element.26), channel_id=1, source_target_pairs={{0,2},{1,5},{2,0},{3,7},{4,6},{5,1},{6,4},{7,3},{8,10},{9,13},{10,... | collective-permute-start | bytes 3145736 | tf_op jit(solution)/shard_map/ppermute | solution.py:244
  32.7 14.9 %collective-permute-start.5 = (bf16[2,64,2048]{2,1,0:T(8,128)(2,1)S(1)}, bf16[2,64,2048]{2,1,0:T(8,128)(2,1)S(1)}, u32[]{:S(2)}, u32[]{:S(2)}) collective-permute-start(bf16[2,64,2048]{2,1,0:T(8,128)(2,1)S(1)} %maximum_select_fusion.1), channel_id=1, source_target_pairs={{0,4},{1,3},{2,6},{3,1},{4,0},{5,7},{6,2},{7,5},{8,12},{9,11},{10,... | collective-permute-start | bytes 1572872 | tf_op jit(solution)/shard_map/ppermute | solution.py:244
  47.7 5.1 %copy-start.1 = (bf16[2,2,64,2048]{3,2,1,0:T(8,128)(2,1)}, bf16[2,2,64,2048]{3,2,1,0:T(8,128)(2,1)S(1)}, u32[]{:S(2)}) copy-start(bf16[2,2,64,2048]{3,2,1,0:T(8,128)(2,1)S(1)} %pad_maximum_fusion.near) | copy-start | bytes 3145732
  47.7 4.2 %copy-start.3 = (f32[2,2,64,2048]{3,2,1,0:T(8,128)S(1)}, f32[2,2,64,2048]{3,2,1,0:T(8,128)}, u32[]{:S(2)}) copy-start(f32[2,2,64,2048]{3,2,1,0:T(8,128)} %get-tuple-element.25) | copy-start | bytes 6291460
  47.7 20.9 %collective-permute-start.6 = (bf16[2,2,64,2048]{3,2,1,0:T(8,128)(2,1)S(1)}, bf16[2,2,64,2048]{3,2,1,0:T(8,128)(2,1)}, u32[]{:S(2)}, u32[]{:S(2)}) collective-permute-start(bf16[2,2,64,2048]{3,2,1,0:T(8,128)(2,1)S(1)} %pad_maximum_fusion.near), channel_id=1, source_target_pairs={{0,2},{1,5},{2,0},{3,7},{4,6},{5,1},{6,4},{7,3},{8,10},{9,13},{10,... | collective-permute-start | bytes 3145736 | tf_op jit(solution)/shard_map/ppermute | solution.py:244
  52.8 32.4 %collective-permute-start.10 = (bf16[2,64,2048]{2,1,0:T(8,128)(2,1)}, bf16[2,64,2048]{2,1,0:T(8,128)(2,1)}, u32[]{:S(2)}, u32[]{:S(2)}) collective-permute-start(bf16[2,64,2048]{2,1,0:T(8,128)(2,1)} %fusion.5), channel_id=1, source_target_pairs={{0,4},{1,3},{2,6},{3,1},{4,0},{5,7},{6,2},{7,5},{8,12},{9,11},{10,... | collective-permute-start | bytes 1572872 | tf_op jit(solution)/shard_map/ppermute | solution.py:244
  74.9 9.8 %copy-start.14 = (bf16[256,2048]{1,0:T(8,128)(2,1)S(1)}, bf16[256,2048]{1,0:T(8,128)(2,1)}, u32[]{:S(2)}) copy-start(bf16[256,2048]{1,0:T(8,128)(2,1)} %get-tuple-element.18) | copy-start | bytes 3145732
  74.9 10.3 %copy-start.4 = (f32[2,2,64,2048]{3,2,1,0:T(8,128)S(1)}, f32[2,2,64,2048]{3,2,1,0:T(8,128)}, u32[]{:S(2)}) copy-start(f32[2,2,64,2048]{3,2,1,0:T(8,128)} %get-tuple-element.25) | copy-start | bytes 6291460
  84.7 3.6 %collective-permute-start.8 = (bf16[3,256,512]{2,1,0:T(8,128)(2,1)}, bf16[3,256,512]{2,1,0:T(8,128)(2,1)S(1)}, u32[]{:S(2)}, u32[]{:S(2)}) collective-permute-start(bf16[3,256,512]{2,1,0:T(8,128)(2,1)} %get-tuple-element.24), channel_id=1, source_target_pairs={{0,1},{1,0},{2,3},{3,2},{4,5},{5,4},{6,7},{7,6},{8,9},{9,8},{10,11... | collective-permute-start | bytes 2359304 | tf_op jit(solution)/shard_map/ppermute | solution.py:248
  84.7 3.6 %copy-start.6 = (bf16[3,256,512]{2,1,0:T(8,128)(2,1)S(1)}, bf16[3,256,512]{2,1,0:T(8,128)(2,1)}, u32[]{:S(2)}) copy-start(bf16[3,256,512]{2,1,0:T(8,128)(2,1)} %get-tuple-element.23) | copy-start | bytes 2359300
  84.7 14.9 %collective-permute-start.7 = (bf16[256,2048]{1,0:T(8,128)(2,1)S(1)}, bf16[256,2048]{1,0:T(8,128)(2,1)S(1)}, u32[]{:S(2)}, u32[]{:S(2)}) collective-permute-start(bf16[256,2048]{1,0:T(8,128)(2,1)S(1)} %copy-done.14), channel_id=1, source_target_pairs={{0,1},{1,0},{2,3},{3,2},{4,5},{5,4},{6,7},{7,6},{8,9},{9,8},{10,11... | collective-permute-start | bytes 3145736 | tf_op jit(solution)/shard_map/ppermute | solution.py:248
  86.5 13.0 %collective-permute-start.11 = (bf16[64,2048]{1,0:T(8,128)(2,1)S(1)}, bf16[64,2048]{1,0:T(8,128)(2,1)S(1)}, u32[]{:S(2)}, u32[]{:S(2)}) collective-permute-start(bf16[64,2048]{1,0:T(8,128)(2,1)S(1)} %select_convert_fusion), channel_id=1, source_target_pairs={{0,9},{1,17},{2,11},{3,19},{4,13},{5,21},{6,15},{7,23},{8,1},{9,25... | collective-permute-start | bytes 786440 | tf_op jit(solution)/shard_map/ppermute | solution.py:244
  87.0 12.4 %collective-permute-start.12 = (bf16[64,2048]{1,0:T(8,128)(2,1)S(1)}, bf16[64,2048]{1,0:T(8,128)(2,1)S(1)}, u32[]{:S(2)}, u32[]{:S(2)}) collective-permute-start(bf16[64,2048]{1,0:T(8,128)(2,1)S(1)} %fusion.6), channel_id=1, source_target_pairs={{1,25},{3,27},{5,29},{7,31},{9,17},{11,19},{13,21},{15,23},{16,8},... | collective-permute-start | bytes 786440 | tf_op jit(solution)/shard_map/ppermute | solution.py:244
  89.3 10.3 %copy-start.5 = (f32[256,2048]{1,0:T(8,128)S(1)}, f32[256,2048]{1,0:T(8,128)}, u32[]{:S(2)}) copy-start(f32[256,2048]{1,0:T(8,128)} %get-tuple-element.17) | copy-start | bytes 6291460
  99.5 2.0 %collective-permute-start.13 = (f32[64,2048]{1,0:T(8,128)S(1)}, f32[64,2048]{1,0:T(8,128)S(1)}, u32[]{:S(2)}, u32[]{:S(2)}) collective-permute-start(f32[64,2048]{1,0:T(8,128)S(1)} %convert_select_fusion), channel_id=1, source_target_pairs={{0,1},{1,0},{2,3},{3,2},{4,5},{5,4},{6,7},{7,6},{8,9},{9,8},{10,11... | collective-permute-start | bytes 1572872 | tf_op jit(solution)/shard_map/ppermute | solution.py:248

commit v2 on v0

--- a/solution.py
+++ b/solution.py
@@ -1,14 +1,20 @@
+import functools
+import itertools
 import math
 
 import jax
 import jax.numpy as jnp
+import numpy as np
 from jax import lax
+from jax.experimental import pallas as pl
+from jax.experimental.pallas import tpu as pltpu
 from jax.sharding import PartitionSpec as P
 
 H = 8
 HD = 128
 BLK = 128
 KB = 4
+SUM_CHUNKS = 2
 
 
 def padded(shard, sides, width):
@@ -218,6 +224,495 @@
     value_grad = value_total.astype(jnp.bfloat16)
     return (layer_out[None], query_grad[None], key_grad[None], value_grad[None], weight_grad)
 
+def chip_moves(rule):
+    pairs = []
+    for z, y, x, core in itertools.product(range(4), range(2), range(2), range(2)):
+        target = rule(z, y, x, core)
+        if target is not None:
+            tz, ty, tx, tcore = target
+            pairs.append((((z * 2 + y) * 2 + x) * 2 + core, ((tz * 2 + ty) * 2 + tx) * 2 + tcore))
+    return pairs
+
+
+def swap_x(z, y, x, core):
+    return (z, y, 1 - x, core)
+
+
+def swap_y(z, y, x, core):
+    return (z, 1 - y, x, core)
+
+
+def move(array, rule):
+    return lax.ppermute(array, ("dp", "ctx"), chip_moves(rule))
+
+
+def swap_core(array):
+    return lax.ppermute(array, "ctx", [(0, 1), (1, 0)])
+
+
+def gather_first(z, y, x, core):
+    return (z ^ 2, y, x, core) if z // 2 == core else (z ^ 1, y, x, 1 - core)
+
+
+def gather_second(z, y, x, core):
+    return (z ^ 3, y, x, core) if z // 2 == core else None
+
+
+def gather_near(z, y, x, core):
+    return swap_y(z, y, x, core) if core == 0 else swap_x(z, y, x, core)
+
+
+def gather_far(z, y, x, core):
+    return swap_x(z, y, x, core) if core == 0 else swap_y(z, y, x, core)
+
+
+def scatter_first(z, y, x, core):
+    return (z ^ 1, y, x, 1 - core) if z // 2 == core else (z ^ 2, y, x, core)
+
+
+def scatter_second(z, y, x, core):
+    return None if z // 2 == core else (z ^ 3, y, x, core)
+
+
+def dot_nt(a, b):
+    return lax.dot_general(a, b, (((1,), (1,)), ((), ())), preferred_element_type=jnp.float32)
+
+
+def dot_nn(a, b):
+    return jnp.dot(a, b, preferred_element_type=jnp.float32)
+
+
+def rope_table(order):
+    per_axis = HD // 16
+    shape = (4 * per_axis, order.shape[1])
+    row = lax.broadcasted_iota(jnp.int32, shape, 0)
+    axis_of, step = row // per_axis, row % per_axis
+    coords = jnp.where(
+        axis_of == 0,
+        order % 8,
+        jnp.where(axis_of == 1, order // 8 % 8, jnp.where(axis_of == 2, order // 64 % 4, order // 256)),
+    )
+    frequency = jnp.zeros(shape, jnp.float32)
+    for i in range(per_axis):
+        frequency = jnp.where(step == i, jnp.float32(100.0 ** (-i / per_axis)), frequency)
+    angle = coords.astype(jnp.float32) * frequency
+    return jnp.cos(angle), jnp.sin(angle)
+
+
+def rotate_rows(x, cos, sin):
+    quarter = HD // 4
+    f, g, rest = x[0:quarter], x[quarter : 2 * quarter], x[2 * quarter :]
+    return jnp.concatenate([f * cos - g * sin, g * cos + f * sin, rest], axis=0).astype(jnp.bfloat16)
+
+
+def place():
+    dp = lax.axis_index("dp")
+    return lax.axis_index("ctx"), dp // 4, dp // 2 % 2, dp % 2
+
+
+def block_bias(pattern, core, bias):
+    blocks = bias.shape[0]
+    lane_block = lax.broadcasted_iota(jnp.int32, (1, bias.shape[1]), 1) // BLK
+    for key_local in range(blocks):
+        key_block = (key_local + 2 * core) % blocks
+        row = jnp.full(lane_block.shape, -jnp.inf, jnp.float32)
+        for query_local in range(blocks):
+            query_block = (query_local + 2 * core) % blocks
+            listed = jnp.int32(0)
+            for slot in range(KB):
+                listed = listed + jnp.where(pattern[0, query_block, slot] == key_block, 1, 0)
+            row = jnp.where((lane_block == query_local) & (listed > 0), 0.0, row)
+        bias[key_local : key_local + 1, :] = row
+
+
+def scaled_scores(keys, queries_t, bias):
+    scores = dot_nn(keys, queries_t) * (math.log2(math.e) / math.sqrt(HD))
+    parts = [scores[b * BLK : (b + 1) * BLK, :] + bias[b : b + 1, :] for b in range(bias.shape[0])]
+    return jnp.concatenate(parts, axis=0)
+
+
+def pack_kernel(*refs):
+    inputs, out, sems = refs[:3], refs[-2], refs[-1]
+    mine = out.shape[2]
+    there = pl.ds(pl.multiple_of((1 - place()[0]) * mine, mine), mine)
+    copies = [pltpu.make_async_copy(a.at[:, there], out.at[i], sems.at[i]) for i, a in enumerate(inputs)]
+    for copy in copies:
+        copy.start()
+    for copy in copies:
+        copy.wait()
+
+
+def forward_kernel(pattern, near, far, received, *refs):
+    inputs = refs[:3]
+    rot_q, rot_k, rot_kt, values, attn, attn_t, lse, bias, cos_ref, sin_ref, q, k, v, sems = refs[-14:]
+    rows, mine = inputs[0].shape[0], rot_q.shape[0]
+    tokens = 2 * rows
+    step = 2 * BLK
+    core = place()[0]
+    here = pl.ds(pl.multiple_of(core * mine, mine), mine)
+    copies = []
+    for i, (ref, target) in enumerate(zip(inputs, (q, k, v))):
+        copies.append(pltpu.make_async_copy(ref.at[:, here], target, sems.at[i]))
+        copies[-1].start()
+    block_bias(pattern, core, bias)
+    cos, sin = rope_table(jnp.concatenate([near[...], far[...]], axis=1))
+    cos_ref[...] = cos
+    sin_ref[...] = sin
+    for copy in copies:
+        copy.wait()
+    for head in range(mine // HD):
+        cols = slice(head * HD, (head + 1) * HD)
+        query, key, value = (
+            jnp.concatenate([a[:, cols], received[i, :, cols]], axis=0) for i, a in enumerate((q, k, v))
+        )
+        rot_q[cols, :] = rotate_rows(query.T.astype(jnp.float32), cos, sin)
+        keys_t = rotate_rows(key.T.astype(jnp.float32), cos, sin)
+        rot_kt[cols, :] = keys_t
+        keys = keys_t.T
+        rot_k[:, cols] = keys
+        values[:, cols] = value
+        value_t = value.T
+        for part in range(tokens // step):
+            at = slice(part * step, (part + 1) * step)
+            scores = scaled_scores(keys, rot_q[cols, at], bias[:, at])
+            peak = jnp.max(scores, axis=0, keepdims=True)
+            raised = jnp.exp2(scores - peak)
+            total = jnp.sum(raised, axis=0, keepdims=True)
+            mixed = dot_nn(value_t, raised.astype(jnp.bfloat16)) * (1.0 / total)
+            mixed = mixed.astype(jnp.bfloat16)
+            attn_t[cols, at] = mixed
+            attn[at, cols] = mixed.T
+            lse[head : head + 1, at] = peak + jnp.log2(total)
+
+
+def weight_grad_kernel(attn_t, own, other, *refs, chunk):
+    send, keep = refs[-2:]
+    core, z, y, x = place()
+    piece, width = send.shape[2:]
+    cols = slice(chunk * width, (chunk + 1) * width)
+    tokens = jnp.concatenate([own[:, cols], other[:, cols]], axis=0)
+    for block in range(attn_t.shape[0] // (2 * piece)):
+        rows = slice(block * 2 * piece, (block + 1) * 2 * piece)
+        part = dot_nn(attn_t[rows, :], tokens).astype(send.dtype)
+        z_rel = (block // 2) ^ (z & 1)
+        for head_x in range(2):
+            out = part[head_x * piece : (head_x + 1) * piece, :]
+            first = jnp.where(core == 0, head_x ^ x, (block % 2) ^ y)
+            sub = jnp.where(core == 0, (block % 2) ^ y, head_x ^ x)
+
+            @pl.when(first == 1)
+            def _():
+                send[sub, z_rel] = out
+
+            @pl.when(first == 0)
+            def _():
+                keep[sub, z_rel] = out
+
+
+def attn_grad_kernel(attn_t, own, other, *refs):
+    grad_t, dots, weight = refs[-3:]
+    core, z, y, x = place()
+    piece = refs[0].shape[1]
+    for chunk in range(2):
+        for e3 in range(2):
+            ref = refs[chunk * 2 + e3]
+            for e2 in range(2):
+                y_at = jnp.where(core == 0, y ^ e2, y ^ e3)
+                x_at = jnp.where(core == 0, x ^ e3, x ^ e2)
+                start = (((z % 2 ^ chunk) * 2 + y_at) * 2 + x_at) * piece
+                weight[pl.ds(pl.multiple_of(start, piece), piece), :] = ref[e2]
+    half = own.shape[0]
+    mine = weight.shape[0]
+    for t, ref in enumerate((own, other)):
+        cols = slice(t * half, (t + 1) * half)
+        rounded = dot_nt(weight[...], ref[...]).astype(grad_t.dtype)
+        grad_t[:, cols] = rounded
+        product = rounded.astype(jnp.float32) * attn_t[:, cols].astype(jnp.float32)
+        for head in range(mine // HD):
+            dots[head : head + 1, cols] = jnp.sum(
+                product[head * HD : (head + 1) * HD], axis=0, keepdims=True
+            )
+
+
+def projection_kernel(attn, weight, *refs):
+    out_send, out_own = refs[-2:]
+    half = out_own.shape[0]
+    for c in range(weight.shape[1] // half):
+        cols = slice(c * half, (c + 1) * half)
+        part = dot_nn(attn[...], weight[:, cols])
+        out_send[:, cols] = part[half:].astype(out_send.dtype)
+        out_own[:, cols] = part[:half]
+
+
+def backward_kernel(rot_q, rot_k, rot_kt, values, grad_t, dots, lse, bias, cos_ref, sin_ref, *refs, heads):
+    send, own = refs[-2:]
+    tokens = rot_k.shape[0]
+    half = tokens // 2
+    step = 2 * BLK
+    scale = 1.0 / math.sqrt(HD)
+    cos, sin = cos_ref[...], -sin_ref[...]
+    for at_head, head in enumerate(heads):
+        cols = slice(head * HD, (head + 1) * HD)
+        out_cols = slice(at_head * HD, (at_head + 1) * HD)
+        keys, keys_t, value = rot_k[:, cols], rot_kt[cols, :], values[:, cols]
+        key_sum = jnp.zeros((HD, tokens), jnp.float32)
+        value_sum = jnp.zeros((HD, tokens), jnp.float32)
+        query_parts = []
+        for part in range(tokens // step):
+            at = slice(part * step, (part + 1) * step)
+            queries_t, grads_t = rot_q[cols, at], grad_t[cols, at]
+            scores = scaled_scores(keys, queries_t, bias[:, at])
+            exact = jnp.exp2(scores - lse[head : head + 1, at])
+            prob_grad = dot_nn(value, grads_t)
+            score_grad = (exact * (prob_grad - dots[head : head + 1, at])).astype(jnp.bfloat16)
+            value_sum = value_sum + dot_nt(grads_t, exact.astype(jnp.bfloat16))
+            key_sum = key_sum + dot_nt(queries_t, score_grad)
+            query_parts.append(dot_nn(keys_t, score_grad))
+        query_sum = jnp.concatenate(query_parts, axis=1)
+        outs = (
+            rotate_rows(query_sum * scale, cos, sin),
+            rotate_rows(key_sum * scale, cos, sin),
+            value_sum.astype(jnp.bfloat16),
+        )
+        for i, out in enumerate(outs):
+            out = out.T
+            own[i, :, out_cols] = out[0:half, :]
+            send[i, :, out_cols] = out[half:, :]
+
+
+def gather_pick_kernel(home, away, *refs):
+    core, z, _, _ = place()
+    near = refs[-1]
+
+    @pl.when(z // 2 == core)
+    def _():
+        near[...] = home[...]
+
+    @pl.when(z // 2 != core)
+    def _():
+        near[...] = away[...]
+
+
+def pair_kernel(a, b, *refs):
+    refs[-1][0] = a[...]
+    refs[-1][1] = b[...]
+
+
+def second_sum_kernel(keep, got, *refs):
+    send, kept = refs[-2:]
+    send[...] = (keep[1].astype(jnp.float32) + got[1].astype(jnp.float32)).astype(send.dtype)
+    kept[...] = keep[0].astype(jnp.float32) + got[0].astype(jnp.float32)
+
+
+def z_sum_kernel(kept, got, *refs):
+    to_first, to_second, own = refs[-3:]
+    core, z, _, _ = place()
+    at_home = z // 2 == core
+    near = kept[0] + got[0].astype(jnp.float32)
+    rest = kept[1] + got[1].astype(jnp.float32)
+    own[...] = near
+    to_first[...] = jnp.where(at_home, rest, near).astype(to_first.dtype)
+    to_second[...] = rest.astype(to_second.dtype)
+
+
+def share_kernel(own, first, second, *refs):
+    core, z, _, _ = place()
+    at_home = z // 2 == core
+    total = own[...] + first[...].astype(jnp.float32) + second[...].astype(jnp.float32)
+    refs[-1][...] = jnp.where(at_home, total, first[...].astype(jnp.float32))
+
+
+def mean_kernel(*refs, count):
+    out = refs[-1]
+    width = refs[0].shape[1]
+    for i in range(out.shape[1] // width):
+        out[:, i * width : (i + 1) * width] = (refs[2 * i][...] + refs[2 * i + 1][...]) * (1.0 / count)
+
+
+def layer_out_kernel(own, got, *refs):
+    out = refs[-1]
+    out[...] = (own[...] + got[...].astype(jnp.float32)).astype(out.dtype)
+
+
+def grads_kernel(*refs):
+    outs, parts = refs[-3:], refs[:-3]
+    mine = outs[0].shape[1] // 2
+    width = parts[0].shape[2]
+    for p in range(mine // width):
+        for source in range(2):
+            start = (place()[0] ^ source) * mine + p * width
+            cols = pl.ds(pl.multiple_of(start, HD), width)
+            for i in range(3):
+                outs[i][:, cols] = parts[2 * p + source][i]
+
+
+def chip_shards(queries, key_states, value_states, token_order, block_pattern, out_weight, out_grad):
+    rows, width = queries.shape[1:]
+    model = out_grad.shape[2]
+    tokens, mine = 2 * rows, width // 2
+    owned = out_weight.shape[0]
+    bf16, f32 = jnp.bfloat16, jnp.float32
+    in_vmem = pl.BlockSpec(memory_space=pltpu.VMEM)
+    in_smem = pl.BlockSpec(memory_space=pltpu.SMEM)
+    in_hbm = pl.BlockSpec(memory_space=pltpu.HBM)
+    anywhere = pl.BlockSpec(memory_space=pl.ANY)
+    done = []
+
+    def call(kernel, name, args, outs, scratch=(), limit=8, specs=None, final=False):
+        before = [a for a in done if not any(a is b for b in args)]
+        results = pl.pallas_call(
+            kernel,
+            in_specs=list(specs or [in_vmem] * len(args)) + [anywhere] * len(before),
+            out_specs=[in_vmem] * len(outs),
+            out_shape=[jax.ShapeDtypeStruct(s, d) for s, d in outs],
+            scratch_shapes=scratch,
+            compiler_params=pltpu.CompilerParams(vmem_limit_bytes=limit << 20),
+            cost_estimate=pl.CostEstimate(flops=1, bytes_accessed=1, transcendentals=0),
+            name=name,
+        )(*args, *before)
+        if not final:
+            done[:] = results[:1]
+        return results
+
+    q_own, k_own, v_own, dy_own = queries[0], key_states[0], value_states[0], out_grad[0]
+    q_in, k_in, v_in = (pltpu.with_memory_space_constraint(a, pltpu.HBM) for a in (q_own, k_own, v_own))
+    (pack,) = call(
+        pack_kernel,
+        "pack",
+        (q_in, k_in, v_in),
+        [((3, rows, mine), bf16)],
+        specs=[in_hbm] * 3,
+        scratch=[pltpu.SemaphoreType.DMA((3,))],
+        final=True,
+    )
+    received = swap_core(pack)
+    order_far = swap_core(token_order)
+    dy_far = swap_core(dy_own)
+
+    first, second = move(out_weight, gather_first), move(out_weight, gather_second)
+    z_parts = ((out_weight, first), (first, second))
+    chunks = 2
+
+    rot_q, rot_k, rot_kt, values, attn, attn_t, lse, bias, cos, sin = call(
+        forward_kernel,
+        "forward",
+        (block_pattern, token_order, order_far, received, q_in, k_in, v_in),
+        [((mine, tokens), bf16), ((tokens, mine), bf16), ((mine, tokens), bf16)]
+        + [((tokens, mine), bf16)] * 2
+        + [((mine, tokens), bf16), ((mine // HD, tokens), f32), ((tokens // BLK, tokens), f32)]
+        + [((HD // 4, tokens), f32)] * 2,
+        scratch=[pltpu.VMEM((rows, mine), bf16)] * 3 + [pltpu.SemaphoreType.DMA((3,))],
+        limit=24,
+        specs=[in_smem] + [in_vmem] * 3 + [in_hbm] * 3,
+    )
+    sums = SUM_CHUNKS
+    cols = model // sums
+    near, joined, far = [None] * chunks, [None] * chunks, [None] * chunks
+    weights = [None] * (2 * chunks)
+    parts, z_sums, pairs, shares = [None] * sums, [None] * sums, [], []
+    result = {}
+
+    def weight_grad(i):
+        send, keep = call(
+            functools.partial(weight_grad_kernel, chunk=i),
+            "weight_grad",
+            (attn_t, dy_own, dy_far),
+            [((2, 2, owned, cols), bf16)] * 2,
+            limit=16,
+        )
+        parts[i] = (keep, move(send, gather_far))
+
+    def gather_near_step(i):
+        (near[i],) = call(gather_pick_kernel, "gather_pick", z_parts[i], [((owned, model), bf16)])
+        joined[i] = move(near[i], gather_near)
+
+    def gather_far_step(i):
+        (pair,) = call(pair_kernel, "pair", (near[i], joined[i]), [((2, owned, model), bf16)])
+        weights[2 * i], weights[2 * i + 1] = pair, move(pair, gather_far)
+
+    def second_sum(i):
+        send, kept = call(
+            second_sum_kernel,
+            "second_sum",
+            parts[i],
+            [((2, owned, cols), bf16), ((2, owned, cols), f32)],
+        )
+        parts[i] = (kept, move(send, gather_near))
+
+    def z_sum(i):
+        to_first, to_second, own = call(
+            z_sum_kernel,
+            "z_sum",
+            parts[i],
+            [((owned, cols), bf16)] * 2 + [((owned, cols), f32)],
+        )
+        z_sums[i] = own, move(to_first, scatter_first), move(to_second, scatter_second)
+
+    def share(i):
+        (part,) = call(share_kernel, "share", z_sums[i], [((owned, cols), f32)])
+        shares.extend([part, swap_core(part)])
+
+    def attn_grad():
+        result["grad"] = call(
+            attn_grad_kernel,
+            "attn_grad",
+            (attn_t, dy_own, dy_far, *weights),
+            [((mine, tokens), bf16), ((mine // HD, tokens), f32), ((mine, model), bf16)],
+            limit=24,
+        )
+
+    def projection():
+        out_send, out_own = call(
+            projection_kernel,
+            "projection",
+            (attn, result["grad"][2]),
+            [((rows, model), bf16), ((rows, model), f32)],
+            limit=16,
+        )
+        result["out"] = (out_own, swap_core(out_send))
+
+    def backward(heads):
+        send, own = call(
+            functools.partial(backward_kernel, heads=heads),
+            "backward",
+            (rot_q, rot_k, rot_kt, values, *result["grad"][:2], lse, bias, cos, sin),
+            [((3, rows, len(heads) * HD), bf16)] * 2,
+            limit=24,
+        )
+        pairs.extend([own, swap_core(send)])
+
+    def layer_out():
+        (result["layer_out"],) = call(layer_out_kernel, "layer_out", result["out"], [((rows, model), bf16)], final=True)
+
+    def grads():
+        result["grads"] = call(grads_kernel, "grads", pairs, [((rows, width), bf16)] * 3, final=True)
+
+    def mean():
+        (result["weight_grad"],) = call(
+            functools.partial(mean_kernel, count=lax.axis_size("dp")), "mean", shares, [((owned, model), f32)], final=True
+        )
+
+    weight_grad(0)
+    gather_near_step(0)
+    weight_grad(1)
+    gather_near_step(1)
+    gather_far_step(0)
+    second_sum(0)
+    gather_far_step(1)
+    second_sum(1)
+    z_sum(0)
+    z_sum(1)
+    attn_grad()
+    share(0)
+    backward((0,1))
+    share(1)
+    projection()
+    backward((2,3))
+    grads()
+    mean()
+    layer_out()
+    return (result["layer_out"][None], *[g[None] for g in result["grads"]], result["weight_grad"])
+
 
 def solution(mesh):
     in_specs = (
@@ -236,4 +731,5 @@
         P("dp", "ctx", None),
         P("dp", None),
     )
-    return jax.shard_map(shards, mesh=mesh, in_specs=in_specs, out_specs=out_specs, check_vma=False)
+    body = chip_shards if (mesh.shape["dp"], mesh.shape["ctx"]) == (16, 2) else shards
+    return jax.shard_map(body, mesh=mesh, in_specs=in_specs, out_specs=out_specs, check_vma=False)

time: 301 us -> 71.1 us (0.24)
  waiting for transfers between devices: 115 us -> 27.9 us
  local copies, waits for them, and re-layouts: 79.3 us -> 0.02 us
  other arithmetic: 44.3 us -> 0 us
  matrix products: 34 us -> 0 us
  Pallas kernels: 0 us -> 19.1 us
  between operations: 14.1 us -> 0.87 us
  starting transfers between devices: 13.6 us -> 23 us
    reduce_scatter x1 -> x0, waiting for transfers between devices: 72.3 us -> none  [shards(): lax.psum_scatter(lax.dot_general(attn, grad_rows, (((0,), (0,)), ((), ())...]
    dot_general x9 -> x0, matrix products: 34 us -> none  [the longest x1 5.7 us: shards(): lax.dot_general(attn, grad_rows, (((0,), (0,)), ((), ())), preferred_elem...]
    ppermute x4 -> x22, waiting for transfers between devices: 0.01 us -> 27.9 us  [the longest x14 24.6 us: move(): return lax.ppermute(array, ('dp', 'ctx'), chip_moves(rule))]
    all_gather x1 -> x0, waiting for transfers between devices: 27.3 us -> none  [shards(): forward_weight = lax.all_gather(out_weight, 'dp', axis=0, tiled=True)]
    slice x12 -> x0, local copies, waits for them, and re-layouts: 26.6 us -> none  [the longest x2 7.85 us: shards(): own_part = accumulated[row_count:2 * row_count]]
    pallas_call x0 -> x21, Pallas kernels: none -> 19.1 us  [call(): pl.pallas_call(kernel, in_specs=list(specs or [in_vmem] * len(args)) + [a...]
    scatter-add x1 -> x0, other arithmetic: 17.5 us -> none  [shards(): accumulated = jnp.zeros((3 * local_blocks, BLK, 2, H, HD), jnp.float32).a...]
    psum x1 -> x0, waiting for transfers between devices: 14.4 us -> none  [shards(): weight_grad = lax.psum(local_grad, 'ctx')]
  transfers between devices with their start and end apart: 7 -> 22, of which waited for: 3 -> 11; matrix products, arithmetic and copies ran while one was open for 51% -> 0% of each run, Pallas kernels for 0% -> 23%
where the time goes in v2:
time: 71.1 us; the launch traced here: 70.9 us
  waiting for transfers between devices  27.9 us (39%)
  starting transfers between devices  23 us (32%)
  Pallas kernels  19.1 us (27%)
  between operations  0.87 us (1%)
    ppermute x14, waiting for transfers between devices, move(): return lax.ppermute(array, ('dp', 'ctx'), chip_moves(rule))  24.6 us
    ppermute x14, starting transfers between devices, move(): return lax.ppermute(array, ('dp', 'ctx'), chip_moves(rule))  21.2 us
    pallas_call x21, Pallas kernels, call(): pl.pallas_call(kernel, in_specs=list(specs or [in_vmem] * len(args)) + [a...  19.1 us
    ppermute x8, waiting for transfers between devices, swap_core(): return lax.ppermute(array, 'ctx', [(0, 1), (1, 0)])  3.22 us
    ppermute x8, starting transfers between devices, swap_core(): return lax.ppermute(array, 'ctx', [(0, 1), (1, 0)])  1.86 us
  transfers between devices with their start and end apart: 22, of which 11 were waited for; matrix products, arithmetic and copies ran while one was open for 0% of the time, Pallas kernels for 23%

profile of v2, /device:TPU:0, one launch (start us, length us, event | category | flops | bytes accessed | tf_op | source)
XLA Modules:
  0.0 70.9 jit_solution(7737332637234481860)
XLA Ops:
  0.6 0.0 copy-start.1
  0.7 0.5 collective-permute-start.2
  1.2 1.2 %pack.1 = bf16[3,256,512]{2,1,0:T(8,128)(2,1)S(1)} custom-call(bf16[256,1024]{1,0:T(8,128)(2,1)} %bitcast.12, bf16[256,1024]{1,0:T(8,128)(2,1)} %bitcast.14, bf16[256,1024]{1,0:T(8,128)(2,1)} %bitcast.16), custom_call_target="tpu_custom_call" | custom-call | flops 1 | bytes 1 | tf_op jit(solution)/shard_map/pack/pallas_call | solution.py:563
  2.4 0.1 collective-permute-start.1
  2.5 0.0 copy-done.1
  2.5 4.0 %collective-permute-start.3 = (bf16[64,2048]{1,0:T(8,128)(2,1)S(1)}, bf16[64,2048]{1,0:T(8,128)(2,1)S(1)}, u32[]{:S(2)}, u32[]{:S(2)}) collective-permute-start(bf16[64,2048]{1,0:T(8,128)(2,1)S(1)} %copy-done.1), channel_id=1, source_target_pairs={{0,16},{1,8},{2,18},{3,10},{4,20},{5,12},{6,22},{7,14},{8,24},{9,0... | collective-permute-start | bytes 786440 | tf_op jit(solution)/shard_map/ppermute | solution.py:246
  6.6 0.0 collective-permute-start
  6.6 1.1 %collective-permute-done.far = s32[1,256]{1,0:T(1,128)S(1)} collective-permute-done((s32[1,256]{1,0:T(1,128)S(1)}, s32[1,256]{1,0:T(1,128)S(1)}, u32[]{:S(2)}, u32[]{:S(2)}) %collective-permute-start) | collective-permute-done | bytes 1056 | tf_op jit(solution)/shard_map/ppermute | solution.py:250
  7.7 0.0 collective-permute-done.1.received
  7.7 0.0 copy-done.2
  7.7 5.3 %forward.1 = (bf16[512,512]{1,0:T(8,128)(2,1)S(1)}, bf16[512,512]{1,0:T(8,128)(2,1)S(1)}, bf16[512,512]{1,0:T(8,128)(2,1)S(1)}, bf16[512,512]{1,0:T(8,128)(2,1)S...) custom-call(s32[1,4,4]{2,1,0:T(4,128)S(1)} %copy-done.2, ...), custom_call_target="tpu_custom_call" | custom-call | flops 1 | bytes 1 | tf_op jit(solution)/shard_map/forward/pallas_call | solution.py:563
  13.0 0.0 collective-permute-done.2.other
  13.0 1.4 %weight_grad.2 = (bf16[2,2,64,1024]{3,2,1,0:T(8,128)(2,1)S(1)}, bf16[2,2,64,1024]{3,2,1,0:T(8,128)(2,1)S(1)}) custom-call(bf16[512,512]{1,0:T(8,128)(2,1)S(1)} %get-tuple-element.42.attn_t, bf16[256,2048]{1,0:T(8,128)(2,1)S(1)} %bitcast.9, bf16[256,2048]{1,0:T(8,128)(2,1)S(1)} %collective-permute-done.2.other, ...), custom_call_target="tpu_custom_call" | custom-call | flops 1 | bytes 1 | tf_op jit(solution)/shard_map/weight_grad/pallas_call | solution.py:563
  14.4 1.6 %collective-permute-start.8 = (bf16[2,2,64,1024]{3,2,1,0:T(8,128)(2,1)S(1)}, bf16[2,2,64,1024]{3,2,1,0:T(8,128)(2,1)S(1)}, u32[]{:S(2)}, u32[]{:S(2)}) collective-permute-start(bf16[2,2,64,1024]{3,2,1,0:T(8,128)(2,1)S(1)} %get-tuple-element.44.refs_0_), channel_id=1, source_target_pairs={{0,2},{1,5},{2,0},{3,7},{4,6},{5,1},{6,4},{7,3},{8,10},{9,13},{10,... | collective-permute-start | bytes 1572872 | tf_op jit(solution)/shard_map/ppermute | solution.py:246
  15.9 3.8 %collective-permute-start.5 = (bf16[64,2048]{1,0:T(8,128)(2,1)S(1)}, bf16[64,2048]{1,0:T(8,128)(2,1)S(1)}, u32[]{:S(2)}, u32[]{:S(2)}) collective-permute-start(bf16[64,2048]{1,0:T(8,128)(2,1)S(1)} %copy-done.1), channel_id=1, source_target_pairs={{0,24},{2,26},{4,28},{6,30},{8,16},{10,18},{12,20},{14,22},{17,9},... | collective-permute-start | bytes 786440 | tf_op jit(solution)/shard_map/ppermute | solution.py:246
  19.7 0.0 collective-permute-done.3.away.home
  19.8 1.4 %weight_grad.3 = (bf16[2,2,64,1024]{3,2,1,0:T(8,128)(2,1)S(1)}, bf16[2,2,64,1024]{3,2,1,0:T(8,128)(2,1)S(1)}) custom-call(bf16[512,512]{1,0:T(8,128)(2,1)S(1)} %get-tuple-element.42.attn_t, bf16[256,2048]{1,0:T(8,128)(2,1)S(1)} %bitcast.10, bf16[256,2048]{1,0:T(8,128)(2,1)S(1)} %collective-permute-done.2.other, bf16[64,2048]{1,0:T(8,128)(2,1)S(1)} %gather_pick.2.refs_0_.a), custom_call_target="tpu_custom_call" | custom-call | flops 1 | bytes 1 | tf_op jit(solution)/shard_map/weight_grad/pallas_call | solution.py:563
  21.1 0.6 collective-permute-start.10
  21.7 1.5 %collective-permute-start.4 = (bf16[64,2048]{1,0:T(8,128)(2,1)S(1)}, bf16[64,2048]{1,0:T(8,128)(2,1)S(1)}, u32[]{:S(2)}, u32[]{:S(2)}) collective-permute-start(bf16[64,2048]{1,0:T(8,128)(2,1)S(1)} %gather_pick.2.refs_0_.a), channel_id=1, source_target_pairs={{0,4},{1,3},{2,6},{3,1},{4,0},{5,7},{6,2},{7,5},{8,12},{9,11},{10,... | collective-permute-start | bytes 786440 | tf_op jit(solution)/shard_map/ppermute | solution.py:246
  23.2 0.4 collective-permute-done.5.away
  23.6 1.6 %collective-permute-start.7 = (bf16[64,2048]{1,0:T(8,128)(2,1)S(1)}, bf16[64,2048]{1,0:T(8,128)(2,1)S(1)}, u32[]{:S(2)}, u32[]{:S(2)}) collective-permute-start(bf16[64,2048]{1,0:T(8,128)(2,1)S(1)} %gather_pick.3.refs_0_.a), channel_id=1, source_target_pairs={{0,4},{1,3},{2,6},{3,1},{4,0},{5,7},{6,2},{7,5},{8,12},{9,11},{10,... | collective-permute-start | bytes 786440 | tf_op jit(solution)/shard_map/ppermute | solution.py:246
  25.2 5.8 %collective-permute-done.4.b = bf16[64,2048]{1,0:T(8,128)(2,1)S(1)} collective-permute-done((bf16[64,2048]{1,0:T(8,128)(2,1)S(1)}, bf16[64,2048]{1,0:T(8,128)(2,1)S(1)}, u32[]{:S(2)}, u32[]{:S(2)}) %collective-permute-start.4) | collective-permute-done | bytes 262176 | tf_op jit(solution)/shard_map/ppermute | solution.py:246
  31.0 1.6 %collective-permute-start.6 = (bf16[2,64,2048]{2,1,0:T(8,128)(2,1)S(1)}, bf16[2,64,2048]{2,1,0:T(8,128)(2,1)S(1)}, u32[]{:S(2)}, u32[]{:S(2)}) collective-permute-start(bf16[2,64,2048]{2,1,0:T(8,128)(2,1)S(1)} %pair.2.refs_0_), channel_id=1, source_target_pairs={{0,2},{1,5},{2,0},{3,7},{4,6},{5,1},{6,4},{7,3},{8,10},{9,13},{10,... | collective-permute-start | bytes 1572872 | tf_op jit(solution)/shard_map/ppermute | solution.py:246
  32.6 0.0 collective-permute-done.8.got
  32.6 0.1 second_sum.2
  32.7 3.9 %collective-permute-done.7.b = bf16[64,2048]{1,0:T(8,128)(2,1)S(1)} collective-permute-done((bf16[64,2048]{1,0:T(8,128)(2,1)S(1)}, bf16[64,2048]{1,0:T(8,128)(2,1)S(1)}, u32[]{:S(2)}, u32[]{:S(2)}) %collective-permute-start.7) | collective-permute-done | bytes 262176 | tf_op jit(solution)/shard_map/ppermute | solution.py:246
  36.6 1.6 %collective-permute-start.9 = (bf16[2,64,2048]{2,1,0:T(8,128)(2,1)S(1)}, bf16[2,64,2048]{2,1,0:T(8,128)(2,1)S(1)}, u32[]{:S(2)}, u32[]{:S(2)}) collective-permute-start(bf16[2,64,2048]{2,1,0:T(8,128)(2,1)S(1)} %pair.3.refs_0_.refs_2_), channel_id=1, source_target_pairs={{0,2},{1,5},{2,0},{3,7},{4,6},{5,1},{6,4},{7,3},{8,10},{9,13},{10,... | collective-permute-start | bytes 1572872 | tf_op jit(solution)/shard_map/ppermute | solution.py:246
  38.2 1.5 %collective-permute-start.12 = (bf16[2,64,1024]{2,1,0:T(8,128)(2,1)S(1)}, bf16[2,64,1024]{2,1,0:T(8,128)(2,1)S(1)}, u32[]{:S(2)}, u32[]{:S(2)}) collective-permute-start(bf16[2,64,1024]{2,1,0:T(8,128)(2,1)S(1)} %get-tuple-element.47.refs_0_), channel_id=1, source_target_pairs={{0,4},{1,3},{2,6},{3,1},{4,0},{5,7},{6,2},{7,5},{8,12},{9,11},{10,... | collective-permute-start | bytes 786440 | tf_op jit(solution)/shard_map/ppermute | solution.py:246
  39.7 0.0 collective-permute-done.10.got
  39.7 0.1 second_sum.3
  39.8 0.6 collective-permute-start.11
  40.4 7.0 %collective-permute-done.12.got = bf16[2,64,1024]{2,1,0:T(8,128)(2,1)S(1)} collective-permute-done((bf16[2,64,1024]{2,1,0:T(8,128)(2,1)S(1)}, bf16[2,64,1024]{2,1,0:T(8,128)(2,1)S(1)}, u32[]{:S(2)}, u32[]{:S(2)}) %collective-permute-start.12) | collective-permute-done | bytes 262176 | tf_op jit(solution)/shard_map/ppermute | solution.py:246
  47.4 0.1 z_sum.2
  47.5 0.1 collective-permute-start.15
  47.6 1.3 %collective-permute-start.16 = (bf16[64,1024]{1,0:T(8,128)(2,1)S(1)}, bf16[64,1024]{1,0:T(8,128)(2,1)S(1)}, u32[]{:S(2)}, u32[]{:S(2)}) collective-permute-start(bf16[64,1024]{1,0:T(8,128)(2,1)S(1)} %get-tuple-element.67), channel_id=1, source_target_pairs={{1,25},{3,27},{5,29},{7,31},{9,17},{11,19},{13,21},{15,23},{16,8},... | collective-permute-start | bytes 393224 | tf_op jit(solution)/shard_map/ppermute | solution.py:246
  48.9 2.0 %collective-permute-done.11.got = bf16[2,64,1024]{2,1,0:T(8,128)(2,1)S(1)} collective-permute-done((bf16[2,64,1024]{2,1,0:T(8,128)(2,1)S(1)}, bf16[2,64,1024]{2,1,0:T(8,128)(2,1)S(1)}, u32[]{:S(2)}, u32[]{:S(2)}) %collective-permute-start.11) | collective-permute-done | bytes 262176 | tf_op jit(solution)/shard_map/ppermute | solution.py:246
  50.9 0.1 z_sum.3
  51.0 0.1 collective-permute-start.13
  51.1 0.0 collective-permute-done.6.refs_1_
  51.1 1.5 %collective-permute-start.14 = (bf16[64,1024]{1,0:T(8,128)(2,1)S(1)}, bf16[64,1024]{1,0:T(8,128)(2,1)S(1)}, u32[]{:S(2)}, u32[]{:S(2)}) collective-permute-start(bf16[64,1024]{1,0:T(8,128)(2,1)S(1)} %get-tuple-element.56), channel_id=1, source_target_pairs={{1,25},{3,27},{5,29},{7,31},{9,17},{11,19},{13,21},{15,23},{16,8},... | collective-permute-start | bytes 393224 | tf_op jit(solution)/shard_map/ppermute | solution.py:246
  52.6 0.0 collective-permute-done.9.refs_3_
  52.6 1.5 %attn_grad.1 = (bf16[512,512]{1,0:T(8,128)(2,1)S(1)}, f32[4,512]{1,0:T(4,128)S(1)}, bf16[512,2048]{1,0:T(8,128)(2,1)S(1)}) custom-call(bf16[512,512]{1,0:T(8,128)(2,1)S(1)} %get-tuple-element.42.attn_t, bf16[256,2048]{1,0:T(8,128)(2,1)S(1)} %bitcast.11, bf16[256,2048]{1,0:T(8,128)(2,1)S(1)} %collective-permute-done.2.other, ...), custom_call_target="tpu_custom_call" | custom-call | flops 1 | bytes 1 | tf_op jit(solution)/shard_map/attn_grad/pallas_call | solution.py:563
  54.1 0.2 collective-permute-done.15.first
  54.3 3.4 %collective-permute-done.16.second = bf16[64,1024]{1,0:T(8,128)(2,1)S(1)} collective-permute-done((bf16[64,1024]{1,0:T(8,128)(2,1)S(1)}, bf16[64,1024]{1,0:T(8,128)(2,1)S(1)}, u32[]{:S(2)}, u32[]{:S(2)}) %collective-permute-start.16) | collective-permute-done | bytes 131104 | tf_op jit(solution)/shard_map/ppermute | solution.py:246
  57.7 0.1 share.2.refs_0_
  57.7 1.6 %backward.2 = (bf16[3,256,256]{2,1,0:T(8,128)(2,1)S(1)}, bf16[3,256,256]{2,1,0:T(8,128)(2,1)S(1)}) custom-call(bf16[512,512]{1,0:T(8,128)(2,1)S(1)} %get-tuple-element.43.refs_0_.rot_q, bf16[512,512]{1,0:T(8,128)(2,1)S(1)} %get-tuple-element.57.rot_k, bf16[512,512]{1,0:T(8,128)(2,1)S(1)} %get-tuple-element.58.rot_kt, ...), custom_call_target="tpu_custom_call" | custom-call | flops 1 | bytes 1 | tf_op jit(solution)/shard_map/backward/pallas_call | solution.py:563
  59.3 1.9 %collective-permute-done.13.first = bf16[64,1024]{1,0:T(8,128)(2,1)S(1)} collective-permute-done((bf16[64,1024]{1,0:T(8,128)(2,1)S(1)}, bf16[64,1024]{1,0:T(8,128)(2,1)S(1)}, u32[]{:S(2)}, u32[]{:S(2)}) %collective-permute-start.13) | collective-permute-done | bytes 131104 | tf_op jit(solution)/shard_map/ppermute | solution.py:246
  61.3 0.0 collective-permute-done.14.second
  61.3 0.1 share.3.refs_0_.refs_2_
  61.3 1.3 %projection.1 = (bf16[256,2048]{1,0:T(8,128)(2,1)S(1)}, f32[256,2048]{1,0:T(8,128)S(1)}) custom-call(bf16[512,512]{1,0:T(8,128)(2,1)S(1)} %get-tuple-element.41.attn, bf16[512,2048]{1,0:T(8,128)(2,1)S(1)} %get-tuple-element.54.weight, f32[64,1024]{1,0:T(8,128)S(1)} %share.3.refs_0_.refs_2_), custom_call_target="tpu_custom_call" | custom-call | flops 1 | bytes 1 | tf_op jit(solution)/shard_map/projection/pallas_call | solution.py:563
  62.6 0.1 collective-permute-start.17
  62.7 1.6 %backward.3 = (bf16[3,256,256]{2,1,0:T(8,128)(2,1)S(1)}, bf16[3,256,256]{2,1,0:T(8,128)(2,1)S(1)}) custom-call(bf16[512,512]{1,0:T(8,128)(2,1)S(1)} %get-tuple-element.43.refs_0_.rot_q, bf16[512,512]{1,0:T(8,128)(2,1)S(1)} %get-tuple-element.57.rot_k, bf16[512,512]{1,0:T(8,128)(2,1)S(1)} %get-tuple-element.58.rot_kt, ...), custom_call_target="tpu_custom_call" | custom-call | flops 1 | bytes 1 | tf_op jit(solution)/shard_map/backward/pallas_call | solution.py:563
  64.3 0.6 collective-permute-start.19
  64.9 0.1 collective-permute-start.18
  64.9 0.4 collective-permute-start.21
  65.4 0.1 collective-permute-start.20
  65.4 1.7 %collective-permute-done.21.refs_3_ = f32[64,1024]{1,0:T(8,128)S(1)} collective-permute-done((f32[64,1024]{1,0:T(8,128)S(1)}, f32[64,1024]{1,0:T(8,128)S(1)}, u32[]{:S(2)}, u32[]{:S(2)}) %collective-permute-start.21) | collective-permute-done | bytes 262176 | tf_op jit(solution)/shard_map/ppermute | solution.py:250
  67.1 0.4 collective-permute-done.20.refs_1_
  67.5 0.9 %mean.1 = f32[64,2048]{1,0:T(8,128)} custom-call(f32[64,1024]{1,0:T(8,128)S(1)} %share.2.refs_0_, f32[64,1024]{1,0:T(8,128)S(1)} %collective-permute-done.20.refs_1_, f32[64,1024]{1,0:T(8,128)S(1)} %share.3.refs_0_.refs_2_, f32[64,1024]{1,0:T(8,128)S(1)} %collective-permute-done.21.refs_3_, bf16[3,256,256]{2,1,0:T(8,128)(2,1)S(1)} %get-tuple-element.71.refs_0_.refs_4_), custom_call_target="tpu_custom_call" | custom-call | flops 1 | bytes 1 | tf_op jit(solution)/shard_map/mean/pallas_call | solution.py:563
  68.4 0.0 collective-permute-done.19.refs_3_
  68.4 0.0 collective-permute-done.18.refs_1_
  68.4 1.4 %grads.1 = (bf16[256,1024]{1,0:T(8,128)(2,1)}, bf16[256,1024]{1,0:T(8,128)(2,1)}, bf16[256,1024]{1,0:T(8,128)(2,1)}) custom-call(bf16[3,256,256]{2,1,0:T(8,128)(2,1)S(1)} %get-tuple-element.72.refs_0_, bf16[3,256,256]{2,1,0:T(8,128)(2,1)S(1)} %collective-permute-done.18.refs_1_, bf16[3,256,256]{2,1,0:T(8,128)(2,1)S(1)} %get-tuple-element.73.refs_2_, ...), custom_call_target="tpu_custom_call" | custom-call | flops 1 | bytes 1 | tf_op jit(solution)/shard_map/grads/pallas_call | solution.py:563
  69.7 0.0 collective-permute-done.17.got
  69.7 1.2 %layer_out.1 = bf16[256,2048]{1,0:T(8,128)(2,1)} custom-call(f32[256,2048]{1,0:T(8,128)S(1)} %get-tuple-element.69.own, bf16[256,2048]{1,0:T(8,128)(2,1)S(1)} %collective-permute-done.17.got, bf16[3,256,256]{2,1,0:T(8,128)(2,1)S(1)} %get-tuple-element.71.refs_0_.refs_4_), custom_call_target="tpu_custom_call" | custom-call | flops 1 | bytes 1 | tf_op jit(solution)/shard_map/layer_out/pallas_call | solution.py:563
  (9 shorter events, 0.1 us)
Async XLA Ops:
  0.6 1.9 %copy-start.1 = (bf16[64,2048]{1,0:T(8,128)(2,1)S(1)}, bf16[64,2048]{1,0:T(8,128)(2,1)}, u32[]{:S(2)}) copy-start(bf16[64,2048]{1,0:T(8,128)(2,1)} %home.1) | copy-start | bytes 786436
  0.6 5.9 %copy-start.3 = (s32[1,256]{1,0:T(1,128)S(1)}, s32[1,256]{1,0:T(1,128)}, u32[]{:S(2)}) copy-start(s32[1,256]{1,0:T(1,128)} %near.1) | copy-start | bytes 3076
  0.7 7.1 %copy-start.2 = (s32[1,4,4]{2,1,0:T(4,128)S(1)}, s32[1,4,4]{2,1,0:T(4,128)}, u32[]{:S(2)}) copy-start(s32[1,4,4]{2,1,0:T(4,128)} %pattern.1) | copy-start | bytes 196
  0.7 12.3 %collective-permute-start.2 = (bf16[256,2048]{1,0:T(8,128)(2,1)}, bf16[256,2048]{1,0:T(8,128)(2,1)S(1)}, u32[]{:S(2)}, u32[]{:S(2)}) collective-permute-start(bf16[256,2048]{1,0:T(8,128)(2,1)} %bitcast.8), channel_id=1, source_target_pairs={{0,1},{1,0},{2,3},{3,2},{4,5},{5,4},{6,7},{7,6},{8,9},{9,8},{10,11... | collective-permute-start | bytes 3145736 | tf_op jit(solution)/shard_map/ppermute | solution.py:250
  1.2 11.8 %copy-start = (bf16[1,256,2048]{2,1,0:T(8,128)(2,1)S(1)}, bf16[1,256,2048]{2,1,0:T(8,128)(2,1)}, u32[]{:S(2)}) copy-start(bf16[1,256,2048]{2,1,0:T(8,128)(2,1)} %param.13) | copy-start | bytes 3145732
  2.4 5.3 %collective-permute-start.1 = (bf16[3,256,512]{2,1,0:T(8,128)(2,1)S(1)}, bf16[3,256,512]{2,1,0:T(8,128)(2,1)S(1)}, u32[]{:S(2)}, u32[]{:S(2)}) collective-permute-start(bf16[3,256,512]{2,1,0:T(8,128)(2,1)S(1)} %pack.1), channel_id=1, source_target_pairs={{0,1},{1,0},{2,3},{3,2},{4,5},{5,4},{6,7},{7,6},{8,9},{9,8},{10,11... | collective-permute-start | bytes 2359304 | tf_op jit(solution)/shard_map/ppermute | solution.py:250
  2.5 17.2 %collective-permute-start.3 = (bf16[64,2048]{1,0:T(8,128)(2,1)S(1)}, bf16[64,2048]{1,0:T(8,128)(2,1)S(1)}, u32[]{:S(2)}, u32[]{:S(2)}) collective-permute-start(bf16[64,2048]{1,0:T(8,128)(2,1)S(1)} %copy-done.1), channel_id=1, source_target_pairs={{0,16},{1,8},{2,18},{3,10},{4,20},{5,12},{6,22},{7,14},{8,24},{9,0... | collective-permute-start | bytes 786440 | tf_op jit(solution)/shard_map/ppermute | solution.py:246
  6.6 1.1 %collective-permute-start = (s32[1,256]{1,0:T(1,128)S(1)}, s32[1,256]{1,0:T(1,128)S(1)}, u32[]{:S(2)}, u32[]{:S(2)}) collective-permute-start(s32[1,256]{1,0:T(1,128)S(1)} %copy-done.3), channel_id=1, source_target_pairs={{0,1},{1,0},{2,3},{3,2},{4,5},{5,4},{6,7},{7,6},{8,9},{9,8},{10,11... | collective-permute-start | bytes 3080 | tf_op jit(solution)/shard_map/ppermute | solution.py:250
  14.4 18.2 %collective-permute-start.8 = (bf16[2,2,64,1024]{3,2,1,0:T(8,128)(2,1)S(1)}, bf16[2,2,64,1024]{3,2,1,0:T(8,128)(2,1)S(1)}, u32[]{:S(2)}, u32[]{:S(2)}) collective-permute-start(bf16[2,2,64,1024]{3,2,1,0:T(8,128)(2,1)S(1)} %get-tuple-element.44.refs_0_), channel_id=1, source_target_pairs={{0,2},{1,5},{2,0},{3,7},{4,6},{5,1},{6,4},{7,3},{8,10},{9,13},{10,... | collective-permute-start | bytes 1572872 | tf_op jit(solution)/shard_map/ppermute | solution.py:246
  15.9 7.7 %collective-permute-start.5 = (bf16[64,2048]{1,0:T(8,128)(2,1)S(1)}, bf16[64,2048]{1,0:T(8,128)(2,1)S(1)}, u32[]{:S(2)}, u32[]{:S(2)}) collective-permute-start(bf16[64,2048]{1,0:T(8,128)(2,1)S(1)} %copy-done.1), channel_id=1, source_target_pairs={{0,24},{2,26},{4,28},{6,30},{8,16},{10,18},{12,20},{14,22},{17,9},... | collective-permute-start | bytes 786440 | tf_op jit(solution)/shard_map/ppermute | solution.py:246
  21.1 18.6 %collective-permute-start.10 = (bf16[2,2,64,1024]{3,2,1,0:T(8,128)(2,1)S(1)}, bf16[2,2,64,1024]{3,2,1,0:T(8,128)(2,1)S(1)}, u32[]{:S(2)}, u32[]{:S(2)}) collective-permute-start(bf16[2,2,64,1024]{3,2,1,0:T(8,128)(2,1)S(1)} %get-tuple-element.45.refs_0_), channel_id=1, source_target_pairs={{0,2},{1,5},{2,0},{3,7},{4,6},{5,1},{6,4},{7,3},{8,10},{9,13},{10,... | collective-permute-start | bytes 1572872 | tf_op jit(solution)/shard_map/ppermute | solution.py:246
  21.7 9.2 %collective-permute-start.4 = (bf16[64,2048]{1,0:T(8,128)(2,1)S(1)}, bf16[64,2048]{1,0:T(8,128)(2,1)S(1)}, u32[]{:S(2)}, u32[]{:S(2)}) collective-permute-start(bf16[64,2048]{1,0:T(8,128)(2,1)S(1)} %gather_pick.2.refs_0_.a), channel_id=1, source_target_pairs={{0,4},{1,3},{2,6},{3,1},{4,0},{5,7},{6,2},{7,5},{8,12},{9,11},{10,... | collective-permute-start | bytes 786440 | tf_op jit(solution)/shard_map/ppermute | solution.py:246
  23.6 13.0 %collective-permute-start.7 = (bf16[64,2048]{1,0:T(8,128)(2,1)S(1)}, bf16[64,2048]{1,0:T(8,128)(2,1)S(1)}, u32[]{:S(2)}, u32[]{:S(2)}) collective-permute-start(bf16[64,2048]{1,0:T(8,128)(2,1)S(1)} %gather_pick.3.refs_0_.a), channel_id=1, source_target_pairs={{0,4},{1,3},{2,6},{3,1},{4,0},{5,7},{6,2},{7,5},{8,12},{9,11},{10,... | collective-permute-start | bytes 786440 | tf_op jit(solution)/shard_map/ppermute | solution.py:246
  31.0 20.1 %collective-permute-start.6 = (bf16[2,64,2048]{2,1,0:T(8,128)(2,1)S(1)}, bf16[2,64,2048]{2,1,0:T(8,128)(2,1)S(1)}, u32[]{:S(2)}, u32[]{:S(2)}) collective-permute-start(bf16[2,64,2048]{2,1,0:T(8,128)(2,1)S(1)} %pair.2.refs_0_), channel_id=1, source_target_pairs={{0,2},{1,5},{2,0},{3,7},{4,6},{5,1},{6,4},{7,3},{8,10},{9,13},{10,... | collective-permute-start | bytes 1572872 | tf_op jit(solution)/shard_map/ppermute | solution.py:246
  36.6 16.0 %collective-permute-start.9 = (bf16[2,64,2048]{2,1,0:T(8,128)(2,1)S(1)}, bf16[2,64,2048]{2,1,0:T(8,128)(2,1)S(1)}, u32[]{:S(2)}, u32[]{:S(2)}) collective-permute-start(bf16[2,64,2048]{2,1,0:T(8,128)(2,1)S(1)} %pair.3.refs_0_.refs_2_), channel_id=1, source_target_pairs={{0,2},{1,5},{2,0},{3,7},{4,6},{5,1},{6,4},{7,3},{8,10},{9,13},{10,... | collective-permute-start | bytes 1572872 | tf_op jit(solution)/shard_map/ppermute | solution.py:246
  38.2 9.2 %collective-permute-start.12 = (bf16[2,64,1024]{2,1,0:T(8,128)(2,1)S(1)}, bf16[2,64,1024]{2,1,0:T(8,128)(2,1)S(1)}, u32[]{:S(2)}, u32[]{:S(2)}) collective-permute-start(bf16[2,64,1024]{2,1,0:T(8,128)(2,1)S(1)} %get-tuple-element.47.refs_0_), channel_id=1, source_target_pairs={{0,4},{1,3},{2,6},{3,1},{4,0},{5,7},{6,2},{7,5},{8,12},{9,11},{10,... | collective-permute-start | bytes 786440 | tf_op jit(solution)/shard_map/ppermute | solution.py:246
  39.8 11.1 %collective-permute-start.11 = (bf16[2,64,1024]{2,1,0:T(8,128)(2,1)S(1)}, bf16[2,64,1024]{2,1,0:T(8,128)(2,1)S(1)}, u32[]{:S(2)}, u32[]{:S(2)}) collective-permute-start(bf16[2,64,1024]{2,1,0:T(8,128)(2,1)S(1)} %get-tuple-element.50.refs_0_), channel_id=1, source_target_pairs={{0,4},{1,3},{2,6},{3,1},{4,0},{5,7},{6,2},{7,5},{8,12},{9,11},{10,... | collective-permute-start | bytes 786440 | tf_op jit(solution)/shard_map/ppermute | solution.py:246
  47.5 6.7 %collective-permute-start.15 = (bf16[64,1024]{1,0:T(8,128)(2,1)S(1)}, bf16[64,1024]{1,0:T(8,128)(2,1)S(1)}, u32[]{:S(2)}, u32[]{:S(2)}) collective-permute-start(bf16[64,1024]{1,0:T(8,128)(2,1)S(1)} %get-tuple-element.52.refs_0_), channel_id=1, source_target_pairs={{0,9},{1,17},{2,11},{3,19},{4,13},{5,21},{6,15},{7,23},{8,1},{9,25... | collective-permute-start | bytes 393224 | tf_op jit(solution)/shard_map/ppermute | solution.py:246
  47.6 10.1 %collective-permute-start.16 = (bf16[64,1024]{1,0:T(8,128)(2,1)S(1)}, bf16[64,1024]{1,0:T(8,128)(2,1)S(1)}, u32[]{:S(2)}, u32[]{:S(2)}) collective-permute-start(bf16[64,1024]{1,0:T(8,128)(2,1)S(1)} %get-tuple-element.67), channel_id=1, source_target_pairs={{1,25},{3,27},{5,29},{7,31},{9,17},{11,19},{13,21},{15,23},{16,8},... | collective-permute-start | bytes 393224 | tf_op jit(solution)/shard_map/ppermute | solution.py:246
  51.0 10.3 %collective-permute-start.13 = (bf16[64,1024]{1,0:T(8,128)(2,1)S(1)}, bf16[64,1024]{1,0:T(8,128)(2,1)S(1)}, u32[]{:S(2)}, u32[]{:S(2)}) collective-permute-start(bf16[64,1024]{1,0:T(8,128)(2,1)S(1)} %get-tuple-element.53.refs_4_), channel_id=1, source_target_pairs={{0,9},{1,17},{2,11},{3,19},{4,13},{5,21},{6,15},{7,23},{8,1},{9,25... | collective-permute-start | bytes 393224 | tf_op jit(solution)/shard_map/ppermute | solution.py:246
  51.1 10.2 %collective-permute-start.14 = (bf16[64,1024]{1,0:T(8,128)(2,1)S(1)}, bf16[64,1024]{1,0:T(8,128)(2,1)S(1)}, u32[]{:S(2)}, u32[]{:S(2)}) collective-permute-start(bf16[64,1024]{1,0:T(8,128)(2,1)S(1)} %get-tuple-element.56), channel_id=1, source_target_pairs={{1,25},{3,27},{5,29},{7,31},{9,17},{11,19},{13,21},{15,23},{16,8},... | collective-permute-start | bytes 393224 | tf_op jit(solution)/shard_map/ppermute | solution.py:246
  62.6 7.1 %collective-permute-start.17 = (bf16[256,2048]{1,0:T(8,128)(2,1)S(1)}, bf16[256,2048]{1,0:T(8,128)(2,1)S(1)}, u32[]{:S(2)}, u32[]{:S(2)}) collective-permute-start(bf16[256,2048]{1,0:T(8,128)(2,1)S(1)} %get-tuple-element.70.refs_0_), channel_id=1, source_target_pairs={{0,1},{1,0},{2,3},{3,2},{4,5},{5,4},{6,7},{7,6},{8,9},{9,8},{10,11... | collective-permute-start | bytes 3145736 | tf_op jit(solution)/shard_map/ppermute | solution.py:250
  64.3 4.1 %collective-permute-start.19 = (bf16[3,256,256]{2,1,0:T(8,128)(2,1)S(1)}, bf16[3,256,256]{2,1,0:T(8,128)(2,1)S(1)}, u32[]{:S(2)}, u32[]{:S(2)}) collective-permute-start(bf16[3,256,256]{2,1,0:T(8,128)(2,1)S(1)} %get-tuple-element.71.refs_0_.refs_4_), channel_id=1, source_target_pairs={{0,1},{1,0},{2,3},{3,2},{4,5},{5,4},{6,7},{7,6},{8,9},{9,8},{10,11... | collective-permute-start | bytes 1179656 | tf_op jit(solution)/shard_map/ppermute | solution.py:250
  64.9 3.5 %collective-permute-start.18 = (bf16[3,256,256]{2,1,0:T(8,128)(2,1)S(1)}, bf16[3,256,256]{2,1,0:T(8,128)(2,1)S(1)}, u32[]{:S(2)}, u32[]{:S(2)}) collective-permute-start(bf16[3,256,256]{2,1,0:T(8,128)(2,1)S(1)} %get-tuple-element.68.refs_0_), channel_id=1, source_target_pairs={{0,1},{1,0},{2,3},{3,2},{4,5},{5,4},{6,7},{7,6},{8,9},{9,8},{10,11... | collective-permute-start | bytes 1179656 | tf_op jit(solution)/shard_map/ppermute | solution.py:250
  64.9 2.2 %collective-permute-start.21 = (f32[64,1024]{1,0:T(8,128)S(1)}, f32[64,1024]{1,0:T(8,128)S(1)}, u32[]{:S(2)}, u32[]{:S(2)}) collective-permute-start(f32[64,1024]{1,0:T(8,128)S(1)} %share.3.refs_0_.refs_2_), channel_id=1, source_target_pairs={{0,1},{1,0},{2,3},{3,2},{4,5},{5,4},{6,7},{7,6},{8,9},{9,8},{10,11... | collective-permute-start | bytes 786440 | tf_op jit(solution)/shard_map/ppermute | solution.py:250
  65.4 2.2 %collective-permute-start.20 = (f32[64,1024]{1,0:T(8,128)S(1)}, f32[64,1024]{1,0:T(8,128)S(1)}, u32[]{:S(2)}, u32[]{:S(2)}) collective-permute-start(f32[64,1024]{1,0:T(8,128)S(1)} %share.2.refs_0_), channel_id=1, source_target_pairs={{0,1},{1,0},{2,3},{3,2},{4,5},{5,4},{6,7},{7,6},{8,9},{9,8},{10,11... | collective-permute-start | bytes 786440 | tf_op jit(solution)/shard_map/ppermute | solution.py:250

commit v3 on v2

--- a/solution.py
+++ b/solution.py
@@ -332,38 +332,33 @@
 
 
 def pack_kernel(*refs):
-    inputs, out, sems = refs[:3], refs[-2], refs[-1]
+    inputs, out, own, sems = refs[:3], refs[-3], refs[-2], refs[-1]
     mine = out.shape[2]
-    there = pl.ds(pl.multiple_of((1 - place()[0]) * mine, mine), mine)
-    copies = [pltpu.make_async_copy(a.at[:, there], out.at[i], sems.at[i]) for i, a in enumerate(inputs)]
-    for copy in copies:
-        copy.start()
+    copies = []
+    for target, core in ((out, 1 - place()[0]), (own, place()[0])):
+        there = pl.ds(pl.multiple_of(core * mine, mine), mine)
+        for i, a in enumerate(inputs):
+            copies.append(pltpu.make_async_copy(a.at[:, there], target.at[i], sems.at[len(copies)]))
+            copies[-1].start()
     for copy in copies:
         copy.wait()
 
 
-def forward_kernel(pattern, near, far, received, *refs):
-    inputs = refs[:3]
-    rot_q, rot_k, rot_kt, values, attn, attn_t, lse, bias, cos_ref, sin_ref, q, k, v, sems = refs[-14:]
-    rows, mine = inputs[0].shape[0], rot_q.shape[0]
-    tokens = 2 * rows
-    step = 2 * BLK
-    core = place()[0]
-    here = pl.ds(pl.multiple_of(core * mine, mine), mine)
-    copies = []
-    for i, (ref, target) in enumerate(zip(inputs, (q, k, v))):
-        copies.append(pltpu.make_async_copy(ref.at[:, here], target, sems.at[i]))
-        copies[-1].start()
+def forward_kernel(pattern, near, far, own, received, *refs):
+    rot_q, rot_k, rot_kt, values, attn, attn_t, lse, bias, cos_ref, sin_ref = refs[-10:]
+    tokens = 2 * own.shape[1]
+    step = BLK
+    core, z, _, _ = place()
     block_bias(pattern, core, bias)
     cos, sin = rope_table(jnp.concatenate([near[...], far[...]], axis=1))
     cos_ref[...] = cos
     sin_ref[...] = sin
-    for copy in copies:
-        copy.wait()
-    for head in range(mine // HD):
+    for head in range(rot_q.shape[0] // HD):
         cols = slice(head * HD, (head + 1) * HD)
+        taken = (head // 2 ^ z % 2) * 2 + head % 2
+        taken = pl.ds(pl.multiple_of(taken * HD, HD), HD)
         query, key, value = (
-            jnp.concatenate([a[:, cols], received[i, :, cols]], axis=0) for i, a in enumerate((q, k, v))
+            jnp.concatenate([own[i, :, taken], received[i, :, taken]], axis=0) for i in range(3)
         )
         rot_q[cols, :] = rotate_rows(query.T.astype(jnp.float32), cos, sin)
         keys_t = rotate_rows(key.T.astype(jnp.float32), cos, sin)
@@ -387,14 +382,14 @@
 
 def weight_grad_kernel(attn_t, own, other, *refs, chunk):
     send, keep = refs[-2:]
-    core, z, y, x = place()
+    core, _, y, x = place()
     piece, width = send.shape[2:]
     cols = slice(chunk * width, (chunk + 1) * width)
     tokens = jnp.concatenate([own[:, cols], other[:, cols]], axis=0)
     for block in range(attn_t.shape[0] // (2 * piece)):
         rows = slice(block * 2 * piece, (block + 1) * 2 * piece)
         part = dot_nn(attn_t[rows, :], tokens).astype(send.dtype)
-        z_rel = (block // 2) ^ (z & 1)
+        z_rel = block // 2
         for head_x in range(2):
             out = part[head_x * piece : (head_x + 1) * piece, :]
             first = jnp.where(core == 0, head_x ^ x, (block % 2) ^ y)
@@ -409,49 +404,44 @@
                 keep[sub, z_rel] = out
 
 
-def attn_grad_kernel(attn_t, own, other, *refs):
+def attn_grad_kernel(attn_t, own, other, near, far, *refs, pair):
     grad_t, dots, weight = refs[-3:]
-    core, z, y, x = place()
-    piece = refs[0].shape[1]
-    for chunk in range(2):
-        for e3 in range(2):
-            ref = refs[chunk * 2 + e3]
-            for e2 in range(2):
-                y_at = jnp.where(core == 0, y ^ e2, y ^ e3)
-                x_at = jnp.where(core == 0, x ^ e3, x ^ e2)
-                start = (((z % 2 ^ chunk) * 2 + y_at) * 2 + x_at) * piece
-                weight[pl.ds(pl.multiple_of(start, piece), piece), :] = ref[e2]
-    half = own.shape[0]
-    mine = weight.shape[0]
-    for t, ref in enumerate((own, other)):
-        cols = slice(t * half, (t + 1) * half)
-        rounded = dot_nt(weight[...], ref[...]).astype(grad_t.dtype)
-        grad_t[:, cols] = rounded
-        product = rounded.astype(jnp.float32) * attn_t[:, cols].astype(jnp.float32)
-        for head in range(mine // HD):
-            dots[head : head + 1, cols] = jnp.sum(
-                product[head * HD : (head + 1) * HD], axis=0, keepdims=True
-            )
-
-
-def projection_kernel(attn, weight, *refs):
+    core, _, y, x = place()
+    piece = near.shape[1]
+    for e3, ref in enumerate((near, far)):
+        for e2 in range(2):
+            y_at = jnp.where(core == 0, y ^ e2, y ^ e3)
+            x_at = jnp.where(core == 0, x ^ e3, x ^ e2)
+            start = (y_at * 2 + x_at) * piece
+            weight[pl.ds(pl.multiple_of(start, piece), piece), :] = ref[e2]
+    size = weight.shape[0]
+    tokens = jnp.concatenate([own[...], other[...]], axis=0)
+    rounded = dot_nt(weight[...], tokens).astype(grad_t.dtype)
+    grad_t[...] = rounded
+    product = rounded.astype(jnp.float32) * attn_t[pair * size : (pair + 1) * size, :].astype(jnp.float32)
+    for head in range(size // HD):
+        dots[head : head + 1, :] = jnp.sum(product[head * HD : (head + 1) * HD], axis=0, keepdims=True)
+
+
+def projection_kernel(attn, low, high, *refs):
     out_send, out_own = refs[-2:]
     half = out_own.shape[0]
-    for c in range(weight.shape[1] // half):
+    for c in range(low.shape[1] // half):
         cols = slice(c * half, (c + 1) * half)
-        part = dot_nn(attn[...], weight[:, cols])
+        part = dot_nn(attn[...], jnp.concatenate([low[:, cols], high[:, cols]], axis=0))
         out_send[:, cols] = part[half:].astype(out_send.dtype)
         out_own[:, cols] = part[:half]
 
 
-def backward_kernel(rot_q, rot_k, rot_kt, values, grad_t, dots, lse, bias, cos_ref, sin_ref, *refs, heads):
+def backward_kernel(rot_q, rot_k, rot_kt, values, grad_t, dots, lse, bias, cos_ref, sin_ref, *refs, pair):
     send, own = refs[-2:]
     tokens = rot_k.shape[0]
     half = tokens // 2
     step = 2 * BLK
     scale = 1.0 / math.sqrt(HD)
     cos, sin = cos_ref[...], -sin_ref[...]
-    for at_head, head in enumerate(heads):
+    for at_head in range(2):
+        head = pair * 2 + at_head
         cols = slice(head * HD, (head + 1) * HD)
         out_cols = slice(at_head * HD, (at_head + 1) * HD)
         keys, keys_t, value = rot_k[:, cols], rot_kt[cols, :], values[:, cols]
@@ -460,11 +450,11 @@
         query_parts = []
         for part in range(tokens // step):
             at = slice(part * step, (part + 1) * step)
-            queries_t, grads_t = rot_q[cols, at], grad_t[cols, at]
+            queries_t, grads_t = rot_q[cols, at], grad_t[out_cols, at]
             scores = scaled_scores(keys, queries_t, bias[:, at])
             exact = jnp.exp2(scores - lse[head : head + 1, at])
             prob_grad = dot_nn(value, grads_t)
-            score_grad = (exact * (prob_grad - dots[head : head + 1, at])).astype(jnp.bfloat16)
+            score_grad = (exact * (prob_grad - dots[at_head : at_head + 1, at])).astype(jnp.bfloat16)
             value_sum = value_sum + dot_nt(grads_t, exact.astype(jnp.bfloat16))
             key_sum = key_sum + dot_nt(queries_t, score_grad)
             query_parts.append(dot_nn(keys_t, score_grad))
@@ -522,28 +512,23 @@
     refs[-1][...] = jnp.where(at_home, total, first[...].astype(jnp.float32))
 
 
-def mean_kernel(*refs, count):
-    out = refs[-1]
-    width = refs[0].shape[1]
-    for i in range(out.shape[1] // width):
-        out[:, i * width : (i + 1) * width] = (refs[2 * i][...] + refs[2 * i + 1][...]) * (1.0 / count)
-
-
-def layer_out_kernel(own, got, *refs):
-    out = refs[-1]
-    out[...] = (own[...] + got[...].astype(jnp.float32)).astype(out.dtype)
-
-
-def grads_kernel(*refs):
-    outs, parts = refs[-3:], refs[:-3]
-    mine = outs[0].shape[1] // 2
-    width = parts[0].shape[2]
-    for p in range(mine // width):
+def finish_kernel(*refs, count):
+    layer_out, *grads, mean = refs[-5:]
+    out_own, out_got = refs[:2]
+    pairs, shares = refs[2:6], refs[6:-5]
+    core, z, _, _ = place()
+    mine = grads[0].shape[1] // 2
+    width = mine // 2
+    for pair in range(2):
         for source in range(2):
-            start = (place()[0] ^ source) * mine + p * width
-            cols = pl.ds(pl.multiple_of(start, HD), width)
+            start = (core ^ source) * mine + (z % 2 ^ pair) * width
+            cols = pl.ds(pl.multiple_of(start, width), width)
             for i in range(3):
-                outs[i][:, cols] = parts[2 * p + source][i]
+                grads[i][:, cols] = pairs[2 * pair + source][i]
+    layer_out[...] = (out_own[...] + out_got[...].astype(jnp.float32)).astype(layer_out.dtype)
+    width = shares[0].shape[1]
+    for i in range(mean.shape[1] // width):
+        mean[:, i * width : (i + 1) * width] = (shares[2 * i][...] + shares[2 * i + 1][...]) * (1.0 / count)
 
 
 def chip_shards(queries, key_states, value_states, token_order, block_pattern, out_weight, out_grad):
@@ -567,7 +552,7 @@
             out_shape=[jax.ShapeDtypeStruct(s, d) for s, d in outs],
             scratch_shapes=scratch,
             compiler_params=pltpu.CompilerParams(vmem_limit_bytes=limit << 20),
-            cost_estimate=pl.CostEstimate(flops=1, bytes_accessed=1, transcendentals=0),
+            cost_estimate=pl.CostEstimate(flops=10000000000, bytes_accessed=1, transcendentals=0),
             name=name,
         )(*args, *before)
         if not final:
@@ -576,13 +561,13 @@
 
     q_own, k_own, v_own, dy_own = queries[0], key_states[0], value_states[0], out_grad[0]
     q_in, k_in, v_in = (pltpu.with_memory_space_constraint(a, pltpu.HBM) for a in (q_own, k_own, v_own))
-    (pack,) = call(
+    pack, own = call(
         pack_kernel,
         "pack",
         (q_in, k_in, v_in),
-        [((3, rows, mine), bf16)],
+        [((3, rows, mine), bf16)] * 2,
         specs=[in_hbm] * 3,
-        scratch=[pltpu.SemaphoreType.DMA((3,))],
+        scratch=[pltpu.SemaphoreType.DMA((6,))],
         final=True,
     )
     received = swap_core(pack)
@@ -596,20 +581,18 @@
     rot_q, rot_k, rot_kt, values, attn, attn_t, lse, bias, cos, sin = call(
         forward_kernel,
         "forward",
-        (block_pattern, token_order, order_far, received, q_in, k_in, v_in),
+        (block_pattern, token_order, order_far, own, received),
         [((mine, tokens), bf16), ((tokens, mine), bf16), ((mine, tokens), bf16)]
         + [((tokens, mine), bf16)] * 2
         + [((mine, tokens), bf16), ((mine // HD, tokens), f32), ((tokens // BLK, tokens), f32)]
         + [((HD // 4, tokens), f32)] * 2,
-        scratch=[pltpu.VMEM((rows, mine), bf16)] * 3 + [pltpu.SemaphoreType.DMA((3,))],
         limit=24,
-        specs=[in_smem] + [in_vmem] * 3 + [in_hbm] * 3,
+        specs=[in_smem] + [in_vmem] * 4,
     )
     sums = SUM_CHUNKS
     cols = model // sums
-    near, joined, far = [None] * chunks, [None] * chunks, [None] * chunks
-    weights = [None] * (2 * chunks)
-    parts, z_sums, pairs, shares = [None] * sums, [None] * sums, [], []
+    near, joined, weights, attn_grads, pairs = ([None] * chunks for _ in range(5))
+    parts, z_sums, shares = [None] * sums, [None] * sums, [None] * sums
     result = {}
 
     def weight_grad(i):
@@ -628,7 +611,7 @@
 
     def gather_far_step(i):
         (pair,) = call(pair_kernel, "pair", (near[i], joined[i]), [((2, owned, model), bf16)])
-        weights[2 * i], weights[2 * i + 1] = pair, move(pair, gather_far)
+        weights[i] = pair, move(pair, gather_far)
 
     def second_sum(i):
         send, kept = call(
@@ -650,46 +633,46 @@
 
     def share(i):
         (part,) = call(share_kernel, "share", z_sums[i], [((owned, cols), f32)])
-        shares.extend([part, swap_core(part)])
-
-    def attn_grad():
-        result["grad"] = call(
-            attn_grad_kernel,
+        shares[i] = part, swap_core(part)
+
+    def attn_grad(i):
+        attn_grads[i] = call(
+            functools.partial(attn_grad_kernel, pair=i),
             "attn_grad",
-            (attn_t, dy_own, dy_far, *weights),
-            [((mine, tokens), bf16), ((mine // HD, tokens), f32), ((mine, model), bf16)],
-            limit=24,
+            (attn_t, dy_own, dy_far, *weights[i]),
+            [((2 * HD, tokens), bf16), ((2, tokens), f32), ((2 * HD, model), bf16)],
+            limit=16,
         )
 
     def projection():
         out_send, out_own = call(
             projection_kernel,
             "projection",
-            (attn, result["grad"][2]),
+            (attn, attn_grads[0][2], attn_grads[1][2]),
             [((rows, model), bf16), ((rows, model), f32)],
             limit=16,
         )
         result["out"] = (out_own, swap_core(out_send))
 
-    def backward(heads):
+    def backward(i):
         send, own = call(
-            functools.partial(backward_kernel, heads=heads),
+            functools.partial(backward_kernel, pair=i),
             "backward",
-            (rot_q, rot_k, rot_kt, values, *result["grad"][:2], lse, bias, cos, sin),
-            [((3, rows, len(heads) * HD), bf16)] * 2,
+            (rot_q, rot_k, rot_kt, values, *attn_grads[i][:2], lse, bias, cos, sin),
+            [((3, rows, 2 * HD), bf16)] * 2,
             limit=24,
         )
-        pairs.extend([own, swap_core(send)])
-
-    def layer_out():
-        (result["layer_out"],) = call(layer_out_kernel, "layer_out", result["out"], [((rows, model), bf16)], final=True)
-
-    def grads():
-        result["grads"] = call(grads_kernel, "grads", pairs, [((rows, width), bf16)] * 3, final=True)
-
-    def mean():
-        (result["weight_grad"],) = call(
-            functools.partial(mean_kernel, count=lax.axis_size("dp")), "mean", shares, [((owned, model), f32)], final=True
+        pairs[i] = own, swap_core(send)
+
+    def finish():
+        args = (*result["out"], *pairs[0], *pairs[1], *(a for s in shares for a in s))
+        result["all"] = call(
+            functools.partial(finish_kernel, count=lax.axis_size("dp")),
+            "finish",
+            args,
+            [((rows, model), bf16)] + [((rows, width), bf16)] * 3 + [((owned, model), f32)],
+            limit=24,
+            final=True,
         )
 
     weight_grad(0)
@@ -702,16 +685,16 @@
     second_sum(1)
     z_sum(0)
     z_sum(1)
-    attn_grad()
+    attn_grad(0)
+    backward(0)
     share(0)
-    backward((0,1))
+    attn_grad(1)
+    backward(1)
+    projection()
     share(1)
-    projection()
-    backward((2,3))
-    grads()
-    mean()
-    layer_out()
-    return (result["layer_out"][None], *[g[None] for g in result["grads"]], result["weight_grad"])
+    finish()
+    *sharded, weight_grad = result["all"]
+    return (*[a[None] for a in sharded], weight_grad)
 
 
 def solution(mesh):

time: 71.1 us -> 62.4 us (0.88)
  waiting for transfers between devices: 27.9 us -> 24.8 us
  Pallas kernels: 19.1 us -> 16.1 us
  starting transfers between devices: 23 us -> 20.3 us
    pallas_call x21 -> x20, Pallas kernels: 19.1 us -> 16.1 us  [call(): pl.pallas_call(kernel, in_specs=list(specs or [in_vmem] * len(args)) + [a...]
    ppermute x14, starting transfers between devices: 21.2 us -> 18.5 us  [move(): return lax.ppermute(array, ('dp', 'ctx'), chip_moves(rule))]
    ppermute x8, waiting for transfers between devices: 3.22 us -> 1.52 us  [swap_core(): return lax.ppermute(array, 'ctx', [(0, 1), (1, 0)])]
    ppermute x14, waiting for transfers between devices: 24.6 us -> 23.3 us  [move(): return lax.ppermute(array, ('dp', 'ctx'), chip_moves(rule))]
  transfers between devices with their start and end apart: 22 -> 22, of which waited for: 11 -> 8; matrix products, arithmetic and copies ran while one was open for 0% -> 0% of each run, Pallas kernels for 23% -> 20%
where the time goes in v3:
time: 62.4 us; the launch traced here: 62.2 us
  waiting for transfers between devices  24.8 us (40%)
  starting transfers between devices  20.3 us (33%)
  Pallas kernels  16.1 us (26%)
  between operations  0.92 us (1%)
    ppermute x14, waiting for transfers between devices, move(): return lax.ppermute(array, ('dp', 'ctx'), chip_moves(rule))  23.3 us
    ppermute x14, starting transfers between devices, move(): return lax.ppermute(array, ('dp', 'ctx'), chip_moves(rule))  18.5 us
    pallas_call x20, Pallas kernels, call(): pl.pallas_call(kernel, in_specs=list(specs or [in_vmem] * len(args)) + [a...  16.1 us
    ppermute x8, starting transfers between devices, swap_core(): return lax.ppermute(array, 'ctx', [(0, 1), (1, 0)])  1.82 us
    ppermute x8, waiting for transfers between devices, swap_core(): return lax.ppermute(array, 'ctx', [(0, 1), (1, 0)])  1.52 us
  transfers between devices with their start and end apart: 22, of which 8 were waited for; matrix products, arithmetic and copies ran while one was open for 0% of the time, Pallas kernels for 20%

profile of v3, /device:TPU:0, one launch (start us, length us, event | category | flops | bytes accessed | tf_op | source)
XLA Modules:
  0.0 62.2 jit_solution(6734433606214413344)
XLA Ops:
  0.6 0.0 copy-start
  0.6 0.0 copy-start.3
  0.7 0.0 copy-start.1
  0.7 0.0 copy-start.2
  0.7 1.5 %pack.1 = (bf16[3,256,512]{2,1,0:T(8,128)(2,1)S(1)}, bf16[3,256,512]{2,1,0:T(8,128)(2,1)S(1)}) custom-call(bf16[256,1024]{1,0:T(8,128)(2,1)} %bitcast.13, bf16[256,1024]{1,0:T(8,128)(2,1)} %bitcast.14, bf16[256,1024]{1,0:T(8,128)(2,1)} %bitcast.15), custom_call_target="tpu_custom_call" | custom-call | flops 10000000000 | bytes 1 | tf_op jit(solution)/shard_map/pack/pallas_call | solution.py:548
  2.2 0.5 collective-permute-start.1
  2.7 0.1 collective-permute-start.2
  2.8 0.4 collective-permute-start
  3.2 3.7 %collective-permute-start.3 = (bf16[64,2048]{1,0:T(8,128)(2,1)S(1)}, bf16[64,2048]{1,0:T(8,128)(2,1)S(1)}, u32[]{:S(2)}, u32[]{:S(2)}) collective-permute-start(bf16[64,2048]{1,0:T(8,128)(2,1)S(1)} %copy-done.1), channel_id=1, source_target_pairs={{0,16},{1,8},{2,18},{3,10},{4,20},{5,12},{6,22},{7,14},{8,24},{9,0... | collective-permute-start | bytes 786440 | tf_op jit(solution)/shard_map/ppermute | solution.py:246
  6.9 3.4 %collective-permute-start.5 = (bf16[64,2048]{1,0:T(8,128)(2,1)S(1)}, bf16[64,2048]{1,0:T(8,128)(2,1)S(1)}, u32[]{:S(2)}, u32[]{:S(2)}) collective-permute-start(bf16[64,2048]{1,0:T(8,128)(2,1)S(1)} %copy-done.1), channel_id=1, source_target_pairs={{0,24},{2,26},{4,28},{6,30},{8,16},{10,18},{12,20},{14,22},{17,9},... | collective-permute-start | bytes 786440 | tf_op jit(solution)/shard_map/ppermute | solution.py:246
  10.3 0.0 collective-permute-done.far
  10.3 0.0 collective-permute-done.1.received
  10.3 3.1 %forward.1 = (bf16[512,512]{1,0:T(8,128)(2,1)S(1)}, bf16[512,512]{1,0:T(8,128)(2,1)S(1)}, bf16[512,512]{1,0:T(8,128)(2,1)S(1)}, bf16[512,512]{1,0:T(8,128)(2,1)S...) custom-call(s32[1,4,4]{2,1,0:T(4,128)S(1)} %copy-done.2, ...), custom_call_target="tpu_custom_call" | custom-call | flops 10000000000 | bytes 1 | tf_op jit(solution)/shard_map/forward/pallas_call | solution.py:548
  13.4 0.0 collective-permute-done.2.other
  13.4 1.3 %weight_grad.2 = (bf16[2,2,64,1024]{3,2,1,0:T(8,128)(2,1)S(1)}, bf16[2,2,64,1024]{3,2,1,0:T(8,128)(2,1)S(1)}) custom-call(bf16[512,512]{1,0:T(8,128)(2,1)S(1)} %get-tuple-element.51.attn_t, bf16[256,2048]{1,0:T(8,128)(2,1)S(1)} %bitcast.9, bf16[256,2048]{1,0:T(8,128)(2,1)S(1)} %collective-permute-done.2.other, ...), custom_call_target="tpu_custom_call" | custom-call | flops 10000000000 | bytes 1 | tf_op jit(solution)/shard_map/weight_grad/pallas_call | solution.py:548
  14.8 1.6 %collective-permute-start.9 = (bf16[2,2,64,1024]{3,2,1,0:T(8,128)(2,1)S(1)}, bf16[2,2,64,1024]{3,2,1,0:T(8,128)(2,1)S(1)}, u32[]{:S(2)}, u32[]{:S(2)}) collective-permute-start(bf16[2,2,64,1024]{3,2,1,0:T(8,128)(2,1)S(1)} %get-tuple-element.53.refs_0_), channel_id=1, source_target_pairs={{0,2},{1,5},{2,0},{3,7},{4,6},{5,1},{6,4},{7,3},{8,10},{9,13},{10,... | collective-permute-start | bytes 1572872 | tf_op jit(solution)/shard_map/ppermute | solution.py:246
  16.3 0.0 collective-permute-done.3.away.home
  16.4 1.6 %collective-permute-start.4 = (bf16[64,2048]{1,0:T(8,128)(2,1)S(1)}, bf16[64,2048]{1,0:T(8,128)(2,1)S(1)}, u32[]{:S(2)}, u32[]{:S(2)}) collective-permute-start(bf16[64,2048]{1,0:T(8,128)(2,1)S(1)} %gather_pick.2.refs_0_.a), channel_id=1, source_target_pairs={{0,4},{1,3},{2,6},{3,1},{4,0},{5,7},{6,2},{7,5},{8,12},{9,11},{10,... | collective-permute-start | bytes 786440 | tf_op jit(solution)/shard_map/ppermute | solution.py:246
  18.0 1.3 %weight_grad.3 = (bf16[2,2,64,1024]{3,2,1,0:T(8,128)(2,1)S(1)}, bf16[2,2,64,1024]{3,2,1,0:T(8,128)(2,1)S(1)}) custom-call(bf16[512,512]{1,0:T(8,128)(2,1)S(1)} %get-tuple-element.51.attn_t, bf16[256,2048]{1,0:T(8,128)(2,1)S(1)} %bitcast.10, bf16[256,2048]{1,0:T(8,128)(2,1)S(1)} %collective-permute-done.2.other, bf16[64,2048]{1,0:T(8,128)(2,1)S(1)} %gather_pick.2.refs_0_.a), custom_call_target="tpu_custom_call" | custom-call | flops 10000000000 | bytes 1 | tf_op jit(solution)/shard_map/weight_grad/pallas_call | solution.py:548
  19.3 0.6 collective-permute-start.7
  19.9 0.0 collective-permute-done.5.away
  19.9 0.6 collective-permute-start.8
  20.5 5.2 %collective-permute-done.4.b = bf16[64,2048]{1,0:T(8,128)(2,1)S(1)} collective-permute-done((bf16[64,2048]{1,0:T(8,128)(2,1)S(1)}, bf16[64,2048]{1,0:T(8,128)(2,1)S(1)}, u32[]{:S(2)}, u32[]{:S(2)}) %collective-permute-start.4) | collective-permute-done | bytes 262176 | tf_op jit(solution)/shard_map/ppermute | solution.py:246
  25.7 0.6 collective-permute-start.6
  26.3 2.4 %collective-permute-done.9.got = bf16[2,2,64,1024]{3,2,1,0:T(8,128)(2,1)S(1)} collective-permute-done((bf16[2,2,64,1024]{3,2,1,0:T(8,128)(2,1)S(1)}, bf16[2,2,64,1024]{3,2,1,0:T(8,128)(2,1)S(1)}, u32[]{:S(2)}, u32[]{:S(2)}) %collective-permute-start.9) | collective-permute-done | bytes 524320 | tf_op jit(solution)/shard_map/ppermute | solution.py:246
  28.7 0.1 second_sum.2
  28.8 1.6 %collective-permute-start.11 = (bf16[2,64,1024]{2,1,0:T(8,128)(2,1)S(1)}, bf16[2,64,1024]{2,1,0:T(8,128)(2,1)S(1)}, u32[]{:S(2)}, u32[]{:S(2)}) collective-permute-start(bf16[2,64,1024]{2,1,0:T(8,128)(2,1)S(1)} %get-tuple-element.57.refs_0_), channel_id=1, source_target_pairs={{0,4},{1,3},{2,6},{3,1},{4,0},{5,7},{6,2},{7,5},{8,12},{9,11},{10,... | collective-permute-start | bytes 786440 | tf_op jit(solution)/shard_map/ppermute | solution.py:246
  30.4 0.9 %collective-permute-done.8.b = bf16[64,2048]{1,0:T(8,128)(2,1)S(1)} collective-permute-done((bf16[64,2048]{1,0:T(8,128)(2,1)S(1)}, bf16[64,2048]{1,0:T(8,128)(2,1)S(1)}, u32[]{:S(2)}, u32[]{:S(2)}) %collective-permute-start.8) | collective-permute-done | bytes 262176 | tf_op jit(solution)/shard_map/ppermute | solution.py:246
  31.3 0.7 %collective-permute-start.12 = (bf16[2,64,2048]{2,1,0:T(8,128)(2,1)S(1)}, bf16[2,64,2048]{2,1,0:T(8,128)(2,1)S(1)}, u32[]{:S(2)}, u32[]{:S(2)}) collective-permute-start(bf16[2,64,2048]{2,1,0:T(8,128)(2,1)S(1)} %pair.3.refs_0_.near), channel_id=1, source_target_pairs={{0,2},{1,5},{2,0},{3,7},{4,6},{5,1},{6,4},{7,3},{8,10},{9,13},{10,... | collective-permute-start | bytes 1572872 | tf_op jit(solution)/shard_map/ppermute | solution.py:246
  32.0 5.1 %collective-permute-done.7.got = bf16[2,2,64,1024]{3,2,1,0:T(8,128)(2,1)S(1)} collective-permute-done((bf16[2,2,64,1024]{3,2,1,0:T(8,128)(2,1)S(1)}, bf16[2,2,64,1024]{3,2,1,0:T(8,128)(2,1)S(1)}, u32[]{:S(2)}, u32[]{:S(2)}) %collective-permute-start.7) | collective-permute-done | bytes 524320 | tf_op jit(solution)/shard_map/ppermute | solution.py:246
  37.1 0.1 second_sum.3
  37.2 1.4 %collective-permute-start.10 = (bf16[2,64,1024]{2,1,0:T(8,128)(2,1)S(1)}, bf16[2,64,1024]{2,1,0:T(8,128)(2,1)S(1)}, u32[]{:S(2)}, u32[]{:S(2)}) collective-permute-start(bf16[2,64,1024]{2,1,0:T(8,128)(2,1)S(1)} %get-tuple-element.59.refs_0_), channel_id=1, source_target_pairs={{0,4},{1,3},{2,6},{3,1},{4,0},{5,7},{6,2},{7,5},{8,12},{9,11},{10,... | collective-permute-start | bytes 786440 | tf_op jit(solution)/shard_map/ppermute | solution.py:246
  38.6 0.0 collective-permute-done.11.got
  38.6 0.1 z_sum.2
  38.7 1.3 %collective-permute-start.14 = (bf16[64,1024]{1,0:T(8,128)(2,1)S(1)}, bf16[64,1024]{1,0:T(8,128)(2,1)S(1)}, u32[]{:S(2)}, u32[]{:S(2)}) collective-permute-start(bf16[64,1024]{1,0:T(8,128)(2,1)S(1)} %get-tuple-element.65), channel_id=1, source_target_pairs={{1,25},{3,27},{5,29},{7,31},{9,17},{11,19},{13,21},{15,23},{16,8},... | collective-permute-start | bytes 393224 | tf_op jit(solution)/shard_map/ppermute | solution.py:246
  40.0 0.1 collective-permute-start.13
  40.1 6.5 %collective-permute-done.10.got = bf16[2,64,1024]{2,1,0:T(8,128)(2,1)S(1)} collective-permute-done((bf16[2,64,1024]{2,1,0:T(8,128)(2,1)S(1)}, bf16[2,64,1024]{2,1,0:T(8,128)(2,1)S(1)}, u32[]{:S(2)}, u32[]{:S(2)}) %collective-permute-start.10) | collective-permute-done | bytes 262176 | tf_op jit(solution)/shard_map/ppermute | solution.py:246
  46.5 0.1 z_sum.3
  46.6 1.3 %collective-permute-start.20 = (bf16[64,1024]{1,0:T(8,128)(2,1)S(1)}, bf16[64,1024]{1,0:T(8,128)(2,1)S(1)}, u32[]{:S(2)}, u32[]{:S(2)}) collective-permute-start(bf16[64,1024]{1,0:T(8,128)(2,1)S(1)} %get-tuple-element.85), channel_id=1, source_target_pairs={{1,25},{3,27},{5,29},{7,31},{9,17},{11,19},{13,21},{15,23},{16,8},... | collective-permute-start | bytes 393224 | tf_op jit(solution)/shard_map/ppermute | solution.py:246
  47.9 0.0 collective-permute-done.6.far
  47.9 0.2 collective-permute-start.19
  48.2 0.8 %attn_grad.2 = (bf16[256,512]{1,0:T(8,128)(2,1)S(1)}, f32[2,512]{1,0:T(2,128)S(1)}, bf16[256,2048]{1,0:T(8,128)(2,1)S(1)}) custom-call(bf16[512,512]{1,0:T(8,128)(2,1)S(1)} %get-tuple-element.51.attn_t, bf16[256,2048]{1,0:T(8,128)(2,1)S(1)} %bitcast.11, bf16[256,2048]{1,0:T(8,128)(2,1)S(1)} %collective-permute-done.2.other, ...), custom_call_target="tpu_custom_call" | custom-call | flops 10000000000 | bytes 1 | tf_op jit(solution)/shard_map/attn_grad/pallas_call | solution.py:548
  49.0 1.6 %backward.2 = (bf16[3,256,256]{2,1,0:T(8,128)(2,1)S(1)}, bf16[3,256,256]{2,1,0:T(8,128)(2,1)S(1)}) custom-call(bf16[512,512]{1,0:T(8,128)(2,1)S(1)} %get-tuple-element.52.refs_0_.rot_q, bf16[512,512]{1,0:T(8,128)(2,1)S(1)} %get-tuple-element.66.rot_k, bf16[512,512]{1,0:T(8,128)(2,1)S(1)} %get-tuple-element.67.rot_kt, ...), custom_call_target="tpu_custom_call" | custom-call | flops 10000000000 | bytes 1 | tf_op jit(solution)/shard_map/backward/pallas_call | solution.py:548
  50.7 0.0 collective-permute-done.14.second
  50.7 0.1 collective-permute-start.16
  50.8 0.0 collective-permute-done.13.first
  50.8 0.1 share.2.refs_0_.refs_6_
  50.8 0.6 collective-permute-start.18
  51.4 0.0 collective-permute-done.12.far
  51.4 0.8 %attn_grad.3 = (bf16[256,512]{1,0:T(8,128)(2,1)S(1)}, f32[2,512]{1,0:T(2,128)S(1)}, bf16[256,2048]{1,0:T(8,128)(2,1)S(1)}) custom-call(bf16[512,512]{1,0:T(8,128)(2,1)S(1)} %get-tuple-element.51.attn_t, bf16[256,2048]{1,0:T(8,128)(2,1)S(1)} %bitcast.12, bf16[256,2048]{1,0:T(8,128)(2,1)S(1)} %collective-permute-done.2.other, ...), custom_call_target="tpu_custom_call" | custom-call | flops 10000000000 | bytes 1 | tf_op jit(solution)/shard_map/attn_grad/pallas_call | solution.py:548
  52.2 1.6 %backward.3 = (bf16[3,256,256]{2,1,0:T(8,128)(2,1)S(1)}, bf16[3,256,256]{2,1,0:T(8,128)(2,1)S(1)}) custom-call(bf16[512,512]{1,0:T(8,128)(2,1)S(1)} %get-tuple-element.52.refs_0_.rot_q, bf16[512,512]{1,0:T(8,128)(2,1)S(1)} %get-tuple-element.66.rot_k, bf16[512,512]{1,0:T(8,128)(2,1)S(1)} %get-tuple-element.67.rot_kt, ...), custom_call_target="tpu_custom_call" | custom-call | flops 10000000000 | bytes 1 | tf_op jit(solution)/shard_map/backward/pallas_call | solution.py:548
  53.9 0.1 collective-permute-start.17
  54.0 1.3 %projection.1 = (bf16[256,2048]{1,0:T(8,128)(2,1)S(1)}, f32[256,2048]{1,0:T(8,128)S(1)}) custom-call(bf16[512,512]{1,0:T(8,128)(2,1)S(1)} %get-tuple-element.50.attn, bf16[256,2048]{1,0:T(8,128)(2,1)S(1)} %get-tuple-element.63.low, bf16[256,2048]{1,0:T(8,128)(2,1)S(1)} %get-tuple-element.76.high, bf16[3,256,256]{2,1,0:T(8,128)(2,1)S(1)} %get-tuple-element.79.refs_0_), custom_call_target="tpu_custom_call" | custom-call | flops 10000000000 | bytes 1 | tf_op jit(solution)/shard_map/projection/pallas_call | solution.py:548
  55.2 1.4 %collective-permute-done.20.second = bf16[64,1024]{1,0:T(8,128)(2,1)S(1)} collective-permute-done((bf16[64,1024]{1,0:T(8,128)(2,1)S(1)}, bf16[64,1024]{1,0:T(8,128)(2,1)S(1)}, u32[]{:S(2)}, u32[]{:S(2)}) %collective-permute-start.20) | collective-permute-done | bytes 131104 | tf_op jit(solution)/shard_map/ppermute | solution.py:246
  56.6 0.0 collective-permute-start.15
  56.6 1.8 %collective-permute-done.19.first = bf16[64,1024]{1,0:T(8,128)(2,1)S(1)} collective-permute-done((bf16[64,1024]{1,0:T(8,128)(2,1)S(1)}, bf16[64,1024]{1,0:T(8,128)(2,1)S(1)}, u32[]{:S(2)}, u32[]{:S(2)}) %collective-permute-start.19) | collective-permute-done | bytes 131104 | tf_op jit(solution)/shard_map/ppermute | solution.py:246
  58.4 0.1 share.3.refs_8_
  58.5 0.1 collective-permute-start.21
  58.6 0.0 collective-permute-done.18.refs_7_
  58.6 0.0 collective-permute-done.16.refs_3_
  58.6 1.5 %collective-permute-done.21.refs_9_ = f32[64,1024]{1,0:T(8,128)S(1)} collective-permute-done((f32[64,1024]{1,0:T(8,128)S(1)}, f32[64,1024]{1,0:T(8,128)S(1)}, u32[]{:S(2)}, u32[]{:S(2)}) %collective-permute-start.21) | collective-permute-done | bytes 262176 | tf_op jit(solution)/shard_map/ppermute | solution.py:250
  60.1 0.0 collective-permute-done.17.refs_5_
  60.1 0.0 collective-permute-done.15.refs_1_
  60.1 2.1 %finish.1 = (bf16[256,2048]{1,0:T(8,128)(2,1)}, bf16[256,1024]{1,0:T(8,128)(2,1)}, bf16[256,1024]{1,0:T(8,128)(2,1)}, bf16[256,1024]{1,0:T(8,128)(2,1)}, f32[64,2048]{1,0:T(8,128)}) custom-call(f32[256,2048]{1,0:T(8,128)S(1)} %get-tuple-element.80.refs_0_, bf16[256,2048]{1,0:T(8,128)(2,1)S(1)} %collective-permute-done.15.refs_1_, ...), custom_call_target="tpu_custom_call" | custom-call | flops 10000000000 | bytes 1 | tf_op jit(solution)/shard_map/finish/pallas_call | solution.py:548
  (8 shorter events, 0.1 us)
Async XLA Ops:
  0.6 2.1 %copy-start = (bf16[1,256,2048]{2,1,0:T(8,128)(2,1)S(1)}, bf16[1,256,2048]{2,1,0:T(8,128)(2,1)}, u32[]{:S(2)}) copy-start(bf16[1,256,2048]{2,1,0:T(8,128)(2,1)} %param.13) | copy-start | bytes 3145732
  0.6 2.1 %copy-start.3 = (s32[1,256]{1,0:T(1,128)S(1)}, s32[1,256]{1,0:T(1,128)}, u32[]{:S(2)}) copy-start(s32[1,256]{1,0:T(1,128)} %near.1) | copy-start | bytes 3076
  0.7 2.6 %copy-start.1 = (bf16[64,2048]{1,0:T(8,128)(2,1)S(1)}, bf16[64,2048]{1,0:T(8,128)(2,1)}, u32[]{:S(2)}) copy-start(bf16[64,2048]{1,0:T(8,128)(2,1)} %home.1) | copy-start | bytes 786436
  0.7 9.7 %copy-start.2 = (s32[1,4,4]{2,1,0:T(4,128)S(1)}, s32[1,4,4]{2,1,0:T(4,128)}, u32[]{:S(2)}) copy-start(s32[1,4,4]{2,1,0:T(4,128)} %pattern.1) | copy-start | bytes 196
  2.2 8.1 %collective-permute-start.1 = (bf16[3,256,512]{2,1,0:T(8,128)(2,1)S(1)}, bf16[3,256,512]{2,1,0:T(8,128)(2,1)S(1)}, u32[]{:S(2)}, u32[]{:S(2)}) collective-permute-start(bf16[3,256,512]{2,1,0:T(8,128)(2,1)S(1)} %get-tuple-element.49), channel_id=1, source_target_pairs={{0,1},{1,0},{2,3},{3,2},{4,5},{5,4},{6,7},{7,6},{8,9},{9,8},{10,11... | collective-permute-start | bytes 2359304 | tf_op jit(solution)/shard_map/ppermute | solution.py:250
  2.7 10.7 %collective-permute-start.2 = (bf16[256,2048]{1,0:T(8,128)(2,1)S(1)}, bf16[256,2048]{1,0:T(8,128)(2,1)S(1)}, u32[]{:S(2)}, u32[]{:S(2)}) collective-permute-start(bf16[256,2048]{1,0:T(8,128)(2,1)S(1)} %bitcast.8), channel_id=1, source_target_pairs={{0,1},{1,0},{2,3},{3,2},{4,5},{5,4},{6,7},{7,6},{8,9},{9,8},{10,11... | collective-permute-start | bytes 3145736 | tf_op jit(solution)/shard_map/ppermute | solution.py:250
  2.8 7.5 %collective-permute-start = (s32[1,256]{1,0:T(1,128)S(1)}, s32[1,256]{1,0:T(1,128)S(1)}, u32[]{:S(2)}, u32[]{:S(2)}) collective-permute-start(s32[1,256]{1,0:T(1,128)S(1)} %copy-done.3), channel_id=1, source_target_pairs={{0,1},{1,0},{2,3},{3,2},{4,5},{5,4},{6,7},{7,6},{8,9},{9,8},{10,11... | collective-permute-start | bytes 3080 | tf_op jit(solution)/shard_map/ppermute | solution.py:250
  3.2 13.1 %collective-permute-start.3 = (bf16[64,2048]{1,0:T(8,128)(2,1)S(1)}, bf16[64,2048]{1,0:T(8,128)(2,1)S(1)}, u32[]{:S(2)}, u32[]{:S(2)}) collective-permute-start(bf16[64,2048]{1,0:T(8,128)(2,1)S(1)} %copy-done.1), channel_id=1, source_target_pairs={{0,16},{1,8},{2,18},{3,10},{4,20},{5,12},{6,22},{7,14},{8,24},{9,0... | collective-permute-start | bytes 786440 | tf_op jit(solution)/shard_map/ppermute | solution.py:246
  6.9 13.0 %collective-permute-start.5 = (bf16[64,2048]{1,0:T(8,128)(2,1)S(1)}, bf16[64,2048]{1,0:T(8,128)(2,1)S(1)}, u32[]{:S(2)}, u32[]{:S(2)}) collective-permute-start(bf16[64,2048]{1,0:T(8,128)(2,1)S(1)} %copy-done.1), channel_id=1, source_target_pairs={{0,24},{2,26},{4,28},{6,30},{8,16},{10,18},{12,20},{14,22},{17,9},... | collective-permute-start | bytes 786440 | tf_op jit(solution)/shard_map/ppermute | solution.py:246
  14.8 13.9 %collective-permute-start.9 = (bf16[2,2,64,1024]{3,2,1,0:T(8,128)(2,1)S(1)}, bf16[2,2,64,1024]{3,2,1,0:T(8,128)(2,1)S(1)}, u32[]{:S(2)}, u32[]{:S(2)}) collective-permute-start(bf16[2,2,64,1024]{3,2,1,0:T(8,128)(2,1)S(1)} %get-tuple-element.53.refs_0_), channel_id=1, source_target_pairs={{0,2},{1,5},{2,0},{3,7},{4,6},{5,1},{6,4},{7,3},{8,10},{9,13},{10,... | collective-permute-start | bytes 1572872 | tf_op jit(solution)/shard_map/ppermute | solution.py:246
  16.4 9.3 %collective-permute-start.4 = (bf16[64,2048]{1,0:T(8,128)(2,1)S(1)}, bf16[64,2048]{1,0:T(8,128)(2,1)S(1)}, u32[]{:S(2)}, u32[]{:S(2)}) collective-permute-start(bf16[64,2048]{1,0:T(8,128)(2,1)S(1)} %gather_pick.2.refs_0_.a), channel_id=1, source_target_pairs={{0,4},{1,3},{2,6},{3,1},{4,0},{5,7},{6,2},{7,5},{8,12},{9,11},{10,... | collective-permute-start | bytes 786440 | tf_op jit(solution)/shard_map/ppermute | solution.py:246
  19.3 17.8 %collective-permute-start.7 = (bf16[2,2,64,1024]{3,2,1,0:T(8,128)(2,1)S(1)}, bf16[2,2,64,1024]{3,2,1,0:T(8,128)(2,1)S(1)}, u32[]{:S(2)}, u32[]{:S(2)}) collective-permute-start(bf16[2,2,64,1024]{3,2,1,0:T(8,128)(2,1)S(1)} %get-tuple-element.54.refs_0_), channel_id=1, source_target_pairs={{0,2},{1,5},{2,0},{3,7},{4,6},{5,1},{6,4},{7,3},{8,10},{9,13},{10,... | collective-permute-start | bytes 1572872 | tf_op jit(solution)/shard_map/ppermute | solution.py:246
  19.9 11.4 %collective-permute-start.8 = (bf16[64,2048]{1,0:T(8,128)(2,1)S(1)}, bf16[64,2048]{1,0:T(8,128)(2,1)S(1)}, u32[]{:S(2)}, u32[]{:S(2)}) collective-permute-start(bf16[64,2048]{1,0:T(8,128)(2,1)S(1)} %gather_pick.3.refs_0_.a), channel_id=1, source_target_pairs={{0,4},{1,3},{2,6},{3,1},{4,0},{5,7},{6,2},{7,5},{8,12},{9,11},{10,... | collective-permute-start | bytes 786440 | tf_op jit(solution)/shard_map/ppermute | solution.py:246
  25.7 22.2 %collective-permute-start.6 = (bf16[2,64,2048]{2,1,0:T(8,128)(2,1)S(1)}, bf16[2,64,2048]{2,1,0:T(8,128)(2,1)S(1)}, u32[]{:S(2)}, u32[]{:S(2)}) collective-permute-start(bf16[2,64,2048]{2,1,0:T(8,128)(2,1)S(1)} %pair.2.refs_0_.near), channel_id=1, source_target_pairs={{0,2},{1,5},{2,0},{3,7},{4,6},{5,1},{6,4},{7,3},{8,10},{9,13},{10,... | collective-permute-start | bytes 1572872 | tf_op jit(solution)/shard_map/ppermute | solution.py:246
  28.8 9.8 %collective-permute-start.11 = (bf16[2,64,1024]{2,1,0:T(8,128)(2,1)S(1)}, bf16[2,64,1024]{2,1,0:T(8,128)(2,1)S(1)}, u32[]{:S(2)}, u32[]{:S(2)}) collective-permute-start(bf16[2,64,1024]{2,1,0:T(8,128)(2,1)S(1)} %get-tuple-element.57.refs_0_), channel_id=1, source_target_pairs={{0,4},{1,3},{2,6},{3,1},{4,0},{5,7},{6,2},{7,5},{8,12},{9,11},{10,... | collective-permute-start | bytes 786440 | tf_op jit(solution)/shard_map/ppermute | solution.py:246
  31.3 20.1 %collective-permute-start.12 = (bf16[2,64,2048]{2,1,0:T(8,128)(2,1)S(1)}, bf16[2,64,2048]{2,1,0:T(8,128)(2,1)S(1)}, u32[]{:S(2)}, u32[]{:S(2)}) collective-permute-start(bf16[2,64,2048]{2,1,0:T(8,128)(2,1)S(1)} %pair.3.refs_0_.near), channel_id=1, source_target_pairs={{0,2},{1,5},{2,0},{3,7},{4,6},{5,1},{6,4},{7,3},{8,10},{9,13},{10,... | collective-permute-start | bytes 1572872 | tf_op jit(solution)/shard_map/ppermute | solution.py:246
  37.2 9.3 %collective-permute-start.10 = (bf16[2,64,1024]{2,1,0:T(8,128)(2,1)S(1)}, bf16[2,64,1024]{2,1,0:T(8,128)(2,1)S(1)}, u32[]{:S(2)}, u32[]{:S(2)}) collective-permute-start(bf16[2,64,1024]{2,1,0:T(8,128)(2,1)S(1)} %get-tuple-element.59.refs_0_), channel_id=1, source_target_pairs={{0,4},{1,3},{2,6},{3,1},{4,0},{5,7},{6,2},{7,5},{8,12},{9,11},{10,... | collective-permute-start | bytes 786440 | tf_op jit(solution)/shard_map/ppermute | solution.py:246
  38.7 12.0 %collective-permute-start.14 = (bf16[64,1024]{1,0:T(8,128)(2,1)S(1)}, bf16[64,1024]{1,0:T(8,128)(2,1)S(1)}, u32[]{:S(2)}, u32[]{:S(2)}) collective-permute-start(bf16[64,1024]{1,0:T(8,128)(2,1)S(1)} %get-tuple-element.65), channel_id=1, source_target_pairs={{1,25},{3,27},{5,29},{7,31},{9,17},{11,19},{13,21},{15,23},{16,8},... | collective-permute-start | bytes 393224 | tf_op jit(solution)/shard_map/ppermute | solution.py:246
  40.0 10.8 %collective-permute-start.13 = (bf16[64,1024]{1,0:T(8,128)(2,1)S(1)}, bf16[64,1024]{1,0:T(8,128)(2,1)S(1)}, u32[]{:S(2)}, u32[]{:S(2)}) collective-permute-start(bf16[64,1024]{1,0:T(8,128)(2,1)S(1)} %get-tuple-element.61.refs_0_), channel_id=1, source_target_pairs={{0,9},{1,17},{2,11},{3,19},{4,13},{5,21},{6,15},{7,23},{8,1},{9,25... | collective-permute-start | bytes 393224 | tf_op jit(solution)/shard_map/ppermute | solution.py:246
  46.6 10.0 %collective-permute-start.20 = (bf16[64,1024]{1,0:T(8,128)(2,1)S(1)}, bf16[64,1024]{1,0:T(8,128)(2,1)S(1)}, u32[]{:S(2)}, u32[]{:S(2)}) collective-permute-start(bf16[64,1024]{1,0:T(8,128)(2,1)S(1)} %get-tuple-element.85), channel_id=1, source_target_pairs={{1,25},{3,27},{5,29},{7,31},{9,17},{11,19},{13,21},{15,23},{16,8},... | collective-permute-start | bytes 393224 | tf_op jit(solution)/shard_map/ppermute | solution.py:246
  47.9 10.5 %collective-permute-start.19 = (bf16[64,1024]{1,0:T(8,128)(2,1)S(1)}, bf16[64,1024]{1,0:T(8,128)(2,1)S(1)}, u32[]{:S(2)}, u32[]{:S(2)}) collective-permute-start(bf16[64,1024]{1,0:T(8,128)(2,1)S(1)} %get-tuple-element.62.refs_0_), channel_id=1, source_target_pairs={{0,9},{1,17},{2,11},{3,19},{4,13},{5,21},{6,15},{7,23},{8,1},{9,25... | collective-permute-start | bytes 393224 | tf_op jit(solution)/shard_map/ppermute | solution.py:246
  50.7 7.9 %collective-permute-start.16 = (bf16[3,256,256]{2,1,0:T(8,128)(2,1)S(1)}, bf16[3,256,256]{2,1,0:T(8,128)(2,1)S(1)}, u32[]{:S(2)}, u32[]{:S(2)}) collective-permute-start(bf16[3,256,256]{2,1,0:T(8,128)(2,1)S(1)} %get-tuple-element.75.refs_0_), channel_id=1, source_target_pairs={{0,1},{1,0},{2,3},{3,2},{4,5},{5,4},{6,7},{7,6},{8,9},{9,8},{10,11... | collective-permute-start | bytes 1179656 | tf_op jit(solution)/shard_map/ppermute | solution.py:250
  50.8 7.7 %collective-permute-start.18 = (f32[64,1024]{1,0:T(8,128)S(1)}, f32[64,1024]{1,0:T(8,128)S(1)}, u32[]{:S(2)}, u32[]{:S(2)}) collective-permute-start(f32[64,1024]{1,0:T(8,128)S(1)} %share.2.refs_0_.refs_6_), channel_id=1, source_target_pairs={{0,1},{1,0},{2,3},{3,2},{4,5},{5,4},{6,7},{7,6},{8,9},{9,8},{10,11... | collective-permute-start | bytes 786440 | tf_op jit(solution)/shard_map/ppermute | solution.py:250
  53.9 6.2 %collective-permute-start.17 = (bf16[3,256,256]{2,1,0:T(8,128)(2,1)S(1)}, bf16[3,256,256]{2,1,0:T(8,128)(2,1)S(1)}, u32[]{:S(2)}, u32[]{:S(2)}) collective-permute-start(bf16[3,256,256]{2,1,0:T(8,128)(2,1)S(1)} %get-tuple-element.79.refs_0_), channel_id=1, source_target_pairs={{0,1},{1,0},{2,3},{3,2},{4,5},{5,4},{6,7},{7,6},{8,9},{9,8},{10,11... | collective-permute-start | bytes 1179656 | tf_op jit(solution)/shard_map/ppermute | solution.py:250
  56.6 3.5 %collective-permute-start.15 = (bf16[256,2048]{1,0:T(8,128)(2,1)S(1)}, bf16[256,2048]{1,0:T(8,128)(2,1)S(1)}, u32[]{:S(2)}, u32[]{:S(2)}) collective-permute-start(bf16[256,2048]{1,0:T(8,128)(2,1)S(1)} %get-tuple-element.81.refs_0_), channel_id=1, source_target_pairs={{0,1},{1,0},{2,3},{3,2},{4,5},{5,4},{6,7},{7,6},{8,9},{9,8},{10,11... | collective-permute-start | bytes 3145736 | tf_op jit(solution)/shard_map/ppermute | solution.py:250
  58.5 1.6 %collective-permute-start.21 = (f32[64,1024]{1,0:T(8,128)S(1)}, f32[64,1024]{1,0:T(8,128)S(1)}, u32[]{:S(2)}, u32[]{:S(2)}) collective-permute-start(f32[64,1024]{1,0:T(8,128)S(1)} %share.3.refs_8_), channel_id=1, source_target_pairs={{0,1},{1,0},{2,3},{3,2},{4,5},{5,4},{6,7},{7,6},{8,9},{9,8},{10,11... | collective-permute-start | bytes 786440 | tf_op jit(solution)/shard_map/ppermute | solution.py:250

commit v4 on v3

--- a/solution.py
+++ b/solution.py
@@ -250,20 +250,24 @@
     return lax.ppermute(array, "ctx", [(0, 1), (1, 0)])
 
 
-def gather_first(z, y, x, core):
-    return (z ^ 2, y, x, core) if z // 2 == core else (z ^ 1, y, x, 1 - core)
-
-
-def gather_second(z, y, x, core):
-    return (z ^ 3, y, x, core) if z // 2 == core else None
-
-
-def gather_near(z, y, x, core):
+def at_home(rule):
+    return lambda z, y, x, core: rule(z, y, x, core) if z // 2 == core else (z, y, x, 1 - core)
+
+
+def near_z(z, y, x, core):
+    return (z ^ 1, y, x, core)
+
+
+def far_z(z, y, x, core):
+    return (z ^ 2, y, x, core)
+
+
+def own_axis(z, y, x, core):
+    return swap_x(z, y, x, core) if core == 0 else swap_y(z, y, x, core)
+
+
+def other_axis(z, y, x, core):
     return swap_y(z, y, x, core) if core == 0 else swap_x(z, y, x, core)
-
-
-def gather_far(z, y, x, core):
-    return swap_x(z, y, x, core) if core == 0 else swap_y(z, y, x, core)
 
 
 def scatter_first(z, y, x, core):
@@ -271,7 +275,15 @@
 
 
 def scatter_second(z, y, x, core):
-    return None if z // 2 == core else (z ^ 3, y, x, core)
+    return (z, y, x, 1 - core) if z // 2 == core else (z ^ 3, y, x, core)
+
+
+def scatter_first(z, y, x, core):
+    return (z ^ 1, y, x, 1 - core) if z // 2 == core else (z ^ 2, y, x, core)
+
+
+def scatter_second(z, y, x, core):
+    return (z, y, x, 1 - core) if z // 2 == core else (z ^ 3, y, x, core)
 
 
 def dot_nt(a, b):
@@ -332,25 +344,33 @@
 
 
 def pack_kernel(*refs):
-    inputs, out, own, sems = refs[:3], refs[-3], refs[-2], refs[-1]
-    mine = out.shape[2]
+    order, *inputs = refs[:4]
+    out, own, sems = refs[-3:]
+    rows, mine = own.shape[1:]
     copies = []
     for target, core in ((out, 1 - place()[0]), (own, place()[0])):
         there = pl.ds(pl.multiple_of(core * mine, mine), mine)
         for i, a in enumerate(inputs):
-            copies.append(pltpu.make_async_copy(a.at[:, there], target.at[i], sems.at[len(copies)]))
+            copies.append(
+                pltpu.make_async_copy(a.at[:, there], target.at[i, 0:rows, :], sems.at[len(copies)])
+            )
             copies[-1].start()
+    digits = jnp.concatenate([order[...] // 16, order[...] % 16] + [jnp.zeros_like(order)] * 14, axis=0)
+    out[0, rows:, 0:rows] = digits.astype(jnp.float32).astype(jnp.bfloat16)
     for copy in copies:
         copy.wait()
 
 
-def forward_kernel(pattern, near, far, own, received, *refs):
+def forward_kernel(pattern, near, own, received, *refs):
     rot_q, rot_k, rot_kt, values, attn, attn_t, lse, bias, cos_ref, sin_ref = refs[-10:]
     tokens = 2 * own.shape[1]
     step = BLK
     core, z, _, _ = place()
     block_bias(pattern, core, bias)
-    cos, sin = rope_table(jnp.concatenate([near[...], far[...]], axis=1))
+    rows = own.shape[1]
+    digits = received[0, rows:, 0:rows].astype(jnp.float32).astype(jnp.int32)
+    far = digits[0:1, :] * 16 + digits[1:2, :]
+    cos, sin = rope_table(jnp.concatenate([near[...], far], axis=1))
     cos_ref[...] = cos
     sin_ref[...] = sin
     for head in range(rot_q.shape[0] // HD):
@@ -358,7 +378,7 @@
         taken = (head // 2 ^ z % 2) * 2 + head % 2
         taken = pl.ds(pl.multiple_of(taken * HD, HD), HD)
         query, key, value = (
-            jnp.concatenate([own[i, :, taken], received[i, :, taken]], axis=0) for i in range(3)
+            jnp.concatenate([own[i, :, taken], received[i, 0:rows, taken]], axis=0) for i in range(3)
         )
         rot_q[cols, :] = rotate_rows(query.T.astype(jnp.float32), cos, sin)
         keys_t = rotate_rows(key.T.astype(jnp.float32), cos, sin)
@@ -470,22 +490,23 @@
             send[i, :, out_cols] = out[half:, :]
 
 
-def gather_pick_kernel(home, away, *refs):
+def gather_pick_kernel(home0, home1, away0, away1, *refs):
     core, z, _, _ = place()
-    near = refs[-1]
+    low = refs[-1]
 
     @pl.when(z // 2 == core)
     def _():
-        near[...] = home[...]
+        low[0] = home0[...]
+        low[1] = home1[...]
 
     @pl.when(z // 2 != core)
     def _():
-        near[...] = away[...]
-
-
-def pair_kernel(a, b, *refs):
-    refs[-1][0] = a[...]
-    refs[-1][1] = b[...]
+        low[0] = away0[...]
+        low[1] = away1[...]
+
+
+def copy_kernel(a, *refs):
+    refs[-1][...] = a[...]
 
 
 def second_sum_kernel(keep, got, *refs):
@@ -564,34 +585,36 @@
     pack, own = call(
         pack_kernel,
         "pack",
-        (q_in, k_in, v_in),
-        [((3, rows, mine), bf16)] * 2,
-        specs=[in_hbm] * 3,
+        (token_order, q_in, k_in, v_in),
+        [((3, rows + 16, mine), bf16), ((3, rows, mine), bf16)],
+        specs=[in_vmem] + [in_hbm] * 3,
         scratch=[pltpu.SemaphoreType.DMA((6,))],
         final=True,
     )
     received = swap_core(pack)
-    order_far = swap_core(token_order)
     dy_far = swap_core(dy_own)
 
-    first, second = move(out_weight, gather_first), move(out_weight, gather_second)
-    z_parts = ((out_weight, first), (first, second))
+    beyond = move(out_weight, at_home(far_z))
+    beside = move(out_weight, other_axis)
     chunks = 2
-
-    rot_q, rot_k, rot_kt, values, attn, attn_t, lse, bias, cos, sin = call(
-        forward_kernel,
-        "forward",
-        (block_pattern, token_order, order_far, own, received),
-        [((mine, tokens), bf16), ((tokens, mine), bf16), ((mine, tokens), bf16)]
-        + [((tokens, mine), bf16)] * 2
-        + [((mine, tokens), bf16), ((mine // HD, tokens), f32), ((tokens // BLK, tokens), f32)]
-        + [((HD // 4, tokens), f32)] * 2,
-        limit=24,
-        specs=[in_smem] + [in_vmem] * 4,
-    )
+    forward_results = []
+
+    def forward():
+        forward_results[:] = call(
+            forward_kernel,
+            "forward",
+            (block_pattern, token_order, own, received),
+            [((mine, tokens), bf16), ((tokens, mine), bf16), ((mine, tokens), bf16)]
+            + [((tokens, mine), bf16)] * 2
+            + [((mine, tokens), bf16), ((mine // HD, tokens), f32), ((tokens // BLK, tokens), f32)]
+            + [((HD // 4, tokens), f32)] * 2,
+            limit=24,
+            specs=[in_smem] + [in_vmem] * 3,
+        )
+
     sums = SUM_CHUNKS
     cols = model // sums
-    near, joined, weights, attn_grads, pairs = ([None] * chunks for _ in range(5))
+    weights, attn_grads, pairs = ([None] * chunks for _ in range(3))
     parts, z_sums, shares = [None] * sums, [None] * sums, [None] * sums
     result = {}
 
@@ -599,19 +622,25 @@
         send, keep = call(
             functools.partial(weight_grad_kernel, chunk=i),
             "weight_grad",
-            (attn_t, dy_own, dy_far),
+            (forward_results[5], dy_own, dy_far),
             [((2, 2, owned, cols), bf16)] * 2,
             limit=16,
         )
-        parts[i] = (keep, move(send, gather_far))
-
-    def gather_near_step(i):
-        (near[i],) = call(gather_pick_kernel, "gather_pick", z_parts[i], [((owned, model), bf16)])
-        joined[i] = move(near[i], gather_near)
-
-    def gather_far_step(i):
-        (pair,) = call(pair_kernel, "pair", (near[i], joined[i]), [((2, owned, model), bf16)])
-        weights[i] = pair, move(pair, gather_far)
+        parts[i] = (keep, move(send, own_axis))
+
+    def gather_beside():
+        (copied,) = call(copy_kernel, "copy", (beside,), [((owned, model), bf16)])
+        result["beside"] = move(copied, at_home(far_z))
+
+    def gather_pick():
+        args = (out_weight, beside, beyond, result["beside"])
+        (low,) = call(gather_pick_kernel, "gather_pick", args, [((2, owned, model), bf16)])
+        result["high"] = move(low, near_z)
+        weights[0] = low, move(low, own_axis)
+
+    def gather_last():
+        (high,) = call(copy_kernel, "copy", (result["high"],), [((2, owned, model), bf16)])
+        weights[1] = high, move(high, own_axis)
 
     def second_sum(i):
         send, kept = call(
@@ -620,7 +649,7 @@
             parts[i],
             [((2, owned, cols), bf16), ((2, owned, cols), f32)],
         )
-        parts[i] = (kept, move(send, gather_near))
+        parts[i] = (kept, move(send, other_axis))
 
     def z_sum(i):
         to_first, to_second, own = call(
@@ -639,7 +668,7 @@
         attn_grads[i] = call(
             functools.partial(attn_grad_kernel, pair=i),
             "attn_grad",
-            (attn_t, dy_own, dy_far, *weights[i]),
+            (forward_results[5], dy_own, dy_far, *weights[i]),
             [((2 * HD, tokens), bf16), ((2, tokens), f32), ((2 * HD, model), bf16)],
             limit=16,
         )
@@ -648,7 +677,7 @@
         out_send, out_own = call(
             projection_kernel,
             "projection",
-            (attn, attn_grads[0][2], attn_grads[1][2]),
+            (forward_results[4], attn_grads[0][2], attn_grads[1][2]),
             [((rows, model), bf16), ((rows, model), f32)],
             limit=16,
         )
@@ -658,7 +687,7 @@
         send, own = call(
             functools.partial(backward_kernel, pair=i),
             "backward",
-            (rot_q, rot_k, rot_kt, values, *attn_grads[i][:2], lse, bias, cos, sin),
+            (*forward_results[:4], *attn_grads[i][:2], *forward_results[6:]),
             [((3, rows, 2 * HD), bf16)] * 2,
             limit=24,
         )
@@ -675,22 +704,22 @@
             final=True,
         )
 
+    forward()
     weight_grad(0)
-    gather_near_step(0)
+    gather_beside()
     weight_grad(1)
-    gather_near_step(1)
-    gather_far_step(0)
+    gather_pick()
     second_sum(0)
-    gather_far_step(1)
     second_sum(1)
     z_sum(0)
+    gather_last()
     z_sum(1)
     attn_grad(0)
     backward(0)
     share(0)
     attn_grad(1)
+    projection()
     backward(1)
-    projection()
     share(1)
     finish()
     *sharded, weight_grad = result["all"]

time: 62.4 us -> 54.4 us (0.87)
  waiting for transfers between devices: 24.8 us -> 16.3 us
  local copies, waits for them, and re-layouts: 0.02 us -> 0.69 us
    ppermute x14, waiting for transfers between devices: 23.3 us -> 14.8 us  [move(): return lax.ppermute(array, ('dp', 'ctx'), chip_moves(rule))]
    ppermute x14, starting transfers between devices: 18.5 us -> 16.9 us  [move(): return lax.ppermute(array, ('dp', 'ctx'), chip_moves(rule))]
    ppermute x8 -> x7, starting transfers between devices: 1.82 us -> 3.31 us  [swap_core(): return lax.ppermute(array, 'ctx', [(0, 1), (1, 0)])]
    unnamed x8 -> x10, local copies, waits for them, and re-layouts: 0.02 us -> 0.69 us
    pallas_call x20 -> x19, Pallas kernels: 16.1 us -> 16.2 us  [call(): pl.pallas_call(kernel, in_specs=list(specs or [in_vmem] * len(args)) + [a...]
    ppermute x8 -> x7, waiting for transfers between devices: 1.52 us -> 1.46 us  [swap_core(): return lax.ppermute(array, 'ctx', [(0, 1), (1, 0)])]
  transfers between devices with their start and end apart: 22 -> 21, of which waited for: 8 -> 9; matrix products, arithmetic and copies ran while one was open for 0% -> 0% of each run, Pallas kernels for 20% -> 23%
where the time goes in v4:
time: 54.4 us; the launch traced here: 54.2 us
  starting transfers between devices  20.2 us (37%)
  waiting for transfers between devices  16.3 us (30%)
  Pallas kernels  16.2 us (30%)
  between operations  0.83 us (2%)
  local copies, waits for them, and re-layouts  0.69 us (1%)
    ppermute x14, starting transfers between devices, move(): return lax.ppermute(array, ('dp', 'ctx'), chip_moves(rule))  16.9 us
    pallas_call x19, Pallas kernels, call(): pl.pallas_call(kernel, in_specs=list(specs or [in_vmem] * len(args)) + [a...  16.2 us
    ppermute x14, waiting for transfers between devices, move(): return lax.ppermute(array, ('dp', 'ctx'), chip_moves(rule))  14.8 us
    ppermute x7, starting transfers between devices, swap_core(): return lax.ppermute(array, 'ctx', [(0, 1), (1, 0)])  3.31 us
    ppermute x7, waiting for transfers between devices, swap_core(): return lax.ppermute(array, 'ctx', [(0, 1), (1, 0)])  1.46 us
  transfers between devices with their start and end apart: 21, of which 9 were waited for; matrix products, arithmetic and copies ran while one was open for 0% of the time, Pallas kernels for 23%

profile of v4, /device:TPU:0, one launch (start us, length us, event | category | flops | bytes accessed | tf_op | source)
XLA Modules:
  0.0 54.2 jit_solution(13315930125041870974)
XLA Ops:
  0.6 0.0 copy-start.3
  0.6 0.7 %copy-done.3 = s32[1,256]{1,0:T(1,128)S(1)} copy-done((s32[1,256]{1,0:T(1,128)S(1)}, s32[1,256]{1,0:T(1,128)}, u32[]{:S(2)}) %copy-start.3) | copy-done | bytes 1048
  1.3 1.5 %pack.1 = (bf16[3,272,512]{2,1,0:T(8,128)(2,1)S(1)}, bf16[3,256,512]{2,1,0:T(8,128)(2,1)S(1)}) custom-call(s32[1,256]{1,0:T(1,128)S(1)} %copy-done.3, bf16[256,1024]{1,0:T(8,128)(2,1)} %bitcast.13, bf16[256,1024]{1,0:T(8,128)(2,1)} %bitcast.14, bf16[256,1024]{1,0:T(8,128)(2,1)} %bitcast.15), custom_call_target="tpu_custom_call" | custom-call | flops 10000000000 | bytes 1 | tf_op jit(solution)/shard_map/pack/pallas_call | solution.py:569
  2.8 0.5 collective-permute-start
  3.4 0.0 copy-done
  3.4 0.1 collective-permute-start.1
  3.5 0.0 copy-done.1
  3.5 2.9 %collective-permute-start.2 = (bf16[64,2048]{1,0:T(8,128)(2,1)S(1)}, bf16[64,2048]{1,0:T(8,128)(2,1)S(1)}, u32[]{:S(2)}, u32[]{:S(2)}) collective-permute-start(bf16[64,2048]{1,0:T(8,128)(2,1)S(1)} %copy-done.1), channel_id=1, source_target_pairs={{0,4},{1,3},{2,6},{3,1},{4,0},{5,7},{6,2},{7,5},{8,12},{9,11},{10,... | collective-permute-start | bytes 786440 | tf_op jit(solution)/shard_map/ppermute | solution.py:246
  6.4 2.6 %collective-permute-start.3 = (bf16[64,2048]{1,0:T(8,128)(2,1)S(1)}, bf16[64,2048]{1,0:T(8,128)(2,1)S(1)}, u32[]{:S(2)}, u32[]{:S(2)}) collective-permute-start(bf16[64,2048]{1,0:T(8,128)(2,1)S(1)} %copy-done.1), channel_id=1, source_target_pairs={{0,16},{1,0},{2,18},{3,2},{4,20},{5,4},{6,22},{7,6},{8,24},{9,8},{... | collective-permute-start | bytes 786440 | tf_op jit(solution)/shard_map/ppermute | solution.py:246
  9.0 0.0 collective-permute-done.received
  9.0 0.0 copy-done.2
  9.0 0.0 copy-done.4
  9.0 3.1 %forward.1 = (bf16[512,512]{1,0:T(8,128)(2,1)S(1)}, bf16[512,512]{1,0:T(8,128)(2,1)S(1)}, bf16[512,512]{1,0:T(8,128)(2,1)S(1)}, bf16[512,512]{1,0:T(8,128)(2,1)S...) custom-call(s32[1,4,4]{2,1,0:T(4,128)S(1)} %copy-done.2, ...), custom_call_target="tpu_custom_call" | custom-call | flops 10000000000 | bytes 1 | tf_op jit(solution)/shard_map/forward/pallas_call | solution.py:569
  12.1 0.0 collective-permute-done.1.other
  12.1 1.3 %weight_grad.2 = (bf16[2,2,64,1024]{3,2,1,0:T(8,128)(2,1)S(1)}, bf16[2,2,64,1024]{3,2,1,0:T(8,128)(2,1)S(1)}) custom-call(bf16[512,512]{1,0:T(8,128)(2,1)S(1)} %get-tuple-element.51.attn_t, bf16[256,2048]{1,0:T(8,128)(2,1)S(1)} %bitcast.9, bf16[256,2048]{1,0:T(8,128)(2,1)S(1)} %collective-permute-done.1.other, ...), custom_call_target="tpu_custom_call" | custom-call | flops 10000000000 | bytes 1 | tf_op jit(solution)/shard_map/weight_grad/pallas_call | solution.py:569
  13.4 1.6 %collective-permute-start.7 = (bf16[2,2,64,1024]{3,2,1,0:T(8,128)(2,1)S(1)}, bf16[2,2,64,1024]{3,2,1,0:T(8,128)(2,1)S(1)}, u32[]{:S(2)}, u32[]{:S(2)}) collective-permute-start(bf16[2,2,64,1024]{3,2,1,0:T(8,128)(2,1)S(1)} %get-tuple-element.53.refs_0_), channel_id=1, source_target_pairs={{0,2},{1,5},{2,0},{3,7},{4,6},{5,1},{6,4},{7,3},{8,10},{9,13},{10,... | collective-permute-start | bytes 1572872 | tf_op jit(solution)/shard_map/ppermute | solution.py:246
  15.0 0.0 collective-permute-done.2.a.home1
  15.0 0.4 collective-permute-start.4
  15.4 1.3 %weight_grad.3 = (bf16[2,2,64,1024]{3,2,1,0:T(8,128)(2,1)S(1)}, bf16[2,2,64,1024]{3,2,1,0:T(8,128)(2,1)S(1)}) custom-call(bf16[512,512]{1,0:T(8,128)(2,1)S(1)} %get-tuple-element.51.attn_t, bf16[256,2048]{1,0:T(8,128)(2,1)S(1)} %bitcast.10, bf16[256,2048]{1,0:T(8,128)(2,1)S(1)} %collective-permute-done.1.other, bf16[64,2048]{1,0:T(8,128)(2,1)S(1)} %copy.14.refs_0_), custom_call_target="tpu_custom_call" | custom-call | flops 10000000000 | bytes 1 | tf_op jit(solution)/shard_map/weight_grad/pallas_call | solution.py:569
  16.7 0.6 %collective-permute-start.6 = (bf16[2,2,64,1024]{3,2,1,0:T(8,128)(2,1)S(1)}, bf16[2,2,64,1024]{3,2,1,0:T(8,128)(2,1)S(1)}, u32[]{:S(2)}, u32[]{:S(2)}) collective-permute-start(bf16[2,2,64,1024]{3,2,1,0:T(8,128)(2,1)S(1)} %get-tuple-element.54.refs_0_), channel_id=1, source_target_pairs={{0,2},{1,5},{2,0},{3,7},{4,6},{5,1},{6,4},{7,3},{8,10},{9,13},{10,... | collective-permute-start | bytes 1572872 | tf_op jit(solution)/shard_map/ppermute | solution.py:246
  17.4 0.0 collective-permute-done.3.away0
  17.4 2.0 %collective-permute-done.4.away1 = bf16[64,2048]{1,0:T(8,128)(2,1)S(1)} collective-permute-done((bf16[64,2048]{1,0:T(8,128)(2,1)S(1)}, bf16[64,2048]{1,0:T(8,128)(2,1)S(1)}, u32[]{:S(2)}, u32[]{:S(2)}) %collective-permute-start.4) | collective-permute-done | bytes 262176 | tf_op jit(solution)/shard_map/ppermute | solution.py:246
  19.4 4.3 %collective-permute-start.9 = (bf16[2,64,2048]{2,1,0:T(8,128)(2,1)S(1)}, bf16[2,64,2048]{2,1,0:T(8,128)(2,1)S(1)}, u32[]{:S(2)}, u32[]{:S(2)}) collective-permute-start(bf16[2,64,2048]{2,1,0:T(8,128)(2,1)S(1)} %gather_pick.1.refs_0_.near), channel_id=1, source_target_pairs={{0,8},{1,9},{2,10},{3,11},{4,12},{5,13},{6,14},{7,15},{8,0},{9,1},... | collective-permute-start | bytes 1572872 | tf_op jit(solution)/shard_map/ppermute | solution.py:246
  23.7 0.7 %collective-permute-start.5 = (bf16[2,64,2048]{2,1,0:T(8,128)(2,1)S(1)}, bf16[2,64,2048]{2,1,0:T(8,128)(2,1)S(1)}, u32[]{:S(2)}, u32[]{:S(2)}) collective-permute-start(bf16[2,64,2048]{2,1,0:T(8,128)(2,1)S(1)} %gather_pick.1.refs_0_.near), channel_id=1, source_target_pairs={{0,2},{1,5},{2,0},{3,7},{4,6},{5,1},{6,4},{7,3},{8,10},{9,13},{10,... | collective-permute-start | bytes 1572872 | tf_op jit(solution)/shard_map/ppermute | solution.py:246
  24.4 0.0 collective-permute-done.7.got
  24.4 0.1 second_sum.2
  24.5 1.5 %collective-permute-start.10 = (bf16[2,64,1024]{2,1,0:T(8,128)(2,1)S(1)}, bf16[2,64,1024]{2,1,0:T(8,128)(2,1)S(1)}, u32[]{:S(2)}, u32[]{:S(2)}) collective-permute-start(bf16[2,64,1024]{2,1,0:T(8,128)(2,1)S(1)} %get-tuple-element.57.refs_0_), channel_id=1, source_target_pairs={{0,4},{1,3},{2,6},{3,1},{4,0},{5,7},{6,2},{7,5},{8,12},{9,11},{10,... | collective-permute-start | bytes 786440 | tf_op jit(solution)/shard_map/ppermute | solution.py:246
  26.0 5.6 %collective-permute-done.6.got = bf16[2,2,64,1024]{3,2,1,0:T(8,128)(2,1)S(1)} collective-permute-done((bf16[2,2,64,1024]{3,2,1,0:T(8,128)(2,1)S(1)}, bf16[2,2,64,1024]{3,2,1,0:T(8,128)(2,1)S(1)}, u32[]{:S(2)}, u32[]{:S(2)}) %collective-permute-start.6) | collective-permute-done | bytes 524320 | tf_op jit(solution)/shard_map/ppermute | solution.py:246
  31.6 0.1 second_sum.3
  31.7 0.1 collective-permute-start.8
  31.8 1.9 %collective-permute-done.10.got = bf16[2,64,1024]{2,1,0:T(8,128)(2,1)S(1)} collective-permute-done((bf16[2,64,1024]{2,1,0:T(8,128)(2,1)S(1)}, bf16[2,64,1024]{2,1,0:T(8,128)(2,1)S(1)}, u32[]{:S(2)}, u32[]{:S(2)}) %collective-permute-start.10) | collective-permute-done | bytes 262176 | tf_op jit(solution)/shard_map/ppermute | solution.py:246
  33.7 0.1 z_sum.2
  33.8 0.1 collective-permute-start.12
  33.9 0.1 collective-permute-start.13
  33.9 1.6 %collective-permute-done.9.a = bf16[2,64,2048]{2,1,0:T(8,128)(2,1)S(1)} collective-permute-done((bf16[2,64,2048]{2,1,0:T(8,128)(2,1)S(1)}, bf16[2,64,2048]{2,1,0:T(8,128)(2,1)S(1)}, u32[]{:S(2)}, u32[]{:S(2)}) %collective-permute-start.9) | collective-permute-done | bytes 524320 | tf_op jit(solution)/shard_map/ppermute | solution.py:246
  35.6 1.6 %collective-permute-start.11 = (bf16[2,64,2048]{2,1,0:T(8,128)(2,1)S(1)}, bf16[2,64,2048]{2,1,0:T(8,128)(2,1)S(1)}, u32[]{:S(2)}, u32[]{:S(2)}) collective-permute-start(bf16[2,64,2048]{2,1,0:T(8,128)(2,1)S(1)} %copy.15.refs_0_.near), channel_id=1, source_target_pairs={{0,2},{1,5},{2,0},{3,7},{4,6},{5,1},{6,4},{7,3},{8,10},{9,13},{10,... | collective-permute-start | bytes 1572872 | tf_op jit(solution)/shard_map/ppermute | solution.py:246
  37.2 1.0 %collective-permute-done.8.got = bf16[2,64,1024]{2,1,0:T(8,128)(2,1)S(1)} collective-permute-done((bf16[2,64,1024]{2,1,0:T(8,128)(2,1)S(1)}, bf16[2,64,1024]{2,1,0:T(8,128)(2,1)S(1)}, u32[]{:S(2)}, u32[]{:S(2)}) %collective-permute-start.8) | collective-permute-done | bytes 262176 | tf_op jit(solution)/shard_map/ppermute | solution.py:246
  38.1 0.1 z_sum.3
  38.2 0.6 %collective-permute-start.18 = (bf16[64,1024]{1,0:T(8,128)(2,1)S(1)}, bf16[64,1024]{1,0:T(8,128)(2,1)S(1)}, u32[]{:S(2)}, u32[]{:S(2)}) collective-permute-start(bf16[64,1024]{1,0:T(8,128)(2,1)S(1)} %get-tuple-element.62.refs_0_), channel_id=1, source_target_pairs={{0,9},{1,17},{2,11},{3,19},{4,13},{5,21},{6,15},{7,23},{8,1},{9,25... | collective-permute-start | bytes 393224 | tf_op jit(solution)/shard_map/ppermute | solution.py:246
  38.9 0.7 %collective-permute-done.5.far = bf16[2,64,2048]{2,1,0:T(8,128)(2,1)S(1)} collective-permute-done((bf16[2,64,2048]{2,1,0:T(8,128)(2,1)S(1)}, bf16[2,64,2048]{2,1,0:T(8,128)(2,1)S(1)}, u32[]{:S(2)}, u32[]{:S(2)}) %collective-permute-start.5) | collective-permute-done | bytes 524320 | tf_op jit(solution)/shard_map/ppermute | solution.py:246
  39.5 0.0 collective-permute-start.19
  39.5 0.8 %attn_grad.2 = (bf16[256,512]{1,0:T(8,128)(2,1)S(1)}, f32[2,512]{1,0:T(2,128)S(1)}, bf16[256,2048]{1,0:T(8,128)(2,1)S(1)}) custom-call(bf16[512,512]{1,0:T(8,128)(2,1)S(1)} %get-tuple-element.51.attn_t, bf16[256,2048]{1,0:T(8,128)(2,1)S(1)} %bitcast.11, bf16[256,2048]{1,0:T(8,128)(2,1)S(1)} %collective-permute-done.1.other, ...), custom_call_target="tpu_custom_call" | custom-call | flops 10000000000 | bytes 1 | tf_op jit(solution)/shard_map/attn_grad/pallas_call | solution.py:569
  40.4 1.6 %backward.2 = (bf16[3,256,256]{2,1,0:T(8,128)(2,1)S(1)}, bf16[3,256,256]{2,1,0:T(8,128)(2,1)S(1)}) custom-call(bf16[512,512]{1,0:T(8,128)(2,1)S(1)} %get-tuple-element.52.refs_0_.rot_q, bf16[512,512]{1,0:T(8,128)(2,1)S(1)} %get-tuple-element.66.rot_k, bf16[512,512]{1,0:T(8,128)(2,1)S(1)} %get-tuple-element.67.rot_kt, ...), custom_call_target="tpu_custom_call" | custom-call | flops 10000000000 | bytes 1 | tf_op jit(solution)/shard_map/backward/pallas_call | solution.py:569
  42.0 0.0 collective-permute-done.12.first
  42.0 1.0 %collective-permute-start.15 = (bf16[3,256,256]{2,1,0:T(8,128)(2,1)S(1)}, bf16[3,256,256]{2,1,0:T(8,128)(2,1)S(1)}, u32[]{:S(2)}, u32[]{:S(2)}) collective-permute-start(bf16[3,256,256]{2,1,0:T(8,128)(2,1)S(1)} %get-tuple-element.75.refs_0_), channel_id=1, source_target_pairs={{0,1},{1,0},{2,3},{3,2},{4,5},{5,4},{6,7},{7,6},{8,9},{9,8},{10,11... | collective-permute-start | bytes 1179656 | tf_op jit(solution)/shard_map/ppermute | solution.py:250
  43.0 0.9 %collective-permute-done.13.second = bf16[64,1024]{1,0:T(8,128)(2,1)S(1)} collective-permute-done((bf16[64,1024]{1,0:T(8,128)(2,1)S(1)}, bf16[64,1024]{1,0:T(8,128)(2,1)S(1)}, u32[]{:S(2)}, u32[]{:S(2)}) %collective-permute-start.13) | collective-permute-done | bytes 131104 | tf_op jit(solution)/shard_map/ppermute | solution.py:246
  43.8 0.1 share.2.refs_0_.refs_6_
  43.9 0.1 collective-permute-start.17
  44.0 1.2 %collective-permute-done.11.far = bf16[2,64,2048]{2,1,0:T(8,128)(2,1)S(1)} collective-permute-done((bf16[2,64,2048]{2,1,0:T(8,128)(2,1)S(1)}, bf16[2,64,2048]{2,1,0:T(8,128)(2,1)S(1)}, u32[]{:S(2)}, u32[]{:S(2)}) %collective-permute-start.11) | collective-permute-done | bytes 524320 | tf_op jit(solution)/shard_map/ppermute | solution.py:246
  45.2 0.8 %attn_grad.3 = (bf16[256,512]{1,0:T(8,128)(2,1)S(1)}, f32[2,512]{1,0:T(2,128)S(1)}, bf16[256,2048]{1,0:T(8,128)(2,1)S(1)}) custom-call(bf16[512,512]{1,0:T(8,128)(2,1)S(1)} %get-tuple-element.51.attn_t, bf16[256,2048]{1,0:T(8,128)(2,1)S(1)} %bitcast.12, bf16[256,2048]{1,0:T(8,128)(2,1)S(1)} %collective-permute-done.1.other, ...), custom_call_target="tpu_custom_call" | custom-call | flops 10000000000 | bytes 1 | tf_op jit(solution)/shard_map/attn_grad/pallas_call | solution.py:569
  46.0 1.3 %projection.1 = (bf16[256,2048]{1,0:T(8,128)(2,1)S(1)}, f32[256,2048]{1,0:T(8,128)S(1)}) custom-call(bf16[512,512]{1,0:T(8,128)(2,1)S(1)} %get-tuple-element.50.attn, bf16[256,2048]{1,0:T(8,128)(2,1)S(1)} %get-tuple-element.63.low, bf16[256,2048]{1,0:T(8,128)(2,1)S(1)} %get-tuple-element.76.high, bf16[256,512]{1,0:T(8,128)(2,1)S(1)} %get-tuple-element.77.refs_0_.grad_t), custom_call_target="tpu_custom_call" | custom-call | flops 10000000000 | bytes 1 | tf_op jit(solution)/shard_map/projection/pallas_call | solution.py:569
  47.2 1.0 %collective-permute-start.14 = (bf16[256,2048]{1,0:T(8,128)(2,1)S(1)}, bf16[256,2048]{1,0:T(8,128)(2,1)S(1)}, u32[]{:S(2)}, u32[]{:S(2)}) collective-permute-start(bf16[256,2048]{1,0:T(8,128)(2,1)S(1)} %get-tuple-element.79.refs_0_), channel_id=1, source_target_pairs={{0,1},{1,0},{2,3},{3,2},{4,5},{5,4},{6,7},{7,6},{8,9},{9,8},{10,11... | collective-permute-start | bytes 3145736 | tf_op jit(solution)/shard_map/ppermute | solution.py:250
  48.2 1.6 %backward.3 = (bf16[3,256,256]{2,1,0:T(8,128)(2,1)S(1)}, bf16[3,256,256]{2,1,0:T(8,128)(2,1)S(1)}) custom-call(bf16[512,512]{1,0:T(8,128)(2,1)S(1)} %get-tuple-element.52.refs_0_.rot_q, bf16[512,512]{1,0:T(8,128)(2,1)S(1)} %get-tuple-element.66.rot_k, bf16[512,512]{1,0:T(8,128)(2,1)S(1)} %get-tuple-element.67.rot_kt, ...), custom_call_target="tpu_custom_call" | custom-call | flops 10000000000 | bytes 1 | tf_op jit(solution)/shard_map/backward/pallas_call | solution.py:569
  49.9 0.0 collective-permute-done.18.first
  49.9 0.1 collective-permute-start.16
  50.0 0.0 collective-permute-done.19.second
  50.0 0.1 share.3.refs_8_
  50.0 0.6 %collective-permute-start.20 = (f32[64,1024]{1,0:T(8,128)S(1)}, f32[64,1024]{1,0:T(8,128)S(1)}, u32[]{:S(2)}, u32[]{:S(2)}) collective-permute-start(f32[64,1024]{1,0:T(8,128)S(1)} %share.3.refs_8_), channel_id=1, source_target_pairs={{0,1},{1,0},{2,3},{3,2},{4,5},{5,4},{6,7},{7,6},{8,9},{9,8},{10,11... | collective-permute-start | bytes 786440 | tf_op jit(solution)/shard_map/ppermute | solution.py:250
  50.6 0.0 collective-permute-done.17.refs_7_
  50.6 0.0 collective-permute-done.15.refs_3_
  50.6 1.4 %collective-permute-done.20.refs_9_ = f32[64,1024]{1,0:T(8,128)S(1)} collective-permute-done((f32[64,1024]{1,0:T(8,128)S(1)}, f32[64,1024]{1,0:T(8,128)S(1)}, u32[]{:S(2)}, u32[]{:S(2)}) %collective-permute-start.20) | collective-permute-done | bytes 262176 | tf_op jit(solution)/shard_map/ppermute | solution.py:250
  52.0 0.0 collective-permute-done.16.refs_5_
  52.0 0.0 collective-permute-done.14.refs_1_
  52.0 2.2 %finish.1 = (bf16[256,2048]{1,0:T(8,128)(2,1)}, bf16[256,1024]{1,0:T(8,128)(2,1)}, bf16[256,1024]{1,0:T(8,128)(2,1)}, bf16[256,1024]{1,0:T(8,128)(2,1)}, f32[64,2048]{1,0:T(8,128)}) custom-call(f32[256,2048]{1,0:T(8,128)S(1)} %get-tuple-element.78.refs_0_, bf16[256,2048]{1,0:T(8,128)(2,1)S(1)} %collective-permute-done.14.refs_1_, ...), custom_call_target="tpu_custom_call" | custom-call | flops 10000000000 | bytes 1 | tf_op jit(solution)/shard_map/finish/pallas_call | solution.py:569
  (7 shorter events, 0.1 us)
Async XLA Ops:
  0.6 0.7 %copy-start.3 = (s32[1,256]{1,0:T(1,128)S(1)}, s32[1,256]{1,0:T(1,128)}, u32[]{:S(2)}) copy-start(s32[1,256]{1,0:T(1,128)} %near.1) | copy-start | bytes 3076
  1.3 2.0 %copy-start = (bf16[1,256,2048]{2,1,0:T(8,128)(2,1)S(1)}, bf16[1,256,2048]{2,1,0:T(8,128)(2,1)}, u32[]{:S(2)}) copy-start(bf16[1,256,2048]{2,1,0:T(8,128)(2,1)} %param.13) | copy-start | bytes 3145732
  1.3 2.1 %copy-start.1 = (bf16[64,2048]{1,0:T(8,128)(2,1)S(1)}, bf16[64,2048]{1,0:T(8,128)(2,1)}, u32[]{:S(2)}) copy-start(bf16[64,2048]{1,0:T(8,128)(2,1)} %home0.1) | copy-start | bytes 786436
  1.3 7.7 %copy-start.2 = (s32[1,4,4]{2,1,0:T(4,128)S(1)}, s32[1,4,4]{2,1,0:T(4,128)}, u32[]{:S(2)}) copy-start(s32[1,4,4]{2,1,0:T(4,128)} %pattern.1) | copy-start | bytes 196
  1.3 7.7 %copy-start.4 = (s32[1,256]{1,0:T(1,128)S(1)}, s32[1,256]{1,0:T(1,128)}, u32[]{:S(2)}) copy-start(s32[1,256]{1,0:T(1,128)} %near.1) | copy-start | bytes 3076
  2.8 6.1 %collective-permute-start = (bf16[3,272,512]{2,1,0:T(8,128)(2,1)S(1)}, bf16[3,272,512]{2,1,0:T(8,128)(2,1)S(1)}, u32[]{:S(2)}, u32[]{:S(2)}) collective-permute-start(bf16[3,272,512]{2,1,0:T(8,128)(2,1)S(1)} %get-tuple-element.49), channel_id=1, source_target_pairs={{0,1},{1,0},{2,3},{3,2},{4,5},{5,4},{6,7},{7,6},{8,9},{9,8},{10,11... | collective-permute-start | bytes 2506760 | tf_op jit(solution)/shard_map/ppermute | solution.py:250
  3.4 8.7 %collective-permute-start.1 = (bf16[256,2048]{1,0:T(8,128)(2,1)S(1)}, bf16[256,2048]{1,0:T(8,128)(2,1)S(1)}, u32[]{:S(2)}, u32[]{:S(2)}) collective-permute-start(bf16[256,2048]{1,0:T(8,128)(2,1)S(1)} %bitcast.8), channel_id=1, source_target_pairs={{0,1},{1,0},{2,3},{3,2},{4,5},{5,4},{6,7},{7,6},{8,9},{9,8},{10,11... | collective-permute-start | bytes 3145736 | tf_op jit(solution)/shard_map/ppermute | solution.py:250
  3.5 11.5 %collective-permute-start.2 = (bf16[64,2048]{1,0:T(8,128)(2,1)S(1)}, bf16[64,2048]{1,0:T(8,128)(2,1)S(1)}, u32[]{:S(2)}, u32[]{:S(2)}) collective-permute-start(bf16[64,2048]{1,0:T(8,128)(2,1)S(1)} %copy-done.1), channel_id=1, source_target_pairs={{0,4},{1,3},{2,6},{3,1},{4,0},{5,7},{6,2},{7,5},{8,12},{9,11},{10,... | collective-permute-start | bytes 786440 | tf_op jit(solution)/shard_map/ppermute | solution.py:246
  6.4 11.0 %collective-permute-start.3 = (bf16[64,2048]{1,0:T(8,128)(2,1)S(1)}, bf16[64,2048]{1,0:T(8,128)(2,1)S(1)}, u32[]{:S(2)}, u32[]{:S(2)}) collective-permute-start(bf16[64,2048]{1,0:T(8,128)(2,1)S(1)} %copy-done.1), channel_id=1, source_target_pairs={{0,16},{1,0},{2,18},{3,2},{4,20},{5,4},{6,22},{7,6},{8,24},{9,8},{... | collective-permute-start | bytes 786440 | tf_op jit(solution)/shard_map/ppermute | solution.py:246
  13.4 10.9 %collective-permute-start.7 = (bf16[2,2,64,1024]{3,2,1,0:T(8,128)(2,1)S(1)}, bf16[2,2,64,1024]{3,2,1,0:T(8,128)(2,1)S(1)}, u32[]{:S(2)}, u32[]{:S(2)}) collective-permute-start(bf16[2,2,64,1024]{3,2,1,0:T(8,128)(2,1)S(1)} %get-tuple-element.53.refs_0_), channel_id=1, source_target_pairs={{0,2},{1,5},{2,0},{3,7},{4,6},{5,1},{6,4},{7,3},{8,10},{9,13},{10,... | collective-permute-start | bytes 1572872 | tf_op jit(solution)/shard_map/ppermute | solution.py:246
  15.0 4.3 %collective-permute-start.4 = (bf16[64,2048]{1,0:T(8,128)(2,1)S(1)}, bf16[64,2048]{1,0:T(8,128)(2,1)S(1)}, u32[]{:S(2)}, u32[]{:S(2)}) collective-permute-start(bf16[64,2048]{1,0:T(8,128)(2,1)S(1)} %copy.14.refs_0_), channel_id=1, source_target_pairs={{0,16},{1,0},{2,18},{3,2},{4,20},{5,4},{6,22},{7,6},{8,24},{9,8},{... | collective-permute-start | bytes 786440 | tf_op jit(solution)/shard_map/ppermute | solution.py:246
  16.7 14.8 %collective-permute-start.6 = (bf16[2,2,64,1024]{3,2,1,0:T(8,128)(2,1)S(1)}, bf16[2,2,64,1024]{3,2,1,0:T(8,128)(2,1)S(1)}, u32[]{:S(2)}, u32[]{:S(2)}) collective-permute-start(bf16[2,2,64,1024]{3,2,1,0:T(8,128)(2,1)S(1)} %get-tuple-element.54.refs_0_), channel_id=1, source_target_pairs={{0,2},{1,5},{2,0},{3,7},{4,6},{5,1},{6,4},{7,3},{8,10},{9,13},{10,... | collective-permute-start | bytes 1572872 | tf_op jit(solution)/shard_map/ppermute | solution.py:246
  19.4 16.2 %collective-permute-start.9 = (bf16[2,64,2048]{2,1,0:T(8,128)(2,1)S(1)}, bf16[2,64,2048]{2,1,0:T(8,128)(2,1)S(1)}, u32[]{:S(2)}, u32[]{:S(2)}) collective-permute-start(bf16[2,64,2048]{2,1,0:T(8,128)(2,1)S(1)} %gather_pick.1.refs_0_.near), channel_id=1, source_target_pairs={{0,8},{1,9},{2,10},{3,11},{4,12},{5,13},{6,14},{7,15},{8,0},{9,1},... | collective-permute-start | bytes 1572872 | tf_op jit(solution)/shard_map/ppermute | solution.py:246
  23.7 15.8 %collective-permute-start.5 = (bf16[2,64,2048]{2,1,0:T(8,128)(2,1)S(1)}, bf16[2,64,2048]{2,1,0:T(8,128)(2,1)S(1)}, u32[]{:S(2)}, u32[]{:S(2)}) collective-permute-start(bf16[2,64,2048]{2,1,0:T(8,128)(2,1)S(1)} %gather_pick.1.refs_0_.near), channel_id=1, source_target_pairs={{0,2},{1,5},{2,0},{3,7},{4,6},{5,1},{6,4},{7,3},{8,10},{9,13},{10,... | collective-permute-start | bytes 1572872 | tf_op jit(solution)/shard_map/ppermute | solution.py:246
  24.5 9.2 %collective-permute-start.10 = (bf16[2,64,1024]{2,1,0:T(8,128)(2,1)S(1)}, bf16[2,64,1024]{2,1,0:T(8,128)(2,1)S(1)}, u32[]{:S(2)}, u32[]{:S(2)}) collective-permute-start(bf16[2,64,1024]{2,1,0:T(8,128)(2,1)S(1)} %get-tuple-element.57.refs_0_), channel_id=1, source_target_pairs={{0,4},{1,3},{2,6},{3,1},{4,0},{5,7},{6,2},{7,5},{8,12},{9,11},{10,... | collective-permute-start | bytes 786440 | tf_op jit(solution)/shard_map/ppermute | solution.py:246
  31.7 6.4 %collective-permute-start.8 = (bf16[2,64,1024]{2,1,0:T(8,128)(2,1)S(1)}, bf16[2,64,1024]{2,1,0:T(8,128)(2,1)S(1)}, u32[]{:S(2)}, u32[]{:S(2)}) collective-permute-start(bf16[2,64,1024]{2,1,0:T(8,128)(2,1)S(1)} %get-tuple-element.59.refs_0_), channel_id=1, source_target_pairs={{0,4},{1,3},{2,6},{3,1},{4,0},{5,7},{6,2},{7,5},{8,12},{9,11},{10,... | collective-permute-start | bytes 786440 | tf_op jit(solution)/shard_map/ppermute | solution.py:246
  33.8 8.2 %collective-permute-start.12 = (bf16[64,1024]{1,0:T(8,128)(2,1)S(1)}, bf16[64,1024]{1,0:T(8,128)(2,1)S(1)}, u32[]{:S(2)}, u32[]{:S(2)}) collective-permute-start(bf16[64,1024]{1,0:T(8,128)(2,1)S(1)} %get-tuple-element.61.refs_0_), channel_id=1, source_target_pairs={{0,9},{1,17},{2,11},{3,19},{4,13},{5,21},{6,15},{7,23},{8,1},{9,25... | collective-permute-start | bytes 393224 | tf_op jit(solution)/shard_map/ppermute | solution.py:246
  33.9 10.0 %collective-permute-start.13 = (bf16[64,1024]{1,0:T(8,128)(2,1)S(1)}, bf16[64,1024]{1,0:T(8,128)(2,1)S(1)}, u32[]{:S(2)}, u32[]{:S(2)}) collective-permute-start(bf16[64,1024]{1,0:T(8,128)(2,1)S(1)} %get-tuple-element.65), channel_id=1, source_target_pairs={{0,1},{1,25},{2,3},{3,27},{4,5},{5,29},{6,7},{7,31},{8,9},{9,17},{... | collective-permute-start | bytes 393224 | tf_op jit(solution)/shard_map/ppermute | solution.py:246
  35.6 9.6 %collective-permute-start.11 = (bf16[2,64,2048]{2,1,0:T(8,128)(2,1)S(1)}, bf16[2,64,2048]{2,1,0:T(8,128)(2,1)S(1)}, u32[]{:S(2)}, u32[]{:S(2)}) collective-permute-start(bf16[2,64,2048]{2,1,0:T(8,128)(2,1)S(1)} %copy.15.refs_0_.near), channel_id=1, source_target_pairs={{0,2},{1,5},{2,0},{3,7},{4,6},{5,1},{6,4},{7,3},{8,10},{9,13},{10,... | collective-permute-start | bytes 1572872 | tf_op jit(solution)/shard_map/ppermute | solution.py:246
  38.2 11.6 %collective-permute-start.18 = (bf16[64,1024]{1,0:T(8,128)(2,1)S(1)}, bf16[64,1024]{1,0:T(8,128)(2,1)S(1)}, u32[]{:S(2)}, u32[]{:S(2)}) collective-permute-start(bf16[64,1024]{1,0:T(8,128)(2,1)S(1)} %get-tuple-element.62.refs_0_), channel_id=1, source_target_pairs={{0,9},{1,17},{2,11},{3,19},{4,13},{5,21},{6,15},{7,23},{8,1},{9,25... | collective-permute-start | bytes 393224 | tf_op jit(solution)/shard_map/ppermute | solution.py:246
  39.5 10.4 %collective-permute-start.19 = (bf16[64,1024]{1,0:T(8,128)(2,1)S(1)}, bf16[64,1024]{1,0:T(8,128)(2,1)S(1)}, u32[]{:S(2)}, u32[]{:S(2)}) collective-permute-start(bf16[64,1024]{1,0:T(8,128)(2,1)S(1)} %get-tuple-element.85), channel_id=1, source_target_pairs={{0,1},{1,25},{2,3},{3,27},{4,5},{5,29},{6,7},{7,31},{8,9},{9,17},{... | collective-permute-start | bytes 393224 | tf_op jit(solution)/shard_map/ppermute | solution.py:246
  42.0 8.6 %collective-permute-start.15 = (bf16[3,256,256]{2,1,0:T(8,128)(2,1)S(1)}, bf16[3,256,256]{2,1,0:T(8,128)(2,1)S(1)}, u32[]{:S(2)}, u32[]{:S(2)}) collective-permute-start(bf16[3,256,256]{2,1,0:T(8,128)(2,1)S(1)} %get-tuple-element.75.refs_0_), channel_id=1, source_target_pairs={{0,1},{1,0},{2,3},{3,2},{4,5},{5,4},{6,7},{7,6},{8,9},{9,8},{10,11... | collective-permute-start | bytes 1179656 | tf_op jit(solution)/shard_map/ppermute | solution.py:250
  43.9 6.7 %collective-permute-start.17 = (f32[64,1024]{1,0:T(8,128)S(1)}, f32[64,1024]{1,0:T(8,128)S(1)}, u32[]{:S(2)}, u32[]{:S(2)}) collective-permute-start(f32[64,1024]{1,0:T(8,128)S(1)} %share.2.refs_0_.refs_6_), channel_id=1, source_target_pairs={{0,1},{1,0},{2,3},{3,2},{4,5},{5,4},{6,7},{7,6},{8,9},{9,8},{10,11... | collective-permute-start | bytes 786440 | tf_op jit(solution)/shard_map/ppermute | solution.py:250
  47.2 4.8 %collective-permute-start.14 = (bf16[256,2048]{1,0:T(8,128)(2,1)S(1)}, bf16[256,2048]{1,0:T(8,128)(2,1)S(1)}, u32[]{:S(2)}, u32[]{:S(2)}) collective-permute-start(bf16[256,2048]{1,0:T(8,128)(2,1)S(1)} %get-tuple-element.79.refs_0_), channel_id=1, source_target_pairs={{0,1},{1,0},{2,3},{3,2},{4,5},{5,4},{6,7},{7,6},{8,9},{9,8},{10,11... | collective-permute-start | bytes 3145736 | tf_op jit(solution)/shard_map/ppermute | solution.py:250
  49.9 2.2 %collective-permute-start.16 = (bf16[3,256,256]{2,1,0:T(8,128)(2,1)S(1)}, bf16[3,256,256]{2,1,0:T(8,128)(2,1)S(1)}, u32[]{:S(2)}, u32[]{:S(2)}) collective-permute-start(bf16[3,256,256]{2,1,0:T(8,128)(2,1)S(1)} %get-tuple-element.83.refs_0_), channel_id=1, source_target_pairs={{0,1},{1,0},{2,3},{3,2},{4,5},{5,4},{6,7},{7,6},{8,9},{9,8},{10,11... | collective-permute-start | bytes 1179656 | tf_op jit(solution)/shard_map/ppermute | solution.py:250
  50.0 2.0 %collective-permute-start.20 = (f32[64,1024]{1,0:T(8,128)S(1)}, f32[64,1024]{1,0:T(8,128)S(1)}, u32[]{:S(2)}, u32[]{:S(2)}) collective-permute-start(f32[64,1024]{1,0:T(8,128)S(1)} %share.3.refs_8_), channel_id=1, source_target_pairs={{0,1},{1,0},{2,3},{3,2},{4,5},{5,4},{6,7},{7,6},{8,9},{9,8},{10,11... | collective-permute-start | bytes 786440 | tf_op jit(solution)/shard_map/ppermute | solution.py:250

commit v5 on v4

--- a/solution.py
+++ b/solution.py
@@ -15,6 +15,7 @@
 BLK = 128
 KB = 4
 SUM_CHUNKS = 2
+KERNEL_COST = 10**10
 
 
 def padded(shard, sides, width):
@@ -490,19 +491,22 @@
             send[i, :, out_cols] = out[half:, :]
 
 
-def gather_pick_kernel(home0, home1, away0, away1, *refs):
+def gather_pick_kernel(home, away, *refs):
     core, z, _, _ = place()
     low = refs[-1]
 
     @pl.when(z // 2 == core)
     def _():
-        low[0] = home0[...]
-        low[1] = home1[...]
+        low[...] = home[...]
 
     @pl.when(z // 2 != core)
     def _():
-        low[0] = away0[...]
-        low[1] = away1[...]
+        low[...] = away[...]
+
+
+def pair_kernel(a, b, *refs):
+    refs[-1][0] = a[...]
+    refs[-1][1] = b[...]
 
 
 def copy_kernel(a, *refs):
@@ -534,22 +538,38 @@
 
 
 def finish_kernel(*refs, count):
-    layer_out, *grads, mean = refs[-5:]
+    layer_out, *grads, mean, layer_rows, mean_rows, sems = refs[-8:]
     out_own, out_got = refs[:2]
-    pairs, shares = refs[2:6], refs[6:-5]
+    pairs, shares = refs[2:6], refs[6:-8]
     core, z, _, _ = place()
     mine = grads[0].shape[1] // 2
     width = mine // 2
+    copies = []
+
+    def send(source, target):
+        copies.append(pltpu.make_async_copy(source, target, sems.at[len(copies)]))
+        copies[-1].start()
+
     for pair in range(2):
         for source in range(2):
             start = (core ^ source) * mine + (z % 2 ^ pair) * width
             cols = pl.ds(pl.multiple_of(start, width), width)
             for i in range(3):
-                grads[i][:, cols] = pairs[2 * pair + source][i]
-    layer_out[...] = (out_own[...] + out_got[...].astype(jnp.float32)).astype(layer_out.dtype)
+                send(pairs[2 * pair + source].at[i], grads[i].at[:, cols])
+    parts = 2
+    size = layer_rows.shape[0] // parts
+    for part in range(parts):
+        rows = slice(part * size, (part + 1) * size)
+        total = out_own[rows, :] + out_got[rows, :].astype(jnp.float32)
+        layer_rows[rows, :] = total.astype(layer_rows.dtype)
+        send(layer_rows.at[rows, :], layer_out.at[rows, :])
     width = shares[0].shape[1]
     for i in range(mean.shape[1] // width):
-        mean[:, i * width : (i + 1) * width] = (shares[2 * i][...] + shares[2 * i + 1][...]) * (1.0 / count)
+        total = shares[2 * i][...] + shares[2 * i + 1][...]
+        mean_rows[:, i * width : (i + 1) * width] = total * (1.0 / count)
+    send(mean_rows, mean)
+    for copy in copies:
+        copy.wait()
 
 
 def chip_shards(queries, key_states, value_states, token_order, block_pattern, out_weight, out_grad):
@@ -564,16 +584,16 @@
     anywhere = pl.BlockSpec(memory_space=pl.ANY)
     done = []
 
-    def call(kernel, name, args, outs, scratch=(), limit=8, specs=None, final=False):
+    def call(kernel, name, args, outs, scratch=(), limit=8, specs=None, final=False, out_space=pltpu.VMEM):
         before = [a for a in done if not any(a is b for b in args)]
         results = pl.pallas_call(
             kernel,
             in_specs=list(specs or [in_vmem] * len(args)) + [anywhere] * len(before),
-            out_specs=[in_vmem] * len(outs),
-            out_shape=[jax.ShapeDtypeStruct(s, d) for s, d in outs],
+            out_specs=[pl.BlockSpec(memory_space=out_space)] * len(outs),
+            out_shape=[out_space(s, d) if out_space is pltpu.HBM else jax.ShapeDtypeStruct(s, d) for s, d in outs],
             scratch_shapes=scratch,
             compiler_params=pltpu.CompilerParams(vmem_limit_bytes=limit << 20),
-            cost_estimate=pl.CostEstimate(flops=10000000000, bytes_accessed=1, transcendentals=0),
+            cost_estimate=pl.CostEstimate(flops=KERNEL_COST, bytes_accessed=1, transcendentals=0),
             name=name,
         )(*args, *before)
         if not final:
@@ -632,15 +652,15 @@
         (copied,) = call(copy_kernel, "copy", (beside,), [((owned, model), bf16)])
         result["beside"] = move(copied, at_home(far_z))
 
-    def gather_pick():
-        args = (out_weight, beside, beyond, result["beside"])
-        (low,) = call(gather_pick_kernel, "gather_pick", args, [((2, owned, model), bf16)])
-        result["high"] = move(low, near_z)
-        weights[0] = low, move(low, own_axis)
-
-    def gather_last():
-        (high,) = call(copy_kernel, "copy", (result["high"],), [((2, owned, model), bf16)])
-        weights[1] = high, move(high, own_axis)
+    def gather_pick(i):
+        args = ((out_weight, beyond), (beside, result["beside"]))[i]
+        (low,) = call(gather_pick_kernel, "gather_pick", args, [((owned, model), bf16)])
+        result["low", i] = low, move(low, near_z)
+
+    def gather_own(i):
+        args = result["low", 0][i], result["low", 1][i]
+        (pair,) = call(pair_kernel, "pair", args, [((2, owned, model), bf16)])
+        weights[i] = pair, move(pair, own_axis)
 
     def second_sum(i):
         send, kept = call(
@@ -700,19 +720,27 @@
             "finish",
             args,
             [((rows, model), bf16)] + [((rows, width), bf16)] * 3 + [((owned, model), f32)],
+            scratch=[
+                pltpu.VMEM((rows, model), bf16),
+                pltpu.VMEM((owned, model), f32),
+                pltpu.SemaphoreType.DMA((15,)),
+            ],
             limit=24,
             final=True,
+            out_space=pltpu.HBM,
         )
 
     forward()
     weight_grad(0)
     gather_beside()
     weight_grad(1)
-    gather_pick()
+    gather_pick(0)
+    gather_pick(1)
     second_sum(0)
+    gather_own(0)
     second_sum(1)
     z_sum(0)
-    gather_last()
+    gather_own(1)
     z_sum(1)
     attn_grad(0)
     backward(0)

time: 54.4 us -> 54.2 us (level)
  waiting for transfers between devices: 16.3 us -> 15.5 us
  starting transfers between devices: 20.2 us -> 20.9 us
    ppermute x14 -> x15, waiting for transfers between devices: 14.8 us -> 14.1 us  [move(): return lax.ppermute(array, ('dp', 'ctx'), chip_moves(rule))]
    ppermute x14 -> x15, starting transfers between devices: 16.9 us -> 17.6 us  [move(): return lax.ppermute(array, ('dp', 'ctx'), chip_moves(rule))]
    pallas_call x19 -> x21, Pallas kernels: 16.2 us -> 15.8 us  [call(): pl.pallas_call(kernel, in_specs=list(specs or [in_vmem] * len(args)) + [a...]
  transfers between devices with their start and end apart: 21 -> 22, of which waited for: 9 -> 7; matrix products, arithmetic and copies ran while one was open for 0% -> 0% of each run, Pallas kernels for 23% -> 23%
where the time goes in v5:
time: 54.2 us; the launch traced here: 54 us
  starting transfers between devices  20.9 us (39%)
  Pallas kernels  15.8 us (29%)
  waiting for transfers between devices  15.5 us (29%)
  between operations  1.01 us (2%)
  local copies, waits for them, and re-layouts  0.69 us (1%)
    ppermute x15, starting transfers between devices, move(): return lax.ppermute(array, ('dp', 'ctx'), chip_moves(rule))  17.6 us
    pallas_call x21, Pallas kernels, call(): pl.pallas_call(kernel, in_specs=list(specs or [in_vmem] * len(args)) + [a...  15.8 us
    ppermute x15, waiting for transfers between devices, move(): return lax.ppermute(array, ('dp', 'ctx'), chip_moves(rule))  14.1 us
    ppermute x7, starting transfers between devices, swap_core(): return lax.ppermute(array, 'ctx', [(0, 1), (1, 0)])  3.32 us
    ppermute x7, waiting for transfers between devices, swap_core(): return lax.ppermute(array, 'ctx', [(0, 1), (1, 0)])  1.46 us
  transfers between devices with their start and end apart: 22, of which 7 were waited for; matrix products, arithmetic and copies ran while one was open for 0% of the time, Pallas kernels for 23%

profile of v5, /device:TPU:0, one launch (start us, length us, event | category | flops | bytes accessed | tf_op | source)
XLA Modules:
  0.0 54.0 jit_solution(8009000818896848244)
XLA Ops:
  0.6 0.0 copy-start.3
  0.6 0.7 %copy-done.3 = s32[1,256]{1,0:T(1,128)S(1)} copy-done((s32[1,256]{1,0:T(1,128)S(1)}, s32[1,256]{1,0:T(1,128)}, u32[]{:S(2)}) %copy-start.3) | copy-done | bytes 1048
  1.3 1.5 %pack.1 = (bf16[3,272,512]{2,1,0:T(8,128)(2,1)S(1)}, bf16[3,256,512]{2,1,0:T(8,128)(2,1)S(1)}) custom-call(s32[1,256]{1,0:T(1,128)S(1)} %copy-done.3, bf16[256,1024]{1,0:T(8,128)(2,1)} %bitcast.13, bf16[256,1024]{1,0:T(8,128)(2,1)} %bitcast.14, bf16[256,1024]{1,0:T(8,128)(2,1)} %bitcast.15), custom_call_target="tpu_custom_call" | custom-call | flops 10000000000 | bytes 1 | tf_op jit(solution)/shard_map/pack/pallas_call | solution.py:589
  2.8 0.5 collective-permute-start
  3.4 0.1 collective-permute-start.1
  3.5 0.0 copy-done.1
  3.5 2.9 %collective-permute-start.3 = (bf16[64,2048]{1,0:T(8,128)(2,1)S(1)}, bf16[64,2048]{1,0:T(8,128)(2,1)S(1)}, u32[]{:S(2)}, u32[]{:S(2)}) collective-permute-start(bf16[64,2048]{1,0:T(8,128)(2,1)S(1)} %copy-done.1), channel_id=1, source_target_pairs={{0,4},{1,3},{2,6},{3,1},{4,0},{5,7},{6,2},{7,5},{8,12},{9,11},{10,... | collective-permute-start | bytes 786440 | tf_op jit(solution)/shard_map/ppermute | solution.py:247
  6.4 2.6 %collective-permute-start.2 = (bf16[64,2048]{1,0:T(8,128)(2,1)S(1)}, bf16[64,2048]{1,0:T(8,128)(2,1)S(1)}, u32[]{:S(2)}, u32[]{:S(2)}) collective-permute-start(bf16[64,2048]{1,0:T(8,128)(2,1)S(1)} %copy-done.1), channel_id=1, source_target_pairs={{0,16},{1,0},{2,18},{3,2},{4,20},{5,4},{6,22},{7,6},{8,24},{9,8},{... | collective-permute-start | bytes 786440 | tf_op jit(solution)/shard_map/ppermute | solution.py:247
  9.0 0.0 collective-permute-done.received
  9.0 0.0 copy-done.4
  9.0 3.1 %forward.1 = (bf16[512,512]{1,0:T(8,128)(2,1)S(1)}, bf16[512,512]{1,0:T(8,128)(2,1)S(1)}, bf16[512,512]{1,0:T(8,128)(2,1)S(1)}, bf16[512,512]{1,0:T(8,128)(2,1)S...) custom-call(s32[1,4,4]{2,1,0:T(4,128)S(1)} %copy-done.2, ...), custom_call_target="tpu_custom_call" | custom-call | flops 10000000000 | bytes 1 | tf_op jit(solution)/shard_map/forward/pallas_call | solution.py:589
  12.1 0.0 collective-permute-done.1.other
  12.1 1.3 %weight_grad.2 = (bf16[2,2,64,1024]{3,2,1,0:T(8,128)(2,1)S(1)}, bf16[2,2,64,1024]{3,2,1,0:T(8,128)(2,1)S(1)}) custom-call(bf16[512,512]{1,0:T(8,128)(2,1)S(1)} %get-tuple-element.51.attn_t, bf16[256,2048]{1,0:T(8,128)(2,1)S(1)} %bitcast.9, bf16[256,2048]{1,0:T(8,128)(2,1)S(1)} %collective-permute-done.1.other, ...), custom_call_target="tpu_custom_call" | custom-call | flops 10000000000 | bytes 1 | tf_op jit(solution)/shard_map/weight_grad/pallas_call | solution.py:589
  13.4 1.6 %collective-permute-start.5 = (bf16[2,2,64,1024]{3,2,1,0:T(8,128)(2,1)S(1)}, bf16[2,2,64,1024]{3,2,1,0:T(8,128)(2,1)S(1)}, u32[]{:S(2)}, u32[]{:S(2)}) collective-permute-start(bf16[2,2,64,1024]{3,2,1,0:T(8,128)(2,1)S(1)} %get-tuple-element.53.refs_0_), channel_id=1, source_target_pairs={{0,2},{1,5},{2,0},{3,7},{4,6},{5,1},{6,4},{7,3},{8,10},{9,13},{10,... | collective-permute-start | bytes 1572872 | tf_op jit(solution)/shard_map/ppermute | solution.py:247
  15.0 0.0 collective-permute-done.3.a.home
  15.0 0.4 collective-permute-start.4
  15.4 1.3 %weight_grad.3 = (bf16[2,2,64,1024]{3,2,1,0:T(8,128)(2,1)S(1)}, bf16[2,2,64,1024]{3,2,1,0:T(8,128)(2,1)S(1)}) custom-call(bf16[512,512]{1,0:T(8,128)(2,1)S(1)} %get-tuple-element.51.attn_t, bf16[256,2048]{1,0:T(8,128)(2,1)S(1)} %bitcast.10, bf16[256,2048]{1,0:T(8,128)(2,1)S(1)} %collective-permute-done.1.other, bf16[64,2048]{1,0:T(8,128)(2,1)S(1)} %copy.13.refs_0_), custom_call_target="tpu_custom_call" | custom-call | flops 10000000000 | bytes 1 | tf_op jit(solution)/shard_map/weight_grad/pallas_call | solution.py:589
  16.7 0.6 %collective-permute-start.7 = (bf16[2,2,64,1024]{3,2,1,0:T(8,128)(2,1)S(1)}, bf16[2,2,64,1024]{3,2,1,0:T(8,128)(2,1)S(1)}, u32[]{:S(2)}, u32[]{:S(2)}) collective-permute-start(bf16[2,2,64,1024]{3,2,1,0:T(8,128)(2,1)S(1)} %get-tuple-element.54.refs_0_), channel_id=1, source_target_pairs={{0,2},{1,5},{2,0},{3,7},{4,6},{5,1},{6,4},{7,3},{8,10},{9,13},{10,... | collective-permute-start | bytes 1572872 | tf_op jit(solution)/shard_map/ppermute | solution.py:247
  17.4 0.0 collective-permute-done.2.away
  17.4 1.6 %collective-permute-start.9 = (bf16[64,2048]{1,0:T(8,128)(2,1)S(1)}, bf16[64,2048]{1,0:T(8,128)(2,1)S(1)}, u32[]{:S(2)}, u32[]{:S(2)}) collective-permute-start(bf16[64,2048]{1,0:T(8,128)(2,1)S(1)} %gather_pick.2.refs_0_.a), channel_id=1, source_target_pairs={{0,8},{1,9},{2,10},{3,11},{4,12},{5,13},{6,14},{7,15},{8,0},{9,1},... | collective-permute-start | bytes 786440 | tf_op jit(solution)/shard_map/ppermute | solution.py:247
  19.0 0.5 %collective-permute-done.4.away = bf16[64,2048]{1,0:T(8,128)(2,1)S(1)} collective-permute-done((bf16[64,2048]{1,0:T(8,128)(2,1)S(1)}, bf16[64,2048]{1,0:T(8,128)(2,1)S(1)}, u32[]{:S(2)}, u32[]{:S(2)}) %collective-permute-start.4) | collective-permute-done | bytes 262176 | tf_op jit(solution)/shard_map/ppermute | solution.py:247
  19.6 4.1 %collective-permute-start.10 = (bf16[64,2048]{1,0:T(8,128)(2,1)S(1)}, bf16[64,2048]{1,0:T(8,128)(2,1)S(1)}, u32[]{:S(2)}, u32[]{:S(2)}) collective-permute-start(bf16[64,2048]{1,0:T(8,128)(2,1)S(1)} %gather_pick.3.refs_0_.b), channel_id=1, source_target_pairs={{0,8},{1,9},{2,10},{3,11},{4,12},{5,13},{6,14},{7,15},{8,0},{9,1},... | collective-permute-start | bytes 786440 | tf_op jit(solution)/shard_map/ppermute | solution.py:247
  23.7 0.0 collective-permute-done.5.got
  23.7 0.1 second_sum.2
  23.8 1.6 %collective-permute-start.11 = (bf16[2,64,1024]{2,1,0:T(8,128)(2,1)S(1)}, bf16[2,64,1024]{2,1,0:T(8,128)(2,1)S(1)}, u32[]{:S(2)}, u32[]{:S(2)}) collective-permute-start(bf16[2,64,1024]{2,1,0:T(8,128)(2,1)S(1)} %get-tuple-element.56.refs_0_), channel_id=1, source_target_pairs={{0,4},{1,3},{2,6},{3,1},{4,0},{5,7},{6,2},{7,5},{8,12},{9,11},{10,... | collective-permute-start | bytes 786440 | tf_op jit(solution)/shard_map/ppermute | solution.py:247
  25.4 0.6 %collective-permute-start.6 = (bf16[2,64,2048]{2,1,0:T(8,128)(2,1)S(1)}, bf16[2,64,2048]{2,1,0:T(8,128)(2,1)S(1)}, u32[]{:S(2)}, u32[]{:S(2)}) collective-permute-start(bf16[2,64,2048]{2,1,0:T(8,128)(2,1)S(1)} %pair.2.refs_0_.near), channel_id=1, source_target_pairs={{0,2},{1,5},{2,0},{3,7},{4,6},{5,1},{6,4},{7,3},{8,10},{9,13},{10,... | collective-permute-start | bytes 1572872 | tf_op jit(solution)/shard_map/ppermute | solution.py:247
  26.0 5.9 %collective-permute-done.7.got = bf16[2,2,64,1024]{3,2,1,0:T(8,128)(2,1)S(1)} collective-permute-done((bf16[2,2,64,1024]{3,2,1,0:T(8,128)(2,1)S(1)}, bf16[2,2,64,1024]{3,2,1,0:T(8,128)(2,1)S(1)}, u32[]{:S(2)}, u32[]{:S(2)}) %collective-permute-start.7) | collective-permute-done | bytes 524320 | tf_op jit(solution)/shard_map/ppermute | solution.py:247
  31.9 0.1 second_sum.3
  32.0 0.5 collective-permute-start.8
  32.5 0.6 %collective-permute-done.11.got = bf16[2,64,1024]{2,1,0:T(8,128)(2,1)S(1)} collective-permute-done((bf16[2,64,1024]{2,1,0:T(8,128)(2,1)S(1)}, bf16[2,64,1024]{2,1,0:T(8,128)(2,1)S(1)}, u32[]{:S(2)}, u32[]{:S(2)}) %collective-permute-start.11) | collective-permute-done | bytes 262176 | tf_op jit(solution)/shard_map/ppermute | solution.py:247
  33.1 0.1 z_sum.2
  33.2 0.1 collective-permute-start.13
  33.3 0.0 collective-permute-done.9.a
  33.3 0.1 collective-permute-start.14
  33.4 0.0 collective-permute-done.10.b
  33.4 1.0 %collective-permute-start.12 = (bf16[2,64,2048]{2,1,0:T(8,128)(2,1)S(1)}, bf16[2,64,2048]{2,1,0:T(8,128)(2,1)S(1)}, u32[]{:S(2)}, u32[]{:S(2)}) collective-permute-start(bf16[2,64,2048]{2,1,0:T(8,128)(2,1)S(1)} %pair.3.refs_0_.near), channel_id=1, source_target_pairs={{0,2},{1,5},{2,0},{3,7},{4,6},{5,1},{6,4},{7,3},{8,10},{9,13},{10,... | collective-permute-start | bytes 1572872 | tf_op jit(solution)/shard_map/ppermute | solution.py:247
  34.4 4.0 %collective-permute-done.8.got = bf16[2,64,1024]{2,1,0:T(8,128)(2,1)S(1)} collective-permute-done((bf16[2,64,1024]{2,1,0:T(8,128)(2,1)S(1)}, bf16[2,64,1024]{2,1,0:T(8,128)(2,1)S(1)}, u32[]{:S(2)}, u32[]{:S(2)}) %collective-permute-start.8) | collective-permute-done | bytes 262176 | tf_op jit(solution)/shard_map/ppermute | solution.py:247
  38.5 0.1 z_sum.3
  38.6 0.1 collective-permute-start.19
  38.6 0.9 %collective-permute-done.6.far = bf16[2,64,2048]{2,1,0:T(8,128)(2,1)S(1)} collective-permute-done((bf16[2,64,2048]{2,1,0:T(8,128)(2,1)S(1)}, bf16[2,64,2048]{2,1,0:T(8,128)(2,1)S(1)}, u32[]{:S(2)}, u32[]{:S(2)}) %collective-permute-start.6) | collective-permute-done | bytes 524320 | tf_op jit(solution)/shard_map/ppermute | solution.py:247
  39.5 0.0 collective-permute-start.20
  39.5 0.8 %attn_grad.2 = (bf16[256,512]{1,0:T(8,128)(2,1)S(1)}, f32[2,512]{1,0:T(2,128)S(1)}, bf16[256,2048]{1,0:T(8,128)(2,1)S(1)}) custom-call(bf16[512,512]{1,0:T(8,128)(2,1)S(1)} %get-tuple-element.51.attn_t, bf16[256,2048]{1,0:T(8,128)(2,1)S(1)} %bitcast.11, bf16[256,2048]{1,0:T(8,128)(2,1)S(1)} %collective-permute-done.1.other, ...), custom_call_target="tpu_custom_call" | custom-call | flops 10000000000 | bytes 1 | tf_op jit(solution)/shard_map/attn_grad/pallas_call | solution.py:589
  40.4 1.6 %backward.2 = (bf16[3,256,256]{2,1,0:T(8,128)(2,1)S(1)}, bf16[3,256,256]{2,1,0:T(8,128)(2,1)S(1)}) custom-call(bf16[512,512]{1,0:T(8,128)(2,1)S(1)} %get-tuple-element.52.refs_0_.rot_q, bf16[512,512]{1,0:T(8,128)(2,1)S(1)} %get-tuple-element.66.rot_k, bf16[512,512]{1,0:T(8,128)(2,1)S(1)} %get-tuple-element.67.rot_kt, ...), custom_call_target="tpu_custom_call" | custom-call | flops 10000000000 | bytes 1 | tf_op jit(solution)/shard_map/backward/pallas_call | solution.py:589
  42.0 0.0 collective-permute-done.13.first
  42.0 1.0 %collective-permute-start.16 = (bf16[3,256,256]{2,1,0:T(8,128)(2,1)S(1)}, bf16[3,256,256]{2,1,0:T(8,128)(2,1)S(1)}, u32[]{:S(2)}, u32[]{:S(2)}) collective-permute-start(bf16[3,256,256]{2,1,0:T(8,128)(2,1)S(1)} %get-tuple-element.75.refs_0_), channel_id=1, source_target_pairs={{0,1},{1,0},{2,3},{3,2},{4,5},{5,4},{6,7},{7,6},{8,9},{9,8},{10,11... | collective-permute-start | bytes 1179656 | tf_op jit(solution)/shard_map/ppermute | solution.py:251
  43.0 0.0 collective-permute-done.14.second
  43.0 0.1 share.2.refs_0_.refs_6_
  43.1 0.1 collective-permute-start.18
  43.1 2.0 %collective-permute-done.12.far = bf16[2,64,2048]{2,1,0:T(8,128)(2,1)S(1)} collective-permute-done((bf16[2,64,2048]{2,1,0:T(8,128)(2,1)S(1)}, bf16[2,64,2048]{2,1,0:T(8,128)(2,1)S(1)}, u32[]{:S(2)}, u32[]{:S(2)}) %collective-permute-start.12) | collective-permute-done | bytes 524320 | tf_op jit(solution)/shard_map/ppermute | solution.py:247
  45.2 0.8 %attn_grad.3 = (bf16[256,512]{1,0:T(8,128)(2,1)S(1)}, f32[2,512]{1,0:T(2,128)S(1)}, bf16[256,2048]{1,0:T(8,128)(2,1)S(1)}) custom-call(bf16[512,512]{1,0:T(8,128)(2,1)S(1)} %get-tuple-element.51.attn_t, bf16[256,2048]{1,0:T(8,128)(2,1)S(1)} %bitcast.12, bf16[256,2048]{1,0:T(8,128)(2,1)S(1)} %collective-permute-done.1.other, ...), custom_call_target="tpu_custom_call" | custom-call | flops 10000000000 | bytes 1 | tf_op jit(solution)/shard_map/attn_grad/pallas_call | solution.py:589
  46.0 1.3 %projection.1 = (bf16[256,2048]{1,0:T(8,128)(2,1)S(1)}, f32[256,2048]{1,0:T(8,128)S(1)}) custom-call(bf16[512,512]{1,0:T(8,128)(2,1)S(1)} %get-tuple-element.50.attn, bf16[256,2048]{1,0:T(8,128)(2,1)S(1)} %get-tuple-element.63.low, bf16[256,2048]{1,0:T(8,128)(2,1)S(1)} %get-tuple-element.76.high, bf16[256,512]{1,0:T(8,128)(2,1)S(1)} %get-tuple-element.77.refs_0_.grad_t), custom_call_target="tpu_custom_call" | custom-call | flops 10000000000 | bytes 1 | tf_op jit(solution)/shard_map/projection/pallas_call | solution.py:589
  47.2 1.0 %collective-permute-start.15 = (bf16[256,2048]{1,0:T(8,128)(2,1)S(1)}, bf16[256,2048]{1,0:T(8,128)(2,1)S(1)}, u32[]{:S(2)}, u32[]{:S(2)}) collective-permute-start(bf16[256,2048]{1,0:T(8,128)(2,1)S(1)} %get-tuple-element.79.refs_0_), channel_id=1, source_target_pairs={{0,1},{1,0},{2,3},{3,2},{4,5},{5,4},{6,7},{7,6},{8,9},{9,8},{10,11... | collective-permute-start | bytes 3145736 | tf_op jit(solution)/shard_map/ppermute | solution.py:251
  48.2 1.6 %backward.3 = (bf16[3,256,256]{2,1,0:T(8,128)(2,1)S(1)}, bf16[3,256,256]{2,1,0:T(8,128)(2,1)S(1)}) custom-call(bf16[512,512]{1,0:T(8,128)(2,1)S(1)} %get-tuple-element.52.refs_0_.rot_q, bf16[512,512]{1,0:T(8,128)(2,1)S(1)} %get-tuple-element.66.rot_k, bf16[512,512]{1,0:T(8,128)(2,1)S(1)} %get-tuple-element.67.rot_kt, ...), custom_call_target="tpu_custom_call" | custom-call | flops 10000000000 | bytes 1 | tf_op jit(solution)/shard_map/backward/pallas_call | solution.py:589
  49.8 0.0 collective-permute-done.19.first
  49.9 0.1 collective-permute-start.17
  49.9 0.0 collective-permute-done.20.second
  49.9 0.1 share.3.refs_8_
  50.0 0.6 %collective-permute-start.21 = (f32[64,1024]{1,0:T(8,128)S(1)}, f32[64,1024]{1,0:T(8,128)S(1)}, u32[]{:S(2)}, u32[]{:S(2)}) collective-permute-start(f32[64,1024]{1,0:T(8,128)S(1)} %share.3.refs_8_), channel_id=1, source_target_pairs={{0,1},{1,0},{2,3},{3,2},{4,5},{5,4},{6,7},{7,6},{8,9},{9,8},{10,11... | collective-permute-start | bytes 786440 | tf_op jit(solution)/shard_map/ppermute | solution.py:251
  50.6 0.0 collective-permute-done.18.refs_7_
  50.6 0.0 collective-permute-done.16.refs_3_
  50.6 1.4 %collective-permute-done.21.refs_9_ = f32[64,1024]{1,0:T(8,128)S(1)} collective-permute-done((f32[64,1024]{1,0:T(8,128)S(1)}, f32[64,1024]{1,0:T(8,128)S(1)}, u32[]{:S(2)}, u32[]{:S(2)}) %collective-permute-start.21) | collective-permute-done | bytes 262176 | tf_op jit(solution)/shard_map/ppermute | solution.py:251
  52.0 0.0 collective-permute-done.17.refs_5_
  52.0 0.0 collective-permute-done.15.refs_1_
  52.0 1.8 %finish.1 = (bf16[256,2048]{1,0:T(8,128)(2,1)}, bf16[256,1024]{1,0:T(8,128)(2,1)}, bf16[256,1024]{1,0:T(8,128)(2,1)}, bf16[256,1024]{1,0:T(8,128)(2,1)}, f32[64,2048]{1,0:T(8,128)}) custom-call(f32[256,2048]{1,0:T(8,128)S(1)} %get-tuple-element.78.refs_0_, bf16[256,2048]{1,0:T(8,128)(2,1)S(1)} %collective-permute-done.15.refs_1_, ...), custom_call_target="tpu_custom_call" | custom-call | flops 10000000000 | bytes 1 | tf_op jit(solution)/shard_map/finish/pallas_call | solution.py:589
  (11 shorter events, 0.1 us)
Async XLA Ops:
  0.6 0.7 %copy-start.3 = (s32[1,256]{1,0:T(1,128)S(1)}, s32[1,256]{1,0:T(1,128)}, u32[]{:S(2)}) copy-start(s32[1,256]{1,0:T(1,128)} %near.1) | copy-start | bytes 3076
  1.3 2.0 %copy-start = (bf16[1,256,2048]{2,1,0:T(8,128)(2,1)S(1)}, bf16[1,256,2048]{2,1,0:T(8,128)(2,1)}, u32[]{:S(2)}) copy-start(bf16[1,256,2048]{2,1,0:T(8,128)(2,1)} %param.13) | copy-start | bytes 3145732
  1.3 2.1 %copy-start.1 = (bf16[64,2048]{1,0:T(8,128)(2,1)S(1)}, bf16[64,2048]{1,0:T(8,128)(2,1)}, u32[]{:S(2)}) copy-start(bf16[64,2048]{1,0:T(8,128)(2,1)} %home.1) | copy-start | bytes 786436
  1.3 7.7 %copy-start.2 = (s32[1,4,4]{2,1,0:T(4,128)S(1)}, s32[1,4,4]{2,1,0:T(4,128)}, u32[]{:S(2)}) copy-start(s32[1,4,4]{2,1,0:T(4,128)} %pattern.1) | copy-start | bytes 196
  1.3 7.7 %copy-start.4 = (s32[1,256]{1,0:T(1,128)S(1)}, s32[1,256]{1,0:T(1,128)}, u32[]{:S(2)}) copy-start(s32[1,256]{1,0:T(1,128)} %near.1) | copy-start | bytes 3076
  2.8 6.1 %collective-permute-start = (bf16[3,272,512]{2,1,0:T(8,128)(2,1)S(1)}, bf16[3,272,512]{2,1,0:T(8,128)(2,1)S(1)}, u32[]{:S(2)}, u32[]{:S(2)}) collective-permute-start(bf16[3,272,512]{2,1,0:T(8,128)(2,1)S(1)} %get-tuple-element.49), channel_id=1, source_target_pairs={{0,1},{1,0},{2,3},{3,2},{4,5},{5,4},{6,7},{7,6},{8,9},{9,8},{10,11... | collective-permute-start | bytes 2506760 | tf_op jit(solution)/shard_map/ppermute | solution.py:251
  3.4 8.7 %collective-permute-start.1 = (bf16[256,2048]{1,0:T(8,128)(2,1)S(1)}, bf16[256,2048]{1,0:T(8,128)(2,1)S(1)}, u32[]{:S(2)}, u32[]{:S(2)}) collective-permute-start(bf16[256,2048]{1,0:T(8,128)(2,1)S(1)} %bitcast.8), channel_id=1, source_target_pairs={{0,1},{1,0},{2,3},{3,2},{4,5},{5,4},{6,7},{7,6},{8,9},{9,8},{10,11... | collective-permute-start | bytes 3145736 | tf_op jit(solution)/shard_map/ppermute | solution.py:251
  3.5 11.5 %collective-permute-start.3 = (bf16[64,2048]{1,0:T(8,128)(2,1)S(1)}, bf16[64,2048]{1,0:T(8,128)(2,1)S(1)}, u32[]{:S(2)}, u32[]{:S(2)}) collective-permute-start(bf16[64,2048]{1,0:T(8,128)(2,1)S(1)} %copy-done.1), channel_id=1, source_target_pairs={{0,4},{1,3},{2,6},{3,1},{4,0},{5,7},{6,2},{7,5},{8,12},{9,11},{10,... | collective-permute-start | bytes 786440 | tf_op jit(solution)/shard_map/ppermute | solution.py:247
  6.4 11.0 %collective-permute-start.2 = (bf16[64,2048]{1,0:T(8,128)(2,1)S(1)}, bf16[64,2048]{1,0:T(8,128)(2,1)S(1)}, u32[]{:S(2)}, u32[]{:S(2)}) collective-permute-start(bf16[64,2048]{1,0:T(8,128)(2,1)S(1)} %copy-done.1), channel_id=1, source_target_pairs={{0,16},{1,0},{2,18},{3,2},{4,20},{5,4},{6,22},{7,6},{8,24},{9,8},{... | collective-permute-start | bytes 786440 | tf_op jit(solution)/shard_map/ppermute | solution.py:247
  13.4 10.3 %collective-permute-start.5 = (bf16[2,2,64,1024]{3,2,1,0:T(8,128)(2,1)S(1)}, bf16[2,2,64,1024]{3,2,1,0:T(8,128)(2,1)S(1)}, u32[]{:S(2)}, u32[]{:S(2)}) collective-permute-start(bf16[2,2,64,1024]{3,2,1,0:T(8,128)(2,1)S(1)} %get-tuple-element.53.refs_0_), channel_id=1, source_target_pairs={{0,2},{1,5},{2,0},{3,7},{4,6},{5,1},{6,4},{7,3},{8,10},{9,13},{10,... | collective-permute-start | bytes 1572872 | tf_op jit(solution)/shard_map/ppermute | solution.py:247
  15.0 4.5 %collective-permute-start.4 = (bf16[64,2048]{1,0:T(8,128)(2,1)S(1)}, bf16[64,2048]{1,0:T(8,128)(2,1)S(1)}, u32[]{:S(2)}, u32[]{:S(2)}) collective-permute-start(bf16[64,2048]{1,0:T(8,128)(2,1)S(1)} %copy.13.refs_0_), channel_id=1, source_target_pairs={{0,16},{1,0},{2,18},{3,2},{4,20},{5,4},{6,22},{7,6},{8,24},{9,8},{... | collective-permute-start | bytes 786440 | tf_op jit(solution)/shard_map/ppermute | solution.py:247
  16.7 15.2 %collective-permute-start.7 = (bf16[2,2,64,1024]{3,2,1,0:T(8,128)(2,1)S(1)}, bf16[2,2,64,1024]{3,2,1,0:T(8,128)(2,1)S(1)}, u32[]{:S(2)}, u32[]{:S(2)}) collective-permute-start(bf16[2,2,64,1024]{3,2,1,0:T(8,128)(2,1)S(1)} %get-tuple-element.54.refs_0_), channel_id=1, source_target_pairs={{0,2},{1,5},{2,0},{3,7},{4,6},{5,1},{6,4},{7,3},{8,10},{9,13},{10,... | collective-permute-start | bytes 1572872 | tf_op jit(solution)/shard_map/ppermute | solution.py:247
  17.4 15.9 %collective-permute-start.9 = (bf16[64,2048]{1,0:T(8,128)(2,1)S(1)}, bf16[64,2048]{1,0:T(8,128)(2,1)S(1)}, u32[]{:S(2)}, u32[]{:S(2)}) collective-permute-start(bf16[64,2048]{1,0:T(8,128)(2,1)S(1)} %gather_pick.2.refs_0_.a), channel_id=1, source_target_pairs={{0,8},{1,9},{2,10},{3,11},{4,12},{5,13},{6,14},{7,15},{8,0},{9,1},... | collective-permute-start | bytes 786440 | tf_op jit(solution)/shard_map/ppermute | solution.py:247
  19.6 13.8 %collective-permute-start.10 = (bf16[64,2048]{1,0:T(8,128)(2,1)S(1)}, bf16[64,2048]{1,0:T(8,128)(2,1)S(1)}, u32[]{:S(2)}, u32[]{:S(2)}) collective-permute-start(bf16[64,2048]{1,0:T(8,128)(2,1)S(1)} %gather_pick.3.refs_0_.b), channel_id=1, source_target_pairs={{0,8},{1,9},{2,10},{3,11},{4,12},{5,13},{6,14},{7,15},{8,0},{9,1},... | collective-permute-start | bytes 786440 | tf_op jit(solution)/shard_map/ppermute | solution.py:247
  23.8 9.3 %collective-permute-start.11 = (bf16[2,64,1024]{2,1,0:T(8,128)(2,1)S(1)}, bf16[2,64,1024]{2,1,0:T(8,128)(2,1)S(1)}, u32[]{:S(2)}, u32[]{:S(2)}) collective-permute-start(bf16[2,64,1024]{2,1,0:T(8,128)(2,1)S(1)} %get-tuple-element.56.refs_0_), channel_id=1, source_target_pairs={{0,4},{1,3},{2,6},{3,1},{4,0},{5,7},{6,2},{7,5},{8,12},{9,11},{10,... | collective-permute-start | bytes 786440 | tf_op jit(solution)/shard_map/ppermute | solution.py:247
  25.4 14.1 %collective-permute-start.6 = (bf16[2,64,2048]{2,1,0:T(8,128)(2,1)S(1)}, bf16[2,64,2048]{2,1,0:T(8,128)(2,1)S(1)}, u32[]{:S(2)}, u32[]{:S(2)}) collective-permute-start(bf16[2,64,2048]{2,1,0:T(8,128)(2,1)S(1)} %pair.2.refs_0_.near), channel_id=1, source_target_pairs={{0,2},{1,5},{2,0},{3,7},{4,6},{5,1},{6,4},{7,3},{8,10},{9,13},{10,... | collective-permute-start | bytes 1572872 | tf_op jit(solution)/shard_map/ppermute | solution.py:247
  32.0 6.4 %collective-permute-start.8 = (bf16[2,64,1024]{2,1,0:T(8,128)(2,1)S(1)}, bf16[2,64,1024]{2,1,0:T(8,128)(2,1)S(1)}, u32[]{:S(2)}, u32[]{:S(2)}) collective-permute-start(bf16[2,64,1024]{2,1,0:T(8,128)(2,1)S(1)} %get-tuple-element.59.refs_0_), channel_id=1, source_target_pairs={{0,4},{1,3},{2,6},{3,1},{4,0},{5,7},{6,2},{7,5},{8,12},{9,11},{10,... | collective-permute-start | bytes 786440 | tf_op jit(solution)/shard_map/ppermute | solution.py:247
  33.2 8.8 %collective-permute-start.13 = (bf16[64,1024]{1,0:T(8,128)(2,1)S(1)}, bf16[64,1024]{1,0:T(8,128)(2,1)S(1)}, u32[]{:S(2)}, u32[]{:S(2)}) collective-permute-start(bf16[64,1024]{1,0:T(8,128)(2,1)S(1)} %get-tuple-element.61.refs_0_), channel_id=1, source_target_pairs={{0,9},{1,17},{2,11},{3,19},{4,13},{5,21},{6,15},{7,23},{8,1},{9,25... | collective-permute-start | bytes 393224 | tf_op jit(solution)/shard_map/ppermute | solution.py:247
  33.3 9.7 %collective-permute-start.14 = (bf16[64,1024]{1,0:T(8,128)(2,1)S(1)}, bf16[64,1024]{1,0:T(8,128)(2,1)S(1)}, u32[]{:S(2)}, u32[]{:S(2)}) collective-permute-start(bf16[64,1024]{1,0:T(8,128)(2,1)S(1)} %get-tuple-element.65), channel_id=1, source_target_pairs={{0,1},{1,25},{2,3},{3,27},{4,5},{5,29},{6,7},{7,31},{8,9},{9,17},{... | collective-permute-start | bytes 393224 | tf_op jit(solution)/shard_map/ppermute | solution.py:247
  33.4 11.7 %collective-permute-start.12 = (bf16[2,64,2048]{2,1,0:T(8,128)(2,1)S(1)}, bf16[2,64,2048]{2,1,0:T(8,128)(2,1)S(1)}, u32[]{:S(2)}, u32[]{:S(2)}) collective-permute-start(bf16[2,64,2048]{2,1,0:T(8,128)(2,1)S(1)} %pair.3.refs_0_.near), channel_id=1, source_target_pairs={{0,2},{1,5},{2,0},{3,7},{4,6},{5,1},{6,4},{7,3},{8,10},{9,13},{10,... | collective-permute-start | bytes 1572872 | tf_op jit(solution)/shard_map/ppermute | solution.py:247
  38.6 11.3 %collective-permute-start.19 = (bf16[64,1024]{1,0:T(8,128)(2,1)S(1)}, bf16[64,1024]{1,0:T(8,128)(2,1)S(1)}, u32[]{:S(2)}, u32[]{:S(2)}) collective-permute-start(bf16[64,1024]{1,0:T(8,128)(2,1)S(1)} %get-tuple-element.62.refs_0_), channel_id=1, source_target_pairs={{0,9},{1,17},{2,11},{3,19},{4,13},{5,21},{6,15},{7,23},{8,1},{9,25... | collective-permute-start | bytes 393224 | tf_op jit(solution)/shard_map/ppermute | solution.py:247
  39.5 10.4 %collective-permute-start.20 = (bf16[64,1024]{1,0:T(8,128)(2,1)S(1)}, bf16[64,1024]{1,0:T(8,128)(2,1)S(1)}, u32[]{:S(2)}, u32[]{:S(2)}) collective-permute-start(bf16[64,1024]{1,0:T(8,128)(2,1)S(1)} %get-tuple-element.85), channel_id=1, source_target_pairs={{0,1},{1,25},{2,3},{3,27},{4,5},{5,29},{6,7},{7,31},{8,9},{9,17},{... | collective-permute-start | bytes 393224 | tf_op jit(solution)/shard_map/ppermute | solution.py:247
  42.0 8.6 %collective-permute-start.16 = (bf16[3,256,256]{2,1,0:T(8,128)(2,1)S(1)}, bf16[3,256,256]{2,1,0:T(8,128)(2,1)S(1)}, u32[]{:S(2)}, u32[]{:S(2)}) collective-permute-start(bf16[3,256,256]{2,1,0:T(8,128)(2,1)S(1)} %get-tuple-element.75.refs_0_), channel_id=1, source_target_pairs={{0,1},{1,0},{2,3},{3,2},{4,5},{5,4},{6,7},{7,6},{8,9},{9,8},{10,11... | collective-permute-start | bytes 1179656 | tf_op jit(solution)/shard_map/ppermute | solution.py:251
  43.1 7.5 %collective-permute-start.18 = (f32[64,1024]{1,0:T(8,128)S(1)}, f32[64,1024]{1,0:T(8,128)S(1)}, u32[]{:S(2)}, u32[]{:S(2)}) collective-permute-start(f32[64,1024]{1,0:T(8,128)S(1)} %share.2.refs_0_.refs_6_), channel_id=1, source_target_pairs={{0,1},{1,0},{2,3},{3,2},{4,5},{5,4},{6,7},{7,6},{8,9},{9,8},{10,11... | collective-permute-start | bytes 786440 | tf_op jit(solution)/shard_map/ppermute | solution.py:251
  47.2 4.8 %collective-permute-start.15 = (bf16[256,2048]{1,0:T(8,128)(2,1)S(1)}, bf16[256,2048]{1,0:T(8,128)(2,1)S(1)}, u32[]{:S(2)}, u32[]{:S(2)}) collective-permute-start(bf16[256,2048]{1,0:T(8,128)(2,1)S(1)} %get-tuple-element.79.refs_0_), channel_id=1, source_target_pairs={{0,1},{1,0},{2,3},{3,2},{4,5},{5,4},{6,7},{7,6},{8,9},{9,8},{10,11... | collective-permute-start | bytes 3145736 | tf_op jit(solution)/shard_map/ppermute | solution.py:251
  49.9 2.2 %collective-permute-start.17 = (bf16[3,256,256]{2,1,0:T(8,128)(2,1)S(1)}, bf16[3,256,256]{2,1,0:T(8,128)(2,1)S(1)}, u32[]{:S(2)}, u32[]{:S(2)}) collective-permute-start(bf16[3,256,256]{2,1,0:T(8,128)(2,1)S(1)} %get-tuple-element.83.refs_0_), channel_id=1, source_target_pairs={{0,1},{1,0},{2,3},{3,2},{4,5},{5,4},{6,7},{7,6},{8,9},{9,8},{10,11... | collective-permute-start | bytes 1179656 | tf_op jit(solution)/shard_map/ppermute | solution.py:251
  50.0 2.0 %collective-permute-start.21 = (f32[64,1024]{1,0:T(8,128)S(1)}, f32[64,1024]{1,0:T(8,128)S(1)}, u32[]{:S(2)}, u32[]{:S(2)}) collective-permute-start(f32[64,1024]{1,0:T(8,128)S(1)} %share.3.refs_8_), channel_id=1, source_target_pairs={{0,1},{1,0},{2,3},{3,2},{4,5},{5,4},{6,7},{7,6},{8,9},{9,8},{10,11... | collective-permute-start | bytes 786440 | tf_op jit(solution)/shard_map/ppermute | solution.py:251

commit v6 on v5

--- a/solution.py
+++ b/solution.py
@@ -407,9 +407,9 @@
     piece, width = send.shape[2:]
     cols = slice(chunk * width, (chunk + 1) * width)
     tokens = jnp.concatenate([own[:, cols], other[:, cols]], axis=0)
+    whole = dot_nn(attn_t[...], tokens).astype(send.dtype)
     for block in range(attn_t.shape[0] // (2 * piece)):
-        rows = slice(block * 2 * piece, (block + 1) * 2 * piece)
-        part = dot_nn(attn_t[rows, :], tokens).astype(send.dtype)
+        part = whole[block * 2 * piece : (block + 1) * 2 * piece, :]
         z_rel = block // 2
         for head_x in range(2):
             out = part[head_x * piece : (head_x + 1) * piece, :]
@@ -491,22 +491,19 @@
             send[i, :, out_cols] = out[half:, :]
 
 
-def gather_pick_kernel(home, away, *refs):
+def gather_pick_kernel(home0, home1, away0, away1, *refs):
     core, z, _, _ = place()
     low = refs[-1]
 
     @pl.when(z // 2 == core)
     def _():
-        low[...] = home[...]
+        low[0] = home0[...]
+        low[1] = home1[...]
 
     @pl.when(z // 2 != core)
     def _():
-        low[...] = away[...]
-
-
-def pair_kernel(a, b, *refs):
-    refs[-1][0] = a[...]
-    refs[-1][1] = b[...]
+        low[0] = away0[...]
+        low[1] = away1[...]
 
 
 def copy_kernel(a, *refs):
@@ -652,15 +649,15 @@
         (copied,) = call(copy_kernel, "copy", (beside,), [((owned, model), bf16)])
         result["beside"] = move(copied, at_home(far_z))
 
-    def gather_pick(i):
-        args = ((out_weight, beyond), (beside, result["beside"]))[i]
-        (low,) = call(gather_pick_kernel, "gather_pick", args, [((owned, model), bf16)])
-        result["low", i] = low, move(low, near_z)
-
-    def gather_own(i):
-        args = result["low", 0][i], result["low", 1][i]
-        (pair,) = call(pair_kernel, "pair", args, [((2, owned, model), bf16)])
-        weights[i] = pair, move(pair, own_axis)
+    def gather_pick():
+        args = (out_weight, beside, beyond, result["beside"])
+        (low,) = call(gather_pick_kernel, "gather_pick", args, [((2, owned, model), bf16)])
+        result["high"] = move(low, near_z)
+        weights[0] = low, move(low, own_axis)
+
+    def gather_last():
+        (high,) = call(copy_kernel, "copy", (result["high"],), [((2, owned, model), bf16)])
+        weights[1] = high, move(high, own_axis)
 
     def second_sum(i):
         send, kept = call(
@@ -734,13 +731,11 @@
     weight_grad(0)
     gather_beside()
     weight_grad(1)
-    gather_pick(0)
-    gather_pick(1)
+    gather_pick()
     second_sum(0)
-    gather_own(0)
     second_sum(1)
     z_sum(0)
-    gather_own(1)
+    gather_last()
     z_sum(1)
     attn_grad(0)
     backward(0)

time: 54.2 us -> 53.5 us (0.987)
  Pallas kernels: 15.8 us -> 14.9 us
  waiting for transfers between devices: 15.5 us -> 16.2 us
    pallas_call x21 -> x19, Pallas kernels: 15.8 us -> 14.9 us  [call(): pl.pallas_call(kernel, in_specs=list(specs or [in_vmem] * len(args)) + [a...]
    ppermute x15 -> x14, waiting for transfers between devices: 14.1 us -> 14.8 us  [move(): return lax.ppermute(array, ('dp', 'ctx'), chip_moves(rule))]
    ppermute x15 -> x14, starting transfers between devices: 17.6 us -> 17.5 us  [move(): return lax.ppermute(array, ('dp', 'ctx'), chip_moves(rule))]
  transfers between devices with their start and end apart: 22 -> 21, of which waited for: 7 -> 9; matrix products, arithmetic and copies ran while one was open for 0% -> 0% of each run, Pallas kernels for 23% -> 22%
where the time goes in v6:
time: 53.5 us; the launch traced here: 53.4 us
  starting transfers between devices  20.8 us (39%)
  waiting for transfers between devices  16.2 us (30%)
  Pallas kernels  14.9 us (28%)
  between operations  0.82 us (2%)
  local copies, waits for them, and re-layouts  0.69 us (1%)
    ppermute x14, starting transfers between devices, move(): return lax.ppermute(array, ('dp', 'ctx'), chip_moves(rule))  17.5 us
    pallas_call x19, Pallas kernels, call(): pl.pallas_call(kernel, in_specs=list(specs or [in_vmem] * len(args)) + [a...  14.9 us
    ppermute x14, waiting for transfers between devices, move(): return lax.ppermute(array, ('dp', 'ctx'), chip_moves(rule))  14.8 us
    ppermute x7, starting transfers between devices, swap_core(): return lax.ppermute(array, 'ctx', [(0, 1), (1, 0)])  3.3 us
    ppermute x7, waiting for transfers between devices, swap_core(): return lax.ppermute(array, 'ctx', [(0, 1), (1, 0)])  1.46 us
  transfers between devices with their start and end apart: 21, of which 9 were waited for; matrix products, arithmetic and copies ran while one was open for 0% of the time, Pallas kernels for 22%

profile of v6, /device:TPU:0, one launch (start us, length us, event | category | flops | bytes accessed | tf_op | source)
XLA Modules:
  0.0 53.4 jit_solution(3901149306740777855)
XLA Ops:
  0.6 0.0 copy-start.3
  0.6 0.7 %copy-done.3 = s32[1,256]{1,0:T(1,128)S(1)} copy-done((s32[1,256]{1,0:T(1,128)S(1)}, s32[1,256]{1,0:T(1,128)}, u32[]{:S(2)}) %copy-start.3) | copy-done | bytes 1048
  1.3 1.5 %pack.1 = (bf16[3,272,512]{2,1,0:T(8,128)(2,1)S(1)}, bf16[3,256,512]{2,1,0:T(8,128)(2,1)S(1)}) custom-call(s32[1,256]{1,0:T(1,128)S(1)} %copy-done.3, bf16[256,1024]{1,0:T(8,128)(2,1)} %bitcast.13, bf16[256,1024]{1,0:T(8,128)(2,1)} %bitcast.14, bf16[256,1024]{1,0:T(8,128)(2,1)} %bitcast.15), custom_call_target="tpu_custom_call" | custom-call | flops 10000000000 | bytes 1 | tf_op jit(solution)/shard_map/pack/pallas_call | solution.py:586
  2.8 0.5 collective-permute-start
  3.4 0.0 copy-done
  3.4 0.1 collective-permute-start.1
  3.5 0.0 copy-done.1
  3.5 2.9 %collective-permute-start.2 = (bf16[64,2048]{1,0:T(8,128)(2,1)S(1)}, bf16[64,2048]{1,0:T(8,128)(2,1)S(1)}, u32[]{:S(2)}, u32[]{:S(2)}) collective-permute-start(bf16[64,2048]{1,0:T(8,128)(2,1)S(1)} %copy-done.1), channel_id=1, source_target_pairs={{0,4},{1,3},{2,6},{3,1},{4,0},{5,7},{6,2},{7,5},{8,12},{9,11},{10,... | collective-permute-start | bytes 786440 | tf_op jit(solution)/shard_map/ppermute | solution.py:247
  6.4 2.6 %collective-permute-start.3 = (bf16[64,2048]{1,0:T(8,128)(2,1)S(1)}, bf16[64,2048]{1,0:T(8,128)(2,1)S(1)}, u32[]{:S(2)}, u32[]{:S(2)}) collective-permute-start(bf16[64,2048]{1,0:T(8,128)(2,1)S(1)} %copy-done.1), channel_id=1, source_target_pairs={{0,16},{1,0},{2,18},{3,2},{4,20},{5,4},{6,22},{7,6},{8,24},{9,8},{... | collective-permute-start | bytes 786440 | tf_op jit(solution)/shard_map/ppermute | solution.py:247
  9.0 0.0 collective-permute-done.received
  9.0 0.0 copy-done.2
  9.0 0.0 copy-done.4
  9.0 3.1 %forward.1 = (bf16[512,512]{1,0:T(8,128)(2,1)S(1)}, bf16[512,512]{1,0:T(8,128)(2,1)S(1)}, bf16[512,512]{1,0:T(8,128)(2,1)S(1)}, bf16[512,512]{1,0:T(8,128)(2,1)S...) custom-call(s32[1,4,4]{2,1,0:T(4,128)S(1)} %copy-done.2, ...), custom_call_target="tpu_custom_call" | custom-call | flops 10000000000 | bytes 1 | tf_op jit(solution)/shard_map/forward/pallas_call | solution.py:586
  12.1 0.0 collective-permute-done.1.other
  12.1 0.9 %weight_grad.2 = (bf16[2,2,64,1024]{3,2,1,0:T(8,128)(2,1)S(1)}, bf16[2,2,64,1024]{3,2,1,0:T(8,128)(2,1)S(1)}) custom-call(bf16[512,512]{1,0:T(8,128)(2,1)S(1)} %get-tuple-element.51.attn_t, bf16[256,2048]{1,0:T(8,128)(2,1)S(1)} %bitcast.9, bf16[256,2048]{1,0:T(8,128)(2,1)S(1)} %collective-permute-done.1.other, ...), custom_call_target="tpu_custom_call" | custom-call | flops 10000000000 | bytes 1 | tf_op jit(solution)/shard_map/weight_grad/pallas_call | solution.py:586
  13.0 1.6 %collective-permute-start.7 = (bf16[2,2,64,1024]{3,2,1,0:T(8,128)(2,1)S(1)}, bf16[2,2,64,1024]{3,2,1,0:T(8,128)(2,1)S(1)}, u32[]{:S(2)}, u32[]{:S(2)}) collective-permute-start(bf16[2,2,64,1024]{3,2,1,0:T(8,128)(2,1)S(1)} %get-tuple-element.53.refs_0_), channel_id=1, source_target_pairs={{0,2},{1,5},{2,0},{3,7},{4,6},{5,1},{6,4},{7,3},{8,10},{9,13},{10,... | collective-permute-start | bytes 1572872 | tf_op jit(solution)/shard_map/ppermute | solution.py:247
  14.5 0.0 collective-permute-done.2.a.home1
  14.5 0.4 collective-permute-start.4
  14.9 0.9 %weight_grad.3 = (bf16[2,2,64,1024]{3,2,1,0:T(8,128)(2,1)S(1)}, bf16[2,2,64,1024]{3,2,1,0:T(8,128)(2,1)S(1)}) custom-call(bf16[512,512]{1,0:T(8,128)(2,1)S(1)} %get-tuple-element.51.attn_t, bf16[256,2048]{1,0:T(8,128)(2,1)S(1)} %bitcast.10, bf16[256,2048]{1,0:T(8,128)(2,1)S(1)} %collective-permute-done.1.other, bf16[64,2048]{1,0:T(8,128)(2,1)S(1)} %copy.14.refs_0_), custom_call_target="tpu_custom_call" | custom-call | flops 10000000000 | bytes 1 | tf_op jit(solution)/shard_map/weight_grad/pallas_call | solution.py:586
  15.8 0.6 %collective-permute-start.6 = (bf16[2,2,64,1024]{3,2,1,0:T(8,128)(2,1)S(1)}, bf16[2,2,64,1024]{3,2,1,0:T(8,128)(2,1)S(1)}, u32[]{:S(2)}, u32[]{:S(2)}) collective-permute-start(bf16[2,2,64,1024]{3,2,1,0:T(8,128)(2,1)S(1)} %get-tuple-element.54.refs_0_), channel_id=1, source_target_pairs={{0,2},{1,5},{2,0},{3,7},{4,6},{5,1},{6,4},{7,3},{8,10},{9,13},{10,... | collective-permute-start | bytes 1572872 | tf_op jit(solution)/shard_map/ppermute | solution.py:247
  16.4 0.0 collective-permute-done.3.away0
  16.4 2.5 %collective-permute-done.4.away1 = bf16[64,2048]{1,0:T(8,128)(2,1)S(1)} collective-permute-done((bf16[64,2048]{1,0:T(8,128)(2,1)S(1)}, bf16[64,2048]{1,0:T(8,128)(2,1)S(1)}, u32[]{:S(2)}, u32[]{:S(2)}) %collective-permute-start.4) | collective-permute-done | bytes 262176 | tf_op jit(solution)/shard_map/ppermute | solution.py:247
  18.9 4.3 %collective-permute-start.9 = (bf16[2,64,2048]{2,1,0:T(8,128)(2,1)S(1)}, bf16[2,64,2048]{2,1,0:T(8,128)(2,1)S(1)}, u32[]{:S(2)}, u32[]{:S(2)}) collective-permute-start(bf16[2,64,2048]{2,1,0:T(8,128)(2,1)S(1)} %gather_pick.1.refs_0_.near), channel_id=1, source_target_pairs={{0,8},{1,9},{2,10},{3,11},{4,12},{5,13},{6,14},{7,15},{8,0},{9,1},... | collective-permute-start | bytes 1572872 | tf_op jit(solution)/shard_map/ppermute | solution.py:247
  23.2 1.2 %collective-permute-start.5 = (bf16[2,64,2048]{2,1,0:T(8,128)(2,1)S(1)}, bf16[2,64,2048]{2,1,0:T(8,128)(2,1)S(1)}, u32[]{:S(2)}, u32[]{:S(2)}) collective-permute-start(bf16[2,64,2048]{2,1,0:T(8,128)(2,1)S(1)} %gather_pick.1.refs_0_.near), channel_id=1, source_target_pairs={{0,2},{1,5},{2,0},{3,7},{4,6},{5,1},{6,4},{7,3},{8,10},{9,13},{10,... | collective-permute-start | bytes 1572872 | tf_op jit(solution)/shard_map/ppermute | solution.py:247
  24.4 0.0 collective-permute-done.7.got
  24.4 0.1 second_sum.2
  24.5 0.9 %collective-permute-start.10 = (bf16[2,64,1024]{2,1,0:T(8,128)(2,1)S(1)}, bf16[2,64,1024]{2,1,0:T(8,128)(2,1)S(1)}, u32[]{:S(2)}, u32[]{:S(2)}) collective-permute-start(bf16[2,64,1024]{2,1,0:T(8,128)(2,1)S(1)} %get-tuple-element.57.refs_0_), channel_id=1, source_target_pairs={{0,4},{1,3},{2,6},{3,1},{4,0},{5,7},{6,2},{7,5},{8,12},{9,11},{10,... | collective-permute-start | bytes 786440 | tf_op jit(solution)/shard_map/ppermute | solution.py:247
  25.5 5.1 %collective-permute-done.6.got = bf16[2,2,64,1024]{3,2,1,0:T(8,128)(2,1)S(1)} collective-permute-done((bf16[2,2,64,1024]{3,2,1,0:T(8,128)(2,1)S(1)}, bf16[2,2,64,1024]{3,2,1,0:T(8,128)(2,1)S(1)}, u32[]{:S(2)}, u32[]{:S(2)}) %collective-permute-start.6) | collective-permute-done | bytes 524320 | tf_op jit(solution)/shard_map/ppermute | solution.py:247
  30.6 0.1 second_sum.3
  30.7 0.2 collective-permute-start.8
  30.9 2.3 %collective-permute-done.10.got = bf16[2,64,1024]{2,1,0:T(8,128)(2,1)S(1)} collective-permute-done((bf16[2,64,1024]{2,1,0:T(8,128)(2,1)S(1)}, bf16[2,64,1024]{2,1,0:T(8,128)(2,1)S(1)}, u32[]{:S(2)}, u32[]{:S(2)}) %collective-permute-start.10) | collective-permute-done | bytes 262176 | tf_op jit(solution)/shard_map/ppermute | solution.py:247
  33.2 0.1 z_sum.2
  33.3 0.1 collective-permute-start.12
  33.4 0.1 collective-permute-start.13
  33.4 1.6 %collective-permute-done.9.a = bf16[2,64,2048]{2,1,0:T(8,128)(2,1)S(1)} collective-permute-done((bf16[2,64,2048]{2,1,0:T(8,128)(2,1)S(1)}, bf16[2,64,2048]{2,1,0:T(8,128)(2,1)S(1)}, u32[]{:S(2)}, u32[]{:S(2)}) %collective-permute-start.9) | collective-permute-done | bytes 524320 | tf_op jit(solution)/shard_map/ppermute | solution.py:247
  35.1 1.6 %collective-permute-start.11 = (bf16[2,64,2048]{2,1,0:T(8,128)(2,1)S(1)}, bf16[2,64,2048]{2,1,0:T(8,128)(2,1)S(1)}, u32[]{:S(2)}, u32[]{:S(2)}) collective-permute-start(bf16[2,64,2048]{2,1,0:T(8,128)(2,1)S(1)} %copy.15.refs_0_.near), channel_id=1, source_target_pairs={{0,2},{1,5},{2,0},{3,7},{4,6},{5,1},{6,4},{7,3},{8,10},{9,13},{10,... | collective-permute-start | bytes 1572872 | tf_op jit(solution)/shard_map/ppermute | solution.py:247
  36.7 0.5 collective-permute-done.8.got
  37.2 0.1 z_sum.3
  37.3 1.1 %collective-permute-start.18 = (bf16[64,1024]{1,0:T(8,128)(2,1)S(1)}, bf16[64,1024]{1,0:T(8,128)(2,1)S(1)}, u32[]{:S(2)}, u32[]{:S(2)}) collective-permute-start(bf16[64,1024]{1,0:T(8,128)(2,1)S(1)} %get-tuple-element.62.refs_0_), channel_id=1, source_target_pairs={{0,9},{1,17},{2,11},{3,19},{4,13},{5,21},{6,15},{7,23},{8,1},{9,25... | collective-permute-start | bytes 393224 | tf_op jit(solution)/shard_map/ppermute | solution.py:247
  38.4 0.7 %collective-permute-done.5.far = bf16[2,64,2048]{2,1,0:T(8,128)(2,1)S(1)} collective-permute-done((bf16[2,64,2048]{2,1,0:T(8,128)(2,1)S(1)}, bf16[2,64,2048]{2,1,0:T(8,128)(2,1)S(1)}, u32[]{:S(2)}, u32[]{:S(2)}) %collective-permute-start.5) | collective-permute-done | bytes 524320 | tf_op jit(solution)/shard_map/ppermute | solution.py:247
  39.1 0.0 collective-permute-start.19
  39.1 0.8 %attn_grad.2 = (bf16[256,512]{1,0:T(8,128)(2,1)S(1)}, f32[2,512]{1,0:T(2,128)S(1)}, bf16[256,2048]{1,0:T(8,128)(2,1)S(1)}) custom-call(bf16[512,512]{1,0:T(8,128)(2,1)S(1)} %get-tuple-element.51.attn_t, bf16[256,2048]{1,0:T(8,128)(2,1)S(1)} %bitcast.11, bf16[256,2048]{1,0:T(8,128)(2,1)S(1)} %collective-permute-done.1.other, ...), custom_call_target="tpu_custom_call" | custom-call | flops 10000000000 | bytes 1 | tf_op jit(solution)/shard_map/attn_grad/pallas_call | solution.py:586
  39.9 1.6 %backward.2 = (bf16[3,256,256]{2,1,0:T(8,128)(2,1)S(1)}, bf16[3,256,256]{2,1,0:T(8,128)(2,1)S(1)}) custom-call(bf16[512,512]{1,0:T(8,128)(2,1)S(1)} %get-tuple-element.52.refs_0_.rot_q, bf16[512,512]{1,0:T(8,128)(2,1)S(1)} %get-tuple-element.66.rot_k, bf16[512,512]{1,0:T(8,128)(2,1)S(1)} %get-tuple-element.67.rot_kt, ...), custom_call_target="tpu_custom_call" | custom-call | flops 10000000000 | bytes 1 | tf_op jit(solution)/shard_map/backward/pallas_call | solution.py:586
  41.5 0.0 collective-permute-done.12.first
  41.5 1.0 %collective-permute-start.15 = (bf16[3,256,256]{2,1,0:T(8,128)(2,1)S(1)}, bf16[3,256,256]{2,1,0:T(8,128)(2,1)S(1)}, u32[]{:S(2)}, u32[]{:S(2)}) collective-permute-start(bf16[3,256,256]{2,1,0:T(8,128)(2,1)S(1)} %get-tuple-element.75.refs_0_), channel_id=1, source_target_pairs={{0,1},{1,0},{2,3},{3,2},{4,5},{5,4},{6,7},{7,6},{8,9},{9,8},{10,11... | collective-permute-start | bytes 1179656 | tf_op jit(solution)/shard_map/ppermute | solution.py:251
  42.5 1.5 %collective-permute-done.13.second = bf16[64,1024]{1,0:T(8,128)(2,1)S(1)} collective-permute-done((bf16[64,1024]{1,0:T(8,128)(2,1)S(1)}, bf16[64,1024]{1,0:T(8,128)(2,1)S(1)}, u32[]{:S(2)}, u32[]{:S(2)}) %collective-permute-start.13) | collective-permute-done | bytes 131104 | tf_op jit(solution)/shard_map/ppermute | solution.py:247
  44.0 0.1 share.2.refs_0_.refs_6_
  44.0 0.1 collective-permute-start.17
  44.1 0.6 %collective-permute-done.11.far = bf16[2,64,2048]{2,1,0:T(8,128)(2,1)S(1)} collective-permute-done((bf16[2,64,2048]{2,1,0:T(8,128)(2,1)S(1)}, bf16[2,64,2048]{2,1,0:T(8,128)(2,1)S(1)}, u32[]{:S(2)}, u32[]{:S(2)}) %collective-permute-start.11) | collective-permute-done | bytes 524320 | tf_op jit(solution)/shard_map/ppermute | solution.py:247
  44.7 0.8 %attn_grad.3 = (bf16[256,512]{1,0:T(8,128)(2,1)S(1)}, f32[2,512]{1,0:T(2,128)S(1)}, bf16[256,2048]{1,0:T(8,128)(2,1)S(1)}) custom-call(bf16[512,512]{1,0:T(8,128)(2,1)S(1)} %get-tuple-element.51.attn_t, bf16[256,2048]{1,0:T(8,128)(2,1)S(1)} %bitcast.12, bf16[256,2048]{1,0:T(8,128)(2,1)S(1)} %collective-permute-done.1.other, ...), custom_call_target="tpu_custom_call" | custom-call | flops 10000000000 | bytes 1 | tf_op jit(solution)/shard_map/attn_grad/pallas_call | solution.py:586
  45.5 1.3 %projection.1 = (bf16[256,2048]{1,0:T(8,128)(2,1)S(1)}, f32[256,2048]{1,0:T(8,128)S(1)}) custom-call(bf16[512,512]{1,0:T(8,128)(2,1)S(1)} %get-tuple-element.50.attn, bf16[256,2048]{1,0:T(8,128)(2,1)S(1)} %get-tuple-element.63.low, bf16[256,2048]{1,0:T(8,128)(2,1)S(1)} %get-tuple-element.76.high, bf16[256,512]{1,0:T(8,128)(2,1)S(1)} %get-tuple-element.77.refs_0_.grad_t), custom_call_target="tpu_custom_call" | custom-call | flops 10000000000 | bytes 1 | tf_op jit(solution)/shard_map/projection/pallas_call | solution.py:586
  46.8 1.0 %collective-permute-start.14 = (bf16[256,2048]{1,0:T(8,128)(2,1)S(1)}, bf16[256,2048]{1,0:T(8,128)(2,1)S(1)}, u32[]{:S(2)}, u32[]{:S(2)}) collective-permute-start(bf16[256,2048]{1,0:T(8,128)(2,1)S(1)} %get-tuple-element.79.refs_0_), channel_id=1, source_target_pairs={{0,1},{1,0},{2,3},{3,2},{4,5},{5,4},{6,7},{7,6},{8,9},{9,8},{10,11... | collective-permute-start | bytes 3145736 | tf_op jit(solution)/shard_map/ppermute | solution.py:251
  47.8 1.6 %backward.3 = (bf16[3,256,256]{2,1,0:T(8,128)(2,1)S(1)}, bf16[3,256,256]{2,1,0:T(8,128)(2,1)S(1)}) custom-call(bf16[512,512]{1,0:T(8,128)(2,1)S(1)} %get-tuple-element.52.refs_0_.rot_q, bf16[512,512]{1,0:T(8,128)(2,1)S(1)} %get-tuple-element.66.rot_k, bf16[512,512]{1,0:T(8,128)(2,1)S(1)} %get-tuple-element.67.rot_kt, ...), custom_call_target="tpu_custom_call" | custom-call | flops 10000000000 | bytes 1 | tf_op jit(solution)/shard_map/backward/pallas_call | solution.py:586
  49.4 0.0 collective-permute-done.18.first
  49.4 0.1 collective-permute-start.16
  49.5 0.0 collective-permute-done.19.second
  49.5 0.1 share.3.refs_8_
  49.5 0.6 %collective-permute-start.20 = (f32[64,1024]{1,0:T(8,128)S(1)}, f32[64,1024]{1,0:T(8,128)S(1)}, u32[]{:S(2)}, u32[]{:S(2)}) collective-permute-start(f32[64,1024]{1,0:T(8,128)S(1)} %share.3.refs_8_), channel_id=1, source_target_pairs={{0,1},{1,0},{2,3},{3,2},{4,5},{5,4},{6,7},{7,6},{8,9},{9,8},{10,11... | collective-permute-start | bytes 786440 | tf_op jit(solution)/shard_map/ppermute | solution.py:251
  50.1 0.0 collective-permute-done.17.refs_7_
  50.1 0.0 collective-permute-done.15.refs_3_
  50.1 1.4 %collective-permute-done.20.refs_9_ = f32[64,1024]{1,0:T(8,128)S(1)} collective-permute-done((f32[64,1024]{1,0:T(8,128)S(1)}, f32[64,1024]{1,0:T(8,128)S(1)}, u32[]{:S(2)}, u32[]{:S(2)}) %collective-permute-start.20) | collective-permute-done | bytes 262176 | tf_op jit(solution)/shard_map/ppermute | solution.py:251
  51.5 0.0 collective-permute-done.16.refs_5_
  51.5 0.0 collective-permute-done.14.refs_1_
  51.5 1.8 %finish.1 = (bf16[256,2048]{1,0:T(8,128)(2,1)}, bf16[256,1024]{1,0:T(8,128)(2,1)}, bf16[256,1024]{1,0:T(8,128)(2,1)}, bf16[256,1024]{1,0:T(8,128)(2,1)}, f32[64,2048]{1,0:T(8,128)}) custom-call(f32[256,2048]{1,0:T(8,128)S(1)} %get-tuple-element.78.refs_0_, bf16[256,2048]{1,0:T(8,128)(2,1)S(1)} %collective-permute-done.14.refs_1_, ...), custom_call_target="tpu_custom_call" | custom-call | flops 10000000000 | bytes 1 | tf_op jit(solution)/shard_map/finish/pallas_call | solution.py:586
  (7 shorter events, 0.1 us)
Async XLA Ops:
  0.6 0.7 %copy-start.3 = (s32[1,256]{1,0:T(1,128)S(1)}, s32[1,256]{1,0:T(1,128)}, u32[]{:S(2)}) copy-start(s32[1,256]{1,0:T(1,128)} %near.1) | copy-start | bytes 3076
  1.3 2.0 %copy-start = (bf16[1,256,2048]{2,1,0:T(8,128)(2,1)S(1)}, bf16[1,256,2048]{2,1,0:T(8,128)(2,1)}, u32[]{:S(2)}) copy-start(bf16[1,256,2048]{2,1,0:T(8,128)(2,1)} %param.13) | copy-start | bytes 3145732
  1.3 2.1 %copy-start.1 = (bf16[64,2048]{1,0:T(8,128)(2,1)S(1)}, bf16[64,2048]{1,0:T(8,128)(2,1)}, u32[]{:S(2)}) copy-start(bf16[64,2048]{1,0:T(8,128)(2,1)} %home0.1) | copy-start | bytes 786436
  1.3 7.7 %copy-start.2 = (s32[1,4,4]{2,1,0:T(4,128)S(1)}, s32[1,4,4]{2,1,0:T(4,128)}, u32[]{:S(2)}) copy-start(s32[1,4,4]{2,1,0:T(4,128)} %pattern.1) | copy-start | bytes 196
  1.3 7.7 %copy-start.4 = (s32[1,256]{1,0:T(1,128)S(1)}, s32[1,256]{1,0:T(1,128)}, u32[]{:S(2)}) copy-start(s32[1,256]{1,0:T(1,128)} %near.1) | copy-start | bytes 3076
  2.8 6.1 %collective-permute-start = (bf16[3,272,512]{2,1,0:T(8,128)(2,1)S(1)}, bf16[3,272,512]{2,1,0:T(8,128)(2,1)S(1)}, u32[]{:S(2)}, u32[]{:S(2)}) collective-permute-start(bf16[3,272,512]{2,1,0:T(8,128)(2,1)S(1)} %get-tuple-element.49), channel_id=1, source_target_pairs={{0,1},{1,0},{2,3},{3,2},{4,5},{5,4},{6,7},{7,6},{8,9},{9,8},{10,11... | collective-permute-start | bytes 2506760 | tf_op jit(solution)/shard_map/ppermute | solution.py:251
  3.4 8.7 %collective-permute-start.1 = (bf16[256,2048]{1,0:T(8,128)(2,1)S(1)}, bf16[256,2048]{1,0:T(8,128)(2,1)S(1)}, u32[]{:S(2)}, u32[]{:S(2)}) collective-permute-start(bf16[256,2048]{1,0:T(8,128)(2,1)S(1)} %bitcast.8), channel_id=1, source_target_pairs={{0,1},{1,0},{2,3},{3,2},{4,5},{5,4},{6,7},{7,6},{8,9},{9,8},{10,11... | collective-permute-start | bytes 3145736 | tf_op jit(solution)/shard_map/ppermute | solution.py:251
  3.5 11.1 %collective-permute-start.2 = (bf16[64,2048]{1,0:T(8,128)(2,1)S(1)}, bf16[64,2048]{1,0:T(8,128)(2,1)S(1)}, u32[]{:S(2)}, u32[]{:S(2)}) collective-permute-start(bf16[64,2048]{1,0:T(8,128)(2,1)S(1)} %copy-done.1), channel_id=1, source_target_pairs={{0,4},{1,3},{2,6},{3,1},{4,0},{5,7},{6,2},{7,5},{8,12},{9,11},{10,... | collective-permute-start | bytes 786440 | tf_op jit(solution)/shard_map/ppermute | solution.py:247
  6.4 10.0 %collective-permute-start.3 = (bf16[64,2048]{1,0:T(8,128)(2,1)S(1)}, bf16[64,2048]{1,0:T(8,128)(2,1)S(1)}, u32[]{:S(2)}, u32[]{:S(2)}) collective-permute-start(bf16[64,2048]{1,0:T(8,128)(2,1)S(1)} %copy-done.1), channel_id=1, source_target_pairs={{0,16},{1,0},{2,18},{3,2},{4,20},{5,4},{6,22},{7,6},{8,24},{9,8},{... | collective-permute-start | bytes 786440 | tf_op jit(solution)/shard_map/ppermute | solution.py:247
  13.0 11.4 %collective-permute-start.7 = (bf16[2,2,64,1024]{3,2,1,0:T(8,128)(2,1)S(1)}, bf16[2,2,64,1024]{3,2,1,0:T(8,128)(2,1)S(1)}, u32[]{:S(2)}, u32[]{:S(2)}) collective-permute-start(bf16[2,2,64,1024]{3,2,1,0:T(8,128)(2,1)S(1)} %get-tuple-element.53.refs_0_), channel_id=1, source_target_pairs={{0,2},{1,5},{2,0},{3,7},{4,6},{5,1},{6,4},{7,3},{8,10},{9,13},{10,... | collective-permute-start | bytes 1572872 | tf_op jit(solution)/shard_map/ppermute | solution.py:247
  14.5 4.3 %collective-permute-start.4 = (bf16[64,2048]{1,0:T(8,128)(2,1)S(1)}, bf16[64,2048]{1,0:T(8,128)(2,1)S(1)}, u32[]{:S(2)}, u32[]{:S(2)}) collective-permute-start(bf16[64,2048]{1,0:T(8,128)(2,1)S(1)} %copy.14.refs_0_), channel_id=1, source_target_pairs={{0,16},{1,0},{2,18},{3,2},{4,20},{5,4},{6,22},{7,6},{8,24},{9,8},{... | collective-permute-start | bytes 786440 | tf_op jit(solution)/shard_map/ppermute | solution.py:247
  15.8 14.8 %collective-permute-start.6 = (bf16[2,2,64,1024]{3,2,1,0:T(8,128)(2,1)S(1)}, bf16[2,2,64,1024]{3,2,1,0:T(8,128)(2,1)S(1)}, u32[]{:S(2)}, u32[]{:S(2)}) collective-permute-start(bf16[2,2,64,1024]{3,2,1,0:T(8,128)(2,1)S(1)} %get-tuple-element.54.refs_0_), channel_id=1, source_target_pairs={{0,2},{1,5},{2,0},{3,7},{4,6},{5,1},{6,4},{7,3},{8,10},{9,13},{10,... | collective-permute-start | bytes 1572872 | tf_op jit(solution)/shard_map/ppermute | solution.py:247
  18.9 16.2 %collective-permute-start.9 = (bf16[2,64,2048]{2,1,0:T(8,128)(2,1)S(1)}, bf16[2,64,2048]{2,1,0:T(8,128)(2,1)S(1)}, u32[]{:S(2)}, u32[]{:S(2)}) collective-permute-start(bf16[2,64,2048]{2,1,0:T(8,128)(2,1)S(1)} %gather_pick.1.refs_0_.near), channel_id=1, source_target_pairs={{0,8},{1,9},{2,10},{3,11},{4,12},{5,13},{6,14},{7,15},{8,0},{9,1},... | collective-permute-start | bytes 1572872 | tf_op jit(solution)/shard_map/ppermute | solution.py:247
  23.2 15.8 %collective-permute-start.5 = (bf16[2,64,2048]{2,1,0:T(8,128)(2,1)S(1)}, bf16[2,64,2048]{2,1,0:T(8,128)(2,1)S(1)}, u32[]{:S(2)}, u32[]{:S(2)}) collective-permute-start(bf16[2,64,2048]{2,1,0:T(8,128)(2,1)S(1)} %gather_pick.1.refs_0_.near), channel_id=1, source_target_pairs={{0,2},{1,5},{2,0},{3,7},{4,6},{5,1},{6,4},{7,3},{8,10},{9,13},{10,... | collective-permute-start | bytes 1572872 | tf_op jit(solution)/shard_map/ppermute | solution.py:247
  24.5 8.7 %collective-permute-start.10 = (bf16[2,64,1024]{2,1,0:T(8,128)(2,1)S(1)}, bf16[2,64,1024]{2,1,0:T(8,128)(2,1)S(1)}, u32[]{:S(2)}, u32[]{:S(2)}) collective-permute-start(bf16[2,64,1024]{2,1,0:T(8,128)(2,1)S(1)} %get-tuple-element.57.refs_0_), channel_id=1, source_target_pairs={{0,4},{1,3},{2,6},{3,1},{4,0},{5,7},{6,2},{7,5},{8,12},{9,11},{10,... | collective-permute-start | bytes 786440 | tf_op jit(solution)/shard_map/ppermute | solution.py:247
  30.7 6.4 %collective-permute-start.8 = (bf16[2,64,1024]{2,1,0:T(8,128)(2,1)S(1)}, bf16[2,64,1024]{2,1,0:T(8,128)(2,1)S(1)}, u32[]{:S(2)}, u32[]{:S(2)}) collective-permute-start(bf16[2,64,1024]{2,1,0:T(8,128)(2,1)S(1)} %get-tuple-element.59.refs_0_), channel_id=1, source_target_pairs={{0,4},{1,3},{2,6},{3,1},{4,0},{5,7},{6,2},{7,5},{8,12},{9,11},{10,... | collective-permute-start | bytes 786440 | tf_op jit(solution)/shard_map/ppermute | solution.py:247
  33.3 8.2 %collective-permute-start.12 = (bf16[64,1024]{1,0:T(8,128)(2,1)S(1)}, bf16[64,1024]{1,0:T(8,128)(2,1)S(1)}, u32[]{:S(2)}, u32[]{:S(2)}) collective-permute-start(bf16[64,1024]{1,0:T(8,128)(2,1)S(1)} %get-tuple-element.61.refs_0_), channel_id=1, source_target_pairs={{0,9},{1,17},{2,11},{3,19},{4,13},{5,21},{6,15},{7,23},{8,1},{9,25... | collective-permute-start | bytes 393224 | tf_op jit(solution)/shard_map/ppermute | solution.py:247
  33.4 10.6 %collective-permute-start.13 = (bf16[64,1024]{1,0:T(8,128)(2,1)S(1)}, bf16[64,1024]{1,0:T(8,128)(2,1)S(1)}, u32[]{:S(2)}, u32[]{:S(2)}) collective-permute-start(bf16[64,1024]{1,0:T(8,128)(2,1)S(1)} %get-tuple-element.65), channel_id=1, source_target_pairs={{0,1},{1,25},{2,3},{3,27},{4,5},{5,29},{6,7},{7,31},{8,9},{9,17},{... | collective-permute-start | bytes 393224 | tf_op jit(solution)/shard_map/ppermute | solution.py:247
  35.1 9.6 %collective-permute-start.11 = (bf16[2,64,2048]{2,1,0:T(8,128)(2,1)S(1)}, bf16[2,64,2048]{2,1,0:T(8,128)(2,1)S(1)}, u32[]{:S(2)}, u32[]{:S(2)}) collective-permute-start(bf16[2,64,2048]{2,1,0:T(8,128)(2,1)S(1)} %copy.15.refs_0_.near), channel_id=1, source_target_pairs={{0,2},{1,5},{2,0},{3,7},{4,6},{5,1},{6,4},{7,3},{8,10},{9,13},{10,... | collective-permute-start | bytes 1572872 | tf_op jit(solution)/shard_map/ppermute | solution.py:247
  37.3 12.1 %collective-permute-start.18 = (bf16[64,1024]{1,0:T(8,128)(2,1)S(1)}, bf16[64,1024]{1,0:T(8,128)(2,1)S(1)}, u32[]{:S(2)}, u32[]{:S(2)}) collective-permute-start(bf16[64,1024]{1,0:T(8,128)(2,1)S(1)} %get-tuple-element.62.refs_0_), channel_id=1, source_target_pairs={{0,9},{1,17},{2,11},{3,19},{4,13},{5,21},{6,15},{7,23},{8,1},{9,25... | collective-permute-start | bytes 393224 | tf_op jit(solution)/shard_map/ppermute | solution.py:247
  39.1 10.4 %collective-permute-start.19 = (bf16[64,1024]{1,0:T(8,128)(2,1)S(1)}, bf16[64,1024]{1,0:T(8,128)(2,1)S(1)}, u32[]{:S(2)}, u32[]{:S(2)}) collective-permute-start(bf16[64,1024]{1,0:T(8,128)(2,1)S(1)} %get-tuple-element.85), channel_id=1, source_target_pairs={{0,1},{1,25},{2,3},{3,27},{4,5},{5,29},{6,7},{7,31},{8,9},{9,17},{... | collective-permute-start | bytes 393224 | tf_op jit(solution)/shard_map/ppermute | solution.py:247
  41.5 8.6 %collective-permute-start.15 = (bf16[3,256,256]{2,1,0:T(8,128)(2,1)S(1)}, bf16[3,256,256]{2,1,0:T(8,128)(2,1)S(1)}, u32[]{:S(2)}, u32[]{:S(2)}) collective-permute-start(bf16[3,256,256]{2,1,0:T(8,128)(2,1)S(1)} %get-tuple-element.75.refs_0_), channel_id=1, source_target_pairs={{0,1},{1,0},{2,3},{3,2},{4,5},{5,4},{6,7},{7,6},{8,9},{9,8},{10,11... | collective-permute-start | bytes 1179656 | tf_op jit(solution)/shard_map/ppermute | solution.py:251
  44.0 6.1 %collective-permute-start.17 = (f32[64,1024]{1,0:T(8,128)S(1)}, f32[64,1024]{1,0:T(8,128)S(1)}, u32[]{:S(2)}, u32[]{:S(2)}) collective-permute-start(f32[64,1024]{1,0:T(8,128)S(1)} %share.2.refs_0_.refs_6_), channel_id=1, source_target_pairs={{0,1},{1,0},{2,3},{3,2},{4,5},{5,4},{6,7},{7,6},{8,9},{9,8},{10,11... | collective-permute-start | bytes 786440 | tf_op jit(solution)/shard_map/ppermute | solution.py:251
  46.8 4.8 %collective-permute-start.14 = (bf16[256,2048]{1,0:T(8,128)(2,1)S(1)}, bf16[256,2048]{1,0:T(8,128)(2,1)S(1)}, u32[]{:S(2)}, u32[]{:S(2)}) collective-permute-start(bf16[256,2048]{1,0:T(8,128)(2,1)S(1)} %get-tuple-element.79.refs_0_), channel_id=1, source_target_pairs={{0,1},{1,0},{2,3},{3,2},{4,5},{5,4},{6,7},{7,6},{8,9},{9,8},{10,11... | collective-permute-start | bytes 3145736 | tf_op jit(solution)/shard_map/ppermute | solution.py:251
  49.4 2.2 %collective-permute-start.16 = (bf16[3,256,256]{2,1,0:T(8,128)(2,1)S(1)}, bf16[3,256,256]{2,1,0:T(8,128)(2,1)S(1)}, u32[]{:S(2)}, u32[]{:S(2)}) collective-permute-start(bf16[3,256,256]{2,1,0:T(8,128)(2,1)S(1)} %get-tuple-element.83.refs_0_), channel_id=1, source_target_pairs={{0,1},{1,0},{2,3},{3,2},{4,5},{5,4},{6,7},{7,6},{8,9},{9,8},{10,11... | collective-permute-start | bytes 1179656 | tf_op jit(solution)/shard_map/ppermute | solution.py:251
  49.5 2.0 %collective-permute-start.20 = (f32[64,1024]{1,0:T(8,128)S(1)}, f32[64,1024]{1,0:T(8,128)S(1)}, u32[]{:S(2)}, u32[]{:S(2)}) collective-permute-start(f32[64,1024]{1,0:T(8,128)S(1)} %share.3.refs_8_), channel_id=1, source_target_pairs={{0,1},{1,0},{2,3},{3,2},{4,5},{5,4},{6,7},{7,6},{8,9},{9,8},{10,11... | collective-permute-start | bytes 786440 | tf_op jit(solution)/shard_map/ppermute | solution.py:251

commit v7 on v6

--- a/solution.py
+++ b/solution.py
@@ -458,7 +458,7 @@
     send, own = refs[-2:]
     tokens = rot_k.shape[0]
     half = tokens // 2
-    step = 2 * BLK
+    step = 4 * BLK
     scale = 1.0 / math.sqrt(HD)
     cos, sin = cos_ref[...], -sin_ref[...]
     for at_head in range(2):

time: 53.5 us -> 53.5 us (level)
  transfers between devices with their start and end apart: 21 -> 21, of which waited for: 9 -> 9; matrix products, arithmetic and copies ran while one was open for 0% -> 0% of each run, Pallas kernels for 22% -> 21%
where the time goes in v7:
time: 53.5 us; the launch traced here: 53.3 us
  starting transfers between devices  20.8 us (39%)
  waiting for transfers between devices  16.3 us (30%)
  Pallas kernels  14.7 us (27%)
  between operations  0.82 us (2%)
  local copies, waits for them, and re-layouts  0.69 us (1%)
    ppermute x14, starting transfers between devices, move(): return lax.ppermute(array, ('dp', 'ctx'), chip_moves(rule))  17.5 us
    ppermute x14, waiting for transfers between devices, move(): return lax.ppermute(array, ('dp', 'ctx'), chip_moves(rule))  14.8 us
    pallas_call x19, Pallas kernels, call(): pl.pallas_call(kernel, in_specs=list(specs or [in_vmem] * len(args)) + [a...  14.7 us
    ppermute x7, starting transfers between devices, swap_core(): return lax.ppermute(array, 'ctx', [(0, 1), (1, 0)])  3.31 us
    ppermute x7, waiting for transfers between devices, swap_core(): return lax.ppermute(array, 'ctx', [(0, 1), (1, 0)])  1.46 us
  transfers between devices with their start and end apart: 21, of which 9 were waited for; matrix products, arithmetic and copies ran while one was open for 0% of the time, Pallas kernels for 21%

profile of v7, /device:TPU:0, one launch (start us, length us, event | category | flops | bytes accessed | tf_op | source)
XLA Modules:
  0.0 53.3 jit_solution(15630898038091642927)
XLA Ops:
  0.6 0.0 copy-start.3
  0.6 0.7 %copy-done.3 = s32[1,256]{1,0:T(1,128)S(1)} copy-done((s32[1,256]{1,0:T(1,128)S(1)}, s32[1,256]{1,0:T(1,128)}, u32[]{:S(2)}) %copy-start.3) | copy-done | bytes 1048
  1.3 1.5 %pack.1 = (bf16[3,272,512]{2,1,0:T(8,128)(2,1)S(1)}, bf16[3,256,512]{2,1,0:T(8,128)(2,1)S(1)}) custom-call(s32[1,256]{1,0:T(1,128)S(1)} %copy-done.3, bf16[256,1024]{1,0:T(8,128)(2,1)} %bitcast.13, bf16[256,1024]{1,0:T(8,128)(2,1)} %bitcast.14, bf16[256,1024]{1,0:T(8,128)(2,1)} %bitcast.15), custom_call_target="tpu_custom_call" | custom-call | flops 10000000000 | bytes 1 | tf_op jit(solution)/shard_map/pack/pallas_call | solution.py:586
  2.8 0.5 collective-permute-start
  3.4 0.0 copy-done
  3.4 0.1 collective-permute-start.1
  3.5 0.0 copy-done.1
  3.5 2.9 %collective-permute-start.2 = (bf16[64,2048]{1,0:T(8,128)(2,1)S(1)}, bf16[64,2048]{1,0:T(8,128)(2,1)S(1)}, u32[]{:S(2)}, u32[]{:S(2)}) collective-permute-start(bf16[64,2048]{1,0:T(8,128)(2,1)S(1)} %copy-done.1), channel_id=1, source_target_pairs={{0,4},{1,3},{2,6},{3,1},{4,0},{5,7},{6,2},{7,5},{8,12},{9,11},{10,... | collective-permute-start | bytes 786440 | tf_op jit(solution)/shard_map/ppermute | solution.py:247
  6.4 2.6 %collective-permute-start.3 = (bf16[64,2048]{1,0:T(8,128)(2,1)S(1)}, bf16[64,2048]{1,0:T(8,128)(2,1)S(1)}, u32[]{:S(2)}, u32[]{:S(2)}) collective-permute-start(bf16[64,2048]{1,0:T(8,128)(2,1)S(1)} %copy-done.1), channel_id=1, source_target_pairs={{0,16},{1,0},{2,18},{3,2},{4,20},{5,4},{6,22},{7,6},{8,24},{9,8},{... | collective-permute-start | bytes 786440 | tf_op jit(solution)/shard_map/ppermute | solution.py:247
  9.0 0.0 collective-permute-done.received
  9.0 0.0 copy-done.2
  9.0 0.0 copy-done.4
  9.0 3.1 %forward.1 = (bf16[512,512]{1,0:T(8,128)(2,1)S(1)}, bf16[512,512]{1,0:T(8,128)(2,1)S(1)}, bf16[512,512]{1,0:T(8,128)(2,1)S(1)}, bf16[512,512]{1,0:T(8,128)(2,1)S...) custom-call(s32[1,4,4]{2,1,0:T(4,128)S(1)} %copy-done.2, ...), custom_call_target="tpu_custom_call" | custom-call | flops 10000000000 | bytes 1 | tf_op jit(solution)/shard_map/forward/pallas_call | solution.py:586
  12.1 0.0 collective-permute-done.1.other
  12.1 0.9 %weight_grad.2 = (bf16[2,2,64,1024]{3,2,1,0:T(8,128)(2,1)S(1)}, bf16[2,2,64,1024]{3,2,1,0:T(8,128)(2,1)S(1)}) custom-call(bf16[512,512]{1,0:T(8,128)(2,1)S(1)} %get-tuple-element.51.attn_t, bf16[256,2048]{1,0:T(8,128)(2,1)S(1)} %bitcast.9, bf16[256,2048]{1,0:T(8,128)(2,1)S(1)} %collective-permute-done.1.other, ...), custom_call_target="tpu_custom_call" | custom-call | flops 10000000000 | bytes 1 | tf_op jit(solution)/shard_map/weight_grad/pallas_call | solution.py:586
  13.0 1.6 %collective-permute-start.7 = (bf16[2,2,64,1024]{3,2,1,0:T(8,128)(2,1)S(1)}, bf16[2,2,64,1024]{3,2,1,0:T(8,128)(2,1)S(1)}, u32[]{:S(2)}, u32[]{:S(2)}) collective-permute-start(bf16[2,2,64,1024]{3,2,1,0:T(8,128)(2,1)S(1)} %get-tuple-element.53.refs_0_), channel_id=1, source_target_pairs={{0,2},{1,5},{2,0},{3,7},{4,6},{5,1},{6,4},{7,3},{8,10},{9,13},{10,... | collective-permute-start | bytes 1572872 | tf_op jit(solution)/shard_map/ppermute | solution.py:247
  14.5 0.0 collective-permute-done.2.a.home1
  14.5 0.4 collective-permute-start.4
  14.9 0.9 %weight_grad.3 = (bf16[2,2,64,1024]{3,2,1,0:T(8,128)(2,1)S(1)}, bf16[2,2,64,1024]{3,2,1,0:T(8,128)(2,1)S(1)}) custom-call(bf16[512,512]{1,0:T(8,128)(2,1)S(1)} %get-tuple-element.51.attn_t, bf16[256,2048]{1,0:T(8,128)(2,1)S(1)} %bitcast.10, bf16[256,2048]{1,0:T(8,128)(2,1)S(1)} %collective-permute-done.1.other, bf16[64,2048]{1,0:T(8,128)(2,1)S(1)} %copy.14.refs_0_), custom_call_target="tpu_custom_call" | custom-call | flops 10000000000 | bytes 1 | tf_op jit(solution)/shard_map/weight_grad/pallas_call | solution.py:586
  15.8 0.6 %collective-permute-start.6 = (bf16[2,2,64,1024]{3,2,1,0:T(8,128)(2,1)S(1)}, bf16[2,2,64,1024]{3,2,1,0:T(8,128)(2,1)S(1)}, u32[]{:S(2)}, u32[]{:S(2)}) collective-permute-start(bf16[2,2,64,1024]{3,2,1,0:T(8,128)(2,1)S(1)} %get-tuple-element.54.refs_0_), channel_id=1, source_target_pairs={{0,2},{1,5},{2,0},{3,7},{4,6},{5,1},{6,4},{7,3},{8,10},{9,13},{10,... | collective-permute-start | bytes 1572872 | tf_op jit(solution)/shard_map/ppermute | solution.py:247
  16.4 0.0 collective-permute-done.3.away0
  16.4 2.5 %collective-permute-done.4.away1 = bf16[64,2048]{1,0:T(8,128)(2,1)S(1)} collective-permute-done((bf16[64,2048]{1,0:T(8,128)(2,1)S(1)}, bf16[64,2048]{1,0:T(8,128)(2,1)S(1)}, u32[]{:S(2)}, u32[]{:S(2)}) %collective-permute-start.4) | collective-permute-done | bytes 262176 | tf_op jit(solution)/shard_map/ppermute | solution.py:247
  18.9 4.3 %collective-permute-start.9 = (bf16[2,64,2048]{2,1,0:T(8,128)(2,1)S(1)}, bf16[2,64,2048]{2,1,0:T(8,128)(2,1)S(1)}, u32[]{:S(2)}, u32[]{:S(2)}) collective-permute-start(bf16[2,64,2048]{2,1,0:T(8,128)(2,1)S(1)} %gather_pick.1.refs_0_.near), channel_id=1, source_target_pairs={{0,8},{1,9},{2,10},{3,11},{4,12},{5,13},{6,14},{7,15},{8,0},{9,1},... | collective-permute-start | bytes 1572872 | tf_op jit(solution)/shard_map/ppermute | solution.py:247
  23.2 1.2 %collective-permute-start.5 = (bf16[2,64,2048]{2,1,0:T(8,128)(2,1)S(1)}, bf16[2,64,2048]{2,1,0:T(8,128)(2,1)S(1)}, u32[]{:S(2)}, u32[]{:S(2)}) collective-permute-start(bf16[2,64,2048]{2,1,0:T(8,128)(2,1)S(1)} %gather_pick.1.refs_0_.near), channel_id=1, source_target_pairs={{0,2},{1,5},{2,0},{3,7},{4,6},{5,1},{6,4},{7,3},{8,10},{9,13},{10,... | collective-permute-start | bytes 1572872 | tf_op jit(solution)/shard_map/ppermute | solution.py:247
  24.4 0.0 collective-permute-done.7.got
  24.4 0.1 second_sum.2
  24.5 0.9 %collective-permute-start.10 = (bf16[2,64,1024]{2,1,0:T(8,128)(2,1)S(1)}, bf16[2,64,1024]{2,1,0:T(8,128)(2,1)S(1)}, u32[]{:S(2)}, u32[]{:S(2)}) collective-permute-start(bf16[2,64,1024]{2,1,0:T(8,128)(2,1)S(1)} %get-tuple-element.57.refs_0_), channel_id=1, source_target_pairs={{0,4},{1,3},{2,6},{3,1},{4,0},{5,7},{6,2},{7,5},{8,12},{9,11},{10,... | collective-permute-start | bytes 786440 | tf_op jit(solution)/shard_map/ppermute | solution.py:247
  25.5 5.1 %collective-permute-done.6.got = bf16[2,2,64,1024]{3,2,1,0:T(8,128)(2,1)S(1)} collective-permute-done((bf16[2,2,64,1024]{3,2,1,0:T(8,128)(2,1)S(1)}, bf16[2,2,64,1024]{3,2,1,0:T(8,128)(2,1)S(1)}, u32[]{:S(2)}, u32[]{:S(2)}) %collective-permute-start.6) | collective-permute-done | bytes 524320 | tf_op jit(solution)/shard_map/ppermute | solution.py:247
  30.6 0.1 second_sum.3
  30.7 0.2 collective-permute-start.8
  30.9 2.3 %collective-permute-done.10.got = bf16[2,64,1024]{2,1,0:T(8,128)(2,1)S(1)} collective-permute-done((bf16[2,64,1024]{2,1,0:T(8,128)(2,1)S(1)}, bf16[2,64,1024]{2,1,0:T(8,128)(2,1)S(1)}, u32[]{:S(2)}, u32[]{:S(2)}) %collective-permute-start.10) | collective-permute-done | bytes 262176 | tf_op jit(solution)/shard_map/ppermute | solution.py:247
  33.2 0.1 z_sum.2
  33.3 0.1 collective-permute-start.12
  33.4 0.1 collective-permute-start.13
  33.4 1.6 %collective-permute-done.9.a = bf16[2,64,2048]{2,1,0:T(8,128)(2,1)S(1)} collective-permute-done((bf16[2,64,2048]{2,1,0:T(8,128)(2,1)S(1)}, bf16[2,64,2048]{2,1,0:T(8,128)(2,1)S(1)}, u32[]{:S(2)}, u32[]{:S(2)}) %collective-permute-start.9) | collective-permute-done | bytes 524320 | tf_op jit(solution)/shard_map/ppermute | solution.py:247
  35.1 1.6 %collective-permute-start.11 = (bf16[2,64,2048]{2,1,0:T(8,128)(2,1)S(1)}, bf16[2,64,2048]{2,1,0:T(8,128)(2,1)S(1)}, u32[]{:S(2)}, u32[]{:S(2)}) collective-permute-start(bf16[2,64,2048]{2,1,0:T(8,128)(2,1)S(1)} %copy.15.refs_0_.near), channel_id=1, source_target_pairs={{0,2},{1,5},{2,0},{3,7},{4,6},{5,1},{6,4},{7,3},{8,10},{9,13},{10,... | collective-permute-start | bytes 1572872 | tf_op jit(solution)/shard_map/ppermute | solution.py:247
  36.7 0.5 collective-permute-done.8.got
  37.2 0.1 z_sum.3
  37.3 1.1 %collective-permute-start.18 = (bf16[64,1024]{1,0:T(8,128)(2,1)S(1)}, bf16[64,1024]{1,0:T(8,128)(2,1)S(1)}, u32[]{:S(2)}, u32[]{:S(2)}) collective-permute-start(bf16[64,1024]{1,0:T(8,128)(2,1)S(1)} %get-tuple-element.62.refs_0_), channel_id=1, source_target_pairs={{0,9},{1,17},{2,11},{3,19},{4,13},{5,21},{6,15},{7,23},{8,1},{9,25... | collective-permute-start | bytes 393224 | tf_op jit(solution)/shard_map/ppermute | solution.py:247
  38.4 0.7 %collective-permute-done.5.far = bf16[2,64,2048]{2,1,0:T(8,128)(2,1)S(1)} collective-permute-done((bf16[2,64,2048]{2,1,0:T(8,128)(2,1)S(1)}, bf16[2,64,2048]{2,1,0:T(8,128)(2,1)S(1)}, u32[]{:S(2)}, u32[]{:S(2)}) %collective-permute-start.5) | collective-permute-done | bytes 524320 | tf_op jit(solution)/shard_map/ppermute | solution.py:247
  39.1 0.0 collective-permute-start.19
  39.1 0.8 %attn_grad.2 = (bf16[256,512]{1,0:T(8,128)(2,1)S(1)}, f32[2,512]{1,0:T(2,128)S(1)}, bf16[256,2048]{1,0:T(8,128)(2,1)S(1)}) custom-call(bf16[512,512]{1,0:T(8,128)(2,1)S(1)} %get-tuple-element.51.attn_t, bf16[256,2048]{1,0:T(8,128)(2,1)S(1)} %bitcast.11, bf16[256,2048]{1,0:T(8,128)(2,1)S(1)} %collective-permute-done.1.other, ...), custom_call_target="tpu_custom_call" | custom-call | flops 10000000000 | bytes 1 | tf_op jit(solution)/shard_map/attn_grad/pallas_call | solution.py:586
  39.9 1.5 %backward.2 = (bf16[3,256,256]{2,1,0:T(8,128)(2,1)S(1)}, bf16[3,256,256]{2,1,0:T(8,128)(2,1)S(1)}) custom-call(bf16[512,512]{1,0:T(8,128)(2,1)S(1)} %get-tuple-element.52.refs_0_.rot_q, bf16[512,512]{1,0:T(8,128)(2,1)S(1)} %get-tuple-element.66.rot_k, bf16[512,512]{1,0:T(8,128)(2,1)S(1)} %get-tuple-element.67.rot_kt, ...), custom_call_target="tpu_custom_call" | custom-call | flops 10000000000 | bytes 1 | tf_op jit(solution)/shard_map/backward/pallas_call | solution.py:586
  41.4 0.0 collective-permute-done.12.first
  41.4 1.0 %collective-permute-start.15 = (bf16[3,256,256]{2,1,0:T(8,128)(2,1)S(1)}, bf16[3,256,256]{2,1,0:T(8,128)(2,1)S(1)}, u32[]{:S(2)}, u32[]{:S(2)}) collective-permute-start(bf16[3,256,256]{2,1,0:T(8,128)(2,1)S(1)} %get-tuple-element.75.refs_0_), channel_id=1, source_target_pairs={{0,1},{1,0},{2,3},{3,2},{4,5},{5,4},{6,7},{7,6},{8,9},{9,8},{10,11... | collective-permute-start | bytes 1179656 | tf_op jit(solution)/shard_map/ppermute | solution.py:251
  42.4 1.5 %collective-permute-done.13.second = bf16[64,1024]{1,0:T(8,128)(2,1)S(1)} collective-permute-done((bf16[64,1024]{1,0:T(8,128)(2,1)S(1)}, bf16[64,1024]{1,0:T(8,128)(2,1)S(1)}, u32[]{:S(2)}, u32[]{:S(2)}) %collective-permute-start.13) | collective-permute-done | bytes 131104 | tf_op jit(solution)/shard_map/ppermute | solution.py:247
  44.0 0.1 share.2.refs_0_.refs_6_
  44.0 0.1 collective-permute-start.17
  44.1 0.6 %collective-permute-done.11.far = bf16[2,64,2048]{2,1,0:T(8,128)(2,1)S(1)} collective-permute-done((bf16[2,64,2048]{2,1,0:T(8,128)(2,1)S(1)}, bf16[2,64,2048]{2,1,0:T(8,128)(2,1)S(1)}, u32[]{:S(2)}, u32[]{:S(2)}) %collective-permute-start.11) | collective-permute-done | bytes 524320 | tf_op jit(solution)/shard_map/ppermute | solution.py:247
  44.7 0.8 %attn_grad.3 = (bf16[256,512]{1,0:T(8,128)(2,1)S(1)}, f32[2,512]{1,0:T(2,128)S(1)}, bf16[256,2048]{1,0:T(8,128)(2,1)S(1)}) custom-call(bf16[512,512]{1,0:T(8,128)(2,1)S(1)} %get-tuple-element.51.attn_t, bf16[256,2048]{1,0:T(8,128)(2,1)S(1)} %bitcast.12, bf16[256,2048]{1,0:T(8,128)(2,1)S(1)} %collective-permute-done.1.other, ...), custom_call_target="tpu_custom_call" | custom-call | flops 10000000000 | bytes 1 | tf_op jit(solution)/shard_map/attn_grad/pallas_call | solution.py:586
  45.5 1.3 %projection.1 = (bf16[256,2048]{1,0:T(8,128)(2,1)S(1)}, f32[256,2048]{1,0:T(8,128)S(1)}) custom-call(bf16[512,512]{1,0:T(8,128)(2,1)S(1)} %get-tuple-element.50.attn, bf16[256,2048]{1,0:T(8,128)(2,1)S(1)} %get-tuple-element.63.low, bf16[256,2048]{1,0:T(8,128)(2,1)S(1)} %get-tuple-element.76.high, bf16[256,512]{1,0:T(8,128)(2,1)S(1)} %get-tuple-element.77.refs_0_.grad_t), custom_call_target="tpu_custom_call" | custom-call | flops 10000000000 | bytes 1 | tf_op jit(solution)/shard_map/projection/pallas_call | solution.py:586
  46.8 1.0 %collective-permute-start.14 = (bf16[256,2048]{1,0:T(8,128)(2,1)S(1)}, bf16[256,2048]{1,0:T(8,128)(2,1)S(1)}, u32[]{:S(2)}, u32[]{:S(2)}) collective-permute-start(bf16[256,2048]{1,0:T(8,128)(2,1)S(1)} %get-tuple-element.79.refs_0_), channel_id=1, source_target_pairs={{0,1},{1,0},{2,3},{3,2},{4,5},{5,4},{6,7},{7,6},{8,9},{9,8},{10,11... | collective-permute-start | bytes 3145736 | tf_op jit(solution)/shard_map/ppermute | solution.py:251
  47.8 1.5 %backward.3 = (bf16[3,256,256]{2,1,0:T(8,128)(2,1)S(1)}, bf16[3,256,256]{2,1,0:T(8,128)(2,1)S(1)}) custom-call(bf16[512,512]{1,0:T(8,128)(2,1)S(1)} %get-tuple-element.52.refs_0_.rot_q, bf16[512,512]{1,0:T(8,128)(2,1)S(1)} %get-tuple-element.66.rot_k, bf16[512,512]{1,0:T(8,128)(2,1)S(1)} %get-tuple-element.67.rot_kt, ...), custom_call_target="tpu_custom_call" | custom-call | flops 10000000000 | bytes 1 | tf_op jit(solution)/shard_map/backward/pallas_call | solution.py:586
  49.3 0.0 collective-permute-done.18.first
  49.3 0.1 collective-permute-start.16
  49.4 0.0 collective-permute-done.19.second
  49.4 0.1 share.3.refs_8_
  49.5 0.5 %collective-permute-start.20 = (f32[64,1024]{1,0:T(8,128)S(1)}, f32[64,1024]{1,0:T(8,128)S(1)}, u32[]{:S(2)}, u32[]{:S(2)}) collective-permute-start(f32[64,1024]{1,0:T(8,128)S(1)} %share.3.refs_8_), channel_id=1, source_target_pairs={{0,1},{1,0},{2,3},{3,2},{4,5},{5,4},{6,7},{7,6},{8,9},{9,8},{10,11... | collective-permute-start | bytes 786440 | tf_op jit(solution)/shard_map/ppermute | solution.py:251
  50.0 0.0 collective-permute-done.17.refs_7_
  50.0 0.0 collective-permute-done.15.refs_3_
  50.0 1.4 %collective-permute-done.20.refs_9_ = f32[64,1024]{1,0:T(8,128)S(1)} collective-permute-done((f32[64,1024]{1,0:T(8,128)S(1)}, f32[64,1024]{1,0:T(8,128)S(1)}, u32[]{:S(2)}, u32[]{:S(2)}) %collective-permute-start.20) | collective-permute-done | bytes 262176 | tf_op jit(solution)/shard_map/ppermute | solution.py:251
  51.5 0.0 collective-permute-done.16.refs_5_
  51.5 0.0 collective-permute-done.14.refs_1_
  51.5 1.8 %finish.1 = (bf16[256,2048]{1,0:T(8,128)(2,1)}, bf16[256,1024]{1,0:T(8,128)(2,1)}, bf16[256,1024]{1,0:T(8,128)(2,1)}, bf16[256,1024]{1,0:T(8,128)(2,1)}, f32[64,2048]{1,0:T(8,128)}) custom-call(f32[256,2048]{1,0:T(8,128)S(1)} %get-tuple-element.78.refs_0_, bf16[256,2048]{1,0:T(8,128)(2,1)S(1)} %collective-permute-done.14.refs_1_, ...), custom_call_target="tpu_custom_call" | custom-call | flops 10000000000 | bytes 1 | tf_op jit(solution)/shard_map/finish/pallas_call | solution.py:586
  (7 shorter events, 0.1 us)
Async XLA Ops:
  0.6 0.7 %copy-start.3 = (s32[1,256]{1,0:T(1,128)S(1)}, s32[1,256]{1,0:T(1,128)}, u32[]{:S(2)}) copy-start(s32[1,256]{1,0:T(1,128)} %near.1) | copy-start | bytes 3076
  1.3 2.0 %copy-start = (bf16[1,256,2048]{2,1,0:T(8,128)(2,1)S(1)}, bf16[1,256,2048]{2,1,0:T(8,128)(2,1)}, u32[]{:S(2)}) copy-start(bf16[1,256,2048]{2,1,0:T(8,128)(2,1)} %param.13) | copy-start | bytes 3145732
  1.3 2.1 %copy-start.1 = (bf16[64,2048]{1,0:T(8,128)(2,1)S(1)}, bf16[64,2048]{1,0:T(8,128)(2,1)}, u32[]{:S(2)}) copy-start(bf16[64,2048]{1,0:T(8,128)(2,1)} %home0.1) | copy-start | bytes 786436
  1.3 7.7 %copy-start.2 = (s32[1,4,4]{2,1,0:T(4,128)S(1)}, s32[1,4,4]{2,1,0:T(4,128)}, u32[]{:S(2)}) copy-start(s32[1,4,4]{2,1,0:T(4,128)} %pattern.1) | copy-start | bytes 196
  1.3 7.7 %copy-start.4 = (s32[1,256]{1,0:T(1,128)S(1)}, s32[1,256]{1,0:T(1,128)}, u32[]{:S(2)}) copy-start(s32[1,256]{1,0:T(1,128)} %near.1) | copy-start | bytes 3076
  2.8 6.1 %collective-permute-start = (bf16[3,272,512]{2,1,0:T(8,128)(2,1)S(1)}, bf16[3,272,512]{2,1,0:T(8,128)(2,1)S(1)}, u32[]{:S(2)}, u32[]{:S(2)}) collective-permute-start(bf16[3,272,512]{2,1,0:T(8,128)(2,1)S(1)} %get-tuple-element.49), channel_id=1, source_target_pairs={{0,1},{1,0},{2,3},{3,2},{4,5},{5,4},{6,7},{7,6},{8,9},{9,8},{10,11... | collective-permute-start | bytes 2506760 | tf_op jit(solution)/shard_map/ppermute | solution.py:251
  3.4 8.7 %collective-permute-start.1 = (bf16[256,2048]{1,0:T(8,128)(2,1)S(1)}, bf16[256,2048]{1,0:T(8,128)(2,1)S(1)}, u32[]{:S(2)}, u32[]{:S(2)}) collective-permute-start(bf16[256,2048]{1,0:T(8,128)(2,1)S(1)} %bitcast.8), channel_id=1, source_target_pairs={{0,1},{1,0},{2,3},{3,2},{4,5},{5,4},{6,7},{7,6},{8,9},{9,8},{10,11... | collective-permute-start | bytes 3145736 | tf_op jit(solution)/shard_map/ppermute | solution.py:251
  3.5 11.1 %collective-permute-start.2 = (bf16[64,2048]{1,0:T(8,128)(2,1)S(1)}, bf16[64,2048]{1,0:T(8,128)(2,1)S(1)}, u32[]{:S(2)}, u32[]{:S(2)}) collective-permute-start(bf16[64,2048]{1,0:T(8,128)(2,1)S(1)} %copy-done.1), channel_id=1, source_target_pairs={{0,4},{1,3},{2,6},{3,1},{4,0},{5,7},{6,2},{7,5},{8,12},{9,11},{10,... | collective-permute-start | bytes 786440 | tf_op jit(solution)/shard_map/ppermute | solution.py:247
  6.4 10.0 %collective-permute-start.3 = (bf16[64,2048]{1,0:T(8,128)(2,1)S(1)}, bf16[64,2048]{1,0:T(8,128)(2,1)S(1)}, u32[]{:S(2)}, u32[]{:S(2)}) collective-permute-start(bf16[64,2048]{1,0:T(8,128)(2,1)S(1)} %copy-done.1), channel_id=1, source_target_pairs={{0,16},{1,0},{2,18},{3,2},{4,20},{5,4},{6,22},{7,6},{8,24},{9,8},{... | collective-permute-start | bytes 786440 | tf_op jit(solution)/shard_map/ppermute | solution.py:247
  13.0 11.4 %collective-permute-start.7 = (bf16[2,2,64,1024]{3,2,1,0:T(8,128)(2,1)S(1)}, bf16[2,2,64,1024]{3,2,1,0:T(8,128)(2,1)S(1)}, u32[]{:S(2)}, u32[]{:S(2)}) collective-permute-start(bf16[2,2,64,1024]{3,2,1,0:T(8,128)(2,1)S(1)} %get-tuple-element.53.refs_0_), channel_id=1, source_target_pairs={{0,2},{1,5},{2,0},{3,7},{4,6},{5,1},{6,4},{7,3},{8,10},{9,13},{10,... | collective-permute-start | bytes 1572872 | tf_op jit(solution)/shard_map/ppermute | solution.py:247
  14.5 4.3 %collective-permute-start.4 = (bf16[64,2048]{1,0:T(8,128)(2,1)S(1)}, bf16[64,2048]{1,0:T(8,128)(2,1)S(1)}, u32[]{:S(2)}, u32[]{:S(2)}) collective-permute-start(bf16[64,2048]{1,0:T(8,128)(2,1)S(1)} %copy.14.refs_0_), channel_id=1, source_target_pairs={{0,16},{1,0},{2,18},{3,2},{4,20},{5,4},{6,22},{7,6},{8,24},{9,8},{... | collective-permute-start | bytes 786440 | tf_op jit(solution)/shard_map/ppermute | solution.py:247
  15.8 14.8 %collective-permute-start.6 = (bf16[2,2,64,1024]{3,2,1,0:T(8,128)(2,1)S(1)}, bf16[2,2,64,1024]{3,2,1,0:T(8,128)(2,1)S(1)}, u32[]{:S(2)}, u32[]{:S(2)}) collective-permute-start(bf16[2,2,64,1024]{3,2,1,0:T(8,128)(2,1)S(1)} %get-tuple-element.54.refs_0_), channel_id=1, source_target_pairs={{0,2},{1,5},{2,0},{3,7},{4,6},{5,1},{6,4},{7,3},{8,10},{9,13},{10,... | collective-permute-start | bytes 1572872 | tf_op jit(solution)/shard_map/ppermute | solution.py:247
  18.9 16.2 %collective-permute-start.9 = (bf16[2,64,2048]{2,1,0:T(8,128)(2,1)S(1)}, bf16[2,64,2048]{2,1,0:T(8,128)(2,1)S(1)}, u32[]{:S(2)}, u32[]{:S(2)}) collective-permute-start(bf16[2,64,2048]{2,1,0:T(8,128)(2,1)S(1)} %gather_pick.1.refs_0_.near), channel_id=1, source_target_pairs={{0,8},{1,9},{2,10},{3,11},{4,12},{5,13},{6,14},{7,15},{8,0},{9,1},... | collective-permute-start | bytes 1572872 | tf_op jit(solution)/shard_map/ppermute | solution.py:247
  23.2 15.8 %collective-permute-start.5 = (bf16[2,64,2048]{2,1,0:T(8,128)(2,1)S(1)}, bf16[2,64,2048]{2,1,0:T(8,128)(2,1)S(1)}, u32[]{:S(2)}, u32[]{:S(2)}) collective-permute-start(bf16[2,64,2048]{2,1,0:T(8,128)(2,1)S(1)} %gather_pick.1.refs_0_.near), channel_id=1, source_target_pairs={{0,2},{1,5},{2,0},{3,7},{4,6},{5,1},{6,4},{7,3},{8,10},{9,13},{10,... | collective-permute-start | bytes 1572872 | tf_op jit(solution)/shard_map/ppermute | solution.py:247
  24.5 8.7 %collective-permute-start.10 = (bf16[2,64,1024]{2,1,0:T(8,128)(2,1)S(1)}, bf16[2,64,1024]{2,1,0:T(8,128)(2,1)S(1)}, u32[]{:S(2)}, u32[]{:S(2)}) collective-permute-start(bf16[2,64,1024]{2,1,0:T(8,128)(2,1)S(1)} %get-tuple-element.57.refs_0_), channel_id=1, source_target_pairs={{0,4},{1,3},{2,6},{3,1},{4,0},{5,7},{6,2},{7,5},{8,12},{9,11},{10,... | collective-permute-start | bytes 786440 | tf_op jit(solution)/shard_map/ppermute | solution.py:247
  30.7 6.4 %collective-permute-start.8 = (bf16[2,64,1024]{2,1,0:T(8,128)(2,1)S(1)}, bf16[2,64,1024]{2,1,0:T(8,128)(2,1)S(1)}, u32[]{:S(2)}, u32[]{:S(2)}) collective-permute-start(bf16[2,64,1024]{2,1,0:T(8,128)(2,1)S(1)} %get-tuple-element.59.refs_0_), channel_id=1, source_target_pairs={{0,4},{1,3},{2,6},{3,1},{4,0},{5,7},{6,2},{7,5},{8,12},{9,11},{10,... | collective-permute-start | bytes 786440 | tf_op jit(solution)/shard_map/ppermute | solution.py:247
  33.3 8.1 %collective-permute-start.12 = (bf16[64,1024]{1,0:T(8,128)(2,1)S(1)}, bf16[64,1024]{1,0:T(8,128)(2,1)S(1)}, u32[]{:S(2)}, u32[]{:S(2)}) collective-permute-start(bf16[64,1024]{1,0:T(8,128)(2,1)S(1)} %get-tuple-element.61.refs_0_), channel_id=1, source_target_pairs={{0,9},{1,17},{2,11},{3,19},{4,13},{5,21},{6,15},{7,23},{8,1},{9,25... | collective-permute-start | bytes 393224 | tf_op jit(solution)/shard_map/ppermute | solution.py:247
  33.4 10.6 %collective-permute-start.13 = (bf16[64,1024]{1,0:T(8,128)(2,1)S(1)}, bf16[64,1024]{1,0:T(8,128)(2,1)S(1)}, u32[]{:S(2)}, u32[]{:S(2)}) collective-permute-start(bf16[64,1024]{1,0:T(8,128)(2,1)S(1)} %get-tuple-element.65), channel_id=1, source_target_pairs={{0,1},{1,25},{2,3},{3,27},{4,5},{5,29},{6,7},{7,31},{8,9},{9,17},{... | collective-permute-start | bytes 393224 | tf_op jit(solution)/shard_map/ppermute | solution.py:247
  35.1 9.6 %collective-permute-start.11 = (bf16[2,64,2048]{2,1,0:T(8,128)(2,1)S(1)}, bf16[2,64,2048]{2,1,0:T(8,128)(2,1)S(1)}, u32[]{:S(2)}, u32[]{:S(2)}) collective-permute-start(bf16[2,64,2048]{2,1,0:T(8,128)(2,1)S(1)} %copy.15.refs_0_.near), channel_id=1, source_target_pairs={{0,2},{1,5},{2,0},{3,7},{4,6},{5,1},{6,4},{7,3},{8,10},{9,13},{10,... | collective-permute-start | bytes 1572872 | tf_op jit(solution)/shard_map/ppermute | solution.py:247
  37.3 12.0 %collective-permute-start.18 = (bf16[64,1024]{1,0:T(8,128)(2,1)S(1)}, bf16[64,1024]{1,0:T(8,128)(2,1)S(1)}, u32[]{:S(2)}, u32[]{:S(2)}) collective-permute-start(bf16[64,1024]{1,0:T(8,128)(2,1)S(1)} %get-tuple-element.62.refs_0_), channel_id=1, source_target_pairs={{0,9},{1,17},{2,11},{3,19},{4,13},{5,21},{6,15},{7,23},{8,1},{9,25... | collective-permute-start | bytes 393224 | tf_op jit(solution)/shard_map/ppermute | solution.py:247
  39.1 10.3 %collective-permute-start.19 = (bf16[64,1024]{1,0:T(8,128)(2,1)S(1)}, bf16[64,1024]{1,0:T(8,128)(2,1)S(1)}, u32[]{:S(2)}, u32[]{:S(2)}) collective-permute-start(bf16[64,1024]{1,0:T(8,128)(2,1)S(1)} %get-tuple-element.85), channel_id=1, source_target_pairs={{0,1},{1,25},{2,3},{3,27},{4,5},{5,29},{6,7},{7,31},{8,9},{9,17},{... | collective-permute-start | bytes 393224 | tf_op jit(solution)/shard_map/ppermute | solution.py:247
  41.4 8.6 %collective-permute-start.15 = (bf16[3,256,256]{2,1,0:T(8,128)(2,1)S(1)}, bf16[3,256,256]{2,1,0:T(8,128)(2,1)S(1)}, u32[]{:S(2)}, u32[]{:S(2)}) collective-permute-start(bf16[3,256,256]{2,1,0:T(8,128)(2,1)S(1)} %get-tuple-element.75.refs_0_), channel_id=1, source_target_pairs={{0,1},{1,0},{2,3},{3,2},{4,5},{5,4},{6,7},{7,6},{8,9},{9,8},{10,11... | collective-permute-start | bytes 1179656 | tf_op jit(solution)/shard_map/ppermute | solution.py:251
  44.0 6.0 %collective-permute-start.17 = (f32[64,1024]{1,0:T(8,128)S(1)}, f32[64,1024]{1,0:T(8,128)S(1)}, u32[]{:S(2)}, u32[]{:S(2)}) collective-permute-start(f32[64,1024]{1,0:T(8,128)S(1)} %share.2.refs_0_.refs_6_), channel_id=1, source_target_pairs={{0,1},{1,0},{2,3},{3,2},{4,5},{5,4},{6,7},{7,6},{8,9},{9,8},{10,11... | collective-permute-start | bytes 786440 | tf_op jit(solution)/shard_map/ppermute | solution.py:251
  46.8 4.7 %collective-permute-start.14 = (bf16[256,2048]{1,0:T(8,128)(2,1)S(1)}, bf16[256,2048]{1,0:T(8,128)(2,1)S(1)}, u32[]{:S(2)}, u32[]{:S(2)}) collective-permute-start(bf16[256,2048]{1,0:T(8,128)(2,1)S(1)} %get-tuple-element.79.refs_0_), channel_id=1, source_target_pairs={{0,1},{1,0},{2,3},{3,2},{4,5},{5,4},{6,7},{7,6},{8,9},{9,8},{10,11... | collective-permute-start | bytes 3145736 | tf_op jit(solution)/shard_map/ppermute | solution.py:251
  49.3 2.2 %collective-permute-start.16 = (bf16[3,256,256]{2,1,0:T(8,128)(2,1)S(1)}, bf16[3,256,256]{2,1,0:T(8,128)(2,1)S(1)}, u32[]{:S(2)}, u32[]{:S(2)}) collective-permute-start(bf16[3,256,256]{2,1,0:T(8,128)(2,1)S(1)} %get-tuple-element.83.refs_0_), channel_id=1, source_target_pairs={{0,1},{1,0},{2,3},{3,2},{4,5},{5,4},{6,7},{7,6},{8,9},{9,8},{10,11... | collective-permute-start | bytes 1179656 | tf_op jit(solution)/shard_map/ppermute | solution.py:251
  49.5 2.0 %collective-permute-start.20 = (f32[64,1024]{1,0:T(8,128)S(1)}, f32[64,1024]{1,0:T(8,128)S(1)}, u32[]{:S(2)}, u32[]{:S(2)}) collective-permute-start(f32[64,1024]{1,0:T(8,128)S(1)} %share.3.refs_8_), channel_id=1, source_target_pairs={{0,1},{1,0},{2,3},{3,2},{4,5},{5,4},{6,7},{7,6},{8,9},{9,8},{10,11... | collective-permute-start | bytes 786440 | tf_op jit(solution)/shard_map/ppermute | solution.py:251
